TPU v7x, 128 devices: a whole 4x4x4 slice. The times are simulated.
128 devices in a mesh: sec: 2 (over z_hi), ctx: 16 (over y, z_lo, core), tp: 4 (over x).
Axes of the slice: x: 4, y: 4, z: 4 (z_hi: 2, z_lo: 2; z = z_hi * 2 + z_lo), core: 2. Of those that a mesh axis runs over, the one named last changes fastest.
Arguments:
- p_query: bfloat16 [2, 8, 512, 3584], P('sec', None, 'ctx', 'tp'), may hold values from -3 to 3
- p_key: bfloat16 [2, 8, 512, 512], P('sec', None, 'ctx', 'tp'), may hold values from -1.5 to 1.5
- p_value: bfloat16 [2, 8, 512, 512], P('sec', None, 'ctx', 'tp'), may hold values from -6 to 6
- p_cache_k: bfloat16 [2, 384, 128, 512], P('sec', 'ctx', None, 'tp'), may hold values from -1.5 to 1.5
- p_cache_v: bfloat16 [2, 384, 128, 512], P('sec', 'ctx', None, 'tp'), may hold values from -6 to 6
- p_slot_req: int32 [2, 384], P('sec', 'ctx'), may hold values from 0 to 7, as said below
- p_slot_blk: int32 [2, 384], P('sec', 'ctx'), may hold values from 0 to 191, as said below
- p_offsets: int32 [2, 8], P('sec'), may hold values from 1 to 24576, as said below
- d_query: bfloat16 [2, 32, 4, 3584], P('sec', 'ctx', None, 'tp'), may hold values from -3 to 3
- d_key: bfloat16 [2, 32, 4, 512], P('sec', 'ctx', None, 'tp'), may hold values from -1.5 to 1.5
- d_value: bfloat16 [2, 32, 4, 512], P('sec', 'ctx', None, 'tp'), may hold values from -6 to 6
- d_cache_k: bfloat16 [2, 384, 128, 512], P('sec', 'ctx', None, 'tp'), may hold values from -1.5 to 1.5
- d_cache_v: bfloat16 [2, 384, 128, 512], P('sec', 'ctx', None, 'tp'), may hold values from -6 to 6
- d_slot_req: int32 [2, 384], P('sec', 'ctx'), may hold values from 0 to 31, as said below
- d_slot_blk: int32 [2, 384], P('sec', 'ctx'), may hold values from 0 to 191, as said below
- d_lengths: int32 [2, 32], P('sec'), may hold values from 1 to 24576, as said below
- out_weight: bfloat16 [3584, 7168], P('tp'), may hold values from -1 to 1
Outputs:
- prefill_out: bfloat16 [2, 8, 512, 7168], P('sec', None, 'ctx', 'tp')
- decode_out: bfloat16 [2, 32, 4, 7168], P('sec', 'ctx', None, 'tp')
Inputs may be any that keep to these rules, and one draw needn't show every extreme that they name: `p_slot_req`: in each section every one of the 384 slots holds a block of one of the 8 requests, and every request holds at least one block. `p_slot_blk`: in each section the blocks of a request are numbered from 0 to its block count minus 1, each held by exactly one slot; one request holds exactly 192 blocks, and no request holds more. `p_offsets`: A request with c blocks has an offset from (c - 1) * 128 + 1 to c * 128. `d_slot_req`: in each section every one of the 384 slots holds a block of one of the 32 requests, and every request holds at least one block. `d_slot_blk`: in each section the blocks of a request are numbered from 0 to its block count minus 1, each held by exactly one slot; one request holds exactly 192 blocks, and no request holds more. `d_lengths`: A request with c blocks has a length from (c - 1) * 128 + 1 to c * 128.
All inputs are finite; a program needn't handle non-finite values.
Results may differ from a plain program's by a relative error of at most 0.025.
Values may be sent and summed in bfloat16 or wider, within the bound.
No kernel may reach another device: no remote copies, remote signals or barrier semaphores. Data moves between devices by JAX's collectives and lax.ppermute only.
A program may use at most 192 MiB of HBM per device.

v0:
```python
import math

import jax
import jax.numpy as jnp
from jax import lax
from jax.sharding import PartitionSpec as P

HD = 128


def swapped(shard, axis, distance):
    return lax.ppermute(shard, axis, [(i, i ^ 1 << distance) for i in range(lax.axis_size(axis))])


def group_size(slot_count, new_count):
    ceiling = 1
    while ceiling * 2 * new_count <= 4096:
        ceiling = ceiling * 2
    return math.gcd(slot_count, ceiling)


def add_blocks(carry, queries, cache_keys, cache_values, slot_req, slot_blk, bounds):
    req_count, new_count, kv_heads, group_len, head_size = queries.shape
    slot_count, page_len, last_width = cache_keys.shape
    per_round = group_size(slot_count, new_count)
    rounds = slot_count // per_round
    softmax_scale = head_size ** (-0.5)
    within = jnp.arange(page_len, dtype=jnp.int32)
    requests = jnp.arange(req_count, dtype=jnp.int32)

    def advance(state, pieces):
        numerator, denominator = state
        key_blk, value_blk, owner_ids, block_ids = pieces
        chosen = jnp.take(queries, owner_ids, axis=0)
        key_rows = key_blk.reshape(per_round, page_len, kv_heads, head_size)
        value_rows = value_blk.reshape(per_round, page_len, kv_heads, head_size)
        scores = (
            jnp.einsum("nqhgd,nkhd->nhgqk", chosen, key_rows, preferred_element_type=jnp.float32)
            * softmax_scale
        )
        matches = requests[:, None] == owner_ids[None, :]
        limits = jnp.sum(jnp.where(matches, bounds[:, None], 0), axis=0)
        visible = block_ids[:, None] * page_len + within[None, :] < limits[:, None]
        weights = jnp.where(visible[:, None, None, None, :], jnp.exp(scores), 0.0)
        products = jnp.einsum(
            "nhgqk,nkhd->nqhgd",
            weights.astype(jnp.bfloat16),
            value_rows,
            preferred_element_type=jnp.float32,
        )
        weight_sums = jnp.moveaxis(jnp.sum(weights, axis=4), 3, 1)
        numerator = numerator.at[owner_ids].add(products)
        denominator = denominator.at[owner_ids].add(weight_sums)
        return ((numerator, denominator), None)

    stacked = (
        cache_keys.reshape(rounds, per_round, page_len, last_width),
        cache_values.reshape(rounds, per_round, page_len, last_width),
        slot_req.reshape(rounds, per_round),
        slot_blk.reshape(rounds, per_round),
    )
    result, unused = lax.scan(advance, carry, stacked)
    return result


def dense_terms(queries, keys, values, visible):
    req_count, new_count, kv_heads, group_len, head_size = queries.shape
    key_rows = keys.reshape(req_count, keys.shape[1], kv_heads, head_size)
    value_rows = values.reshape(req_count, values.shape[1], kv_heads, head_size)
    scores = jnp.einsum(
        "rqhgd,rkhd->rqhgk", queries, key_rows, preferred_element_type=jnp.float32
    ) * head_size ** (-0.5)
    weights = jnp.where(visible[None, :, None, None, :], jnp.exp(scores), 0.0)
    products = jnp.einsum(
        "rqhgk,rkhd->rqhgd",
        weights.astype(jnp.bfloat16),
        value_rows,
        preferred_element_type=jnp.float32,
    )
    return (products, jnp.sum(weights, axis=4))


def on_device(
    p_query,
    p_key,
    p_value,
    p_cache_k,
    p_cache_v,
    p_slot_req,
    p_slot_blk,
    p_offsets,
    d_query,
    d_key,
    d_value,
    d_cache_k,
    d_cache_v,
    d_slot_req,
    d_slot_blk,
    d_lengths,
    out_weight,
):
    heads_local = p_query.shape[3] // HD
    kv_local = p_key.shape[3] // HD
    group_len = heads_local // kv_local
    prefill_req, span_local = (p_query.shape[1], p_query.shape[2])
    step_local, step_count = (d_query.shape[1], d_query.shape[2])
    ctx_count = lax.axis_size("ctx")
    local_queries = p_query[0].reshape(prefill_req, span_local, kv_local, group_len, HD)
    own_queries = d_query[0].reshape(step_local, step_count, kv_local, group_len, HD)
    start_num = jnp.zeros((prefill_req, span_local, kv_local, group_len, HD), jnp.float32)
    start_den = jnp.zeros((prefill_req, span_local, kv_local, group_len), jnp.float32)
    prefill_num, prefill_den = add_blocks(
        (start_num, start_den),
        local_queries,
        lax.all_gather(p_cache_k[0], "ctx", axis=0, tiled=True),
        lax.all_gather(p_cache_v[0], "ctx", axis=0, tiled=True),
        lax.all_gather(p_slot_req[0], "ctx", axis=0, tiled=True),
        lax.all_gather(p_slot_blk[0], "ctx", axis=0, tiled=True),
        p_offsets[0],
    )
    span_keys, span_values, step_queries = (
        lax.all_gather(p_key[0], "ctx", axis=1, tiled=True),
        lax.all_gather(p_value[0], "ctx", axis=1, tiled=True),
        lax.all_gather(own_queries, "ctx", axis=0, tiled=True),
    )
    query_pos = lax.axis_index("ctx") * span_local + jnp.arange(span_local, dtype=jnp.int32)
    key_pos = jnp.arange(span_local * ctx_count, dtype=jnp.int32)
    span_num, span_den = dense_terms(
        local_queries, span_keys, span_values, query_pos[:, None] >= key_pos[None, :]
    )
    prefill_num = prefill_num + span_num
    prefill_den = prefill_den + span_den
    handed_keys, handed_values = swapped((p_key[0], p_value[0]), "sec", 0)
    req_total = step_queries.shape[0]
    start_num = jnp.zeros((req_total, step_count, kv_local, group_len, HD), jnp.float32)
    start_den = jnp.zeros((req_total, step_count, kv_local, group_len), jnp.float32)
    decode_num, decode_den = add_blocks(
        (start_num, start_den),
        step_queries,
        d_cache_k[0],
        d_cache_v[0],
        d_slot_req[0],
        d_slot_blk[0],
        d_lengths[0],
    )
    hand_num, hand_den = dense_terms(
        step_queries[:prefill_req],
        handed_keys,
        handed_values,
        jnp.ones((step_count, span_local), dtype=bool),
    )
    decode_num = decode_num.at[:prefill_req].add(hand_num)
    decode_den = decode_den.at[:prefill_req].add(hand_den)
    own_num, own_den = (
        lax.psum_scatter(
            decode_num.astype(jnp.bfloat16), "ctx", scatter_dimension=0, tiled=True
        ).astype(jnp.float32),
        lax.psum_scatter(
            decode_den.astype(jnp.bfloat16), "ctx", scatter_dimension=0, tiled=True
        ).astype(jnp.float32),
    )
    step_pos = jnp.arange(step_count, dtype=jnp.int32)
    self_num, self_den = dense_terms(
        own_queries, d_key[0], d_value[0], step_pos[:, None] >= step_pos[None, :]
    )
    own_num = own_num + self_num
    own_den = own_den + self_den
    prefill_attention = (
        (prefill_num / prefill_den[..., None])
        .astype(jnp.bfloat16)
        .reshape(prefill_req * span_local, heads_local * HD)
    )
    decode_attention = (
        (own_num / own_den[..., None])
        .astype(jnp.bfloat16)
        .reshape(step_local * step_count, heads_local * HD)
    )
    joined = jnp.concatenate([prefill_attention, decode_attention], axis=0)
    projected = jnp.dot(joined, out_weight, preferred_element_type=jnp.float32)
    shares = lax.psum_scatter(projected.astype(jnp.bfloat16), "tp", scatter_dimension=1, tiled=True)
    prefill_rows = prefill_req * span_local
    prefill_out = shares[:prefill_rows].reshape(1, prefill_req, span_local, shares.shape[1])
    decode_out = shares[prefill_rows:].reshape(1, step_local, step_count, shares.shape[1])
    return (prefill_out, decode_out)


def solution(mesh):
    placed = (
        P("sec", None, "ctx", "tp"),
        P("sec", None, "ctx", "tp"),
        P("sec", None, "ctx", "tp"),
        P("sec", "ctx", None, "tp"),
        P("sec", "ctx", None, "tp"),
        P("sec", "ctx"),
        P("sec", "ctx"),
        P("sec", None),
        P("sec", "ctx", None, "tp"),
        P("sec", "ctx", None, "tp"),
        P("sec", "ctx", None, "tp"),
        P("sec", "ctx", None, "tp"),
        P("sec", "ctx", None, "tp"),
        P("sec", "ctx"),
        P("sec", "ctx"),
        P("sec", None),
        P("tp", None),
    )
    return jax.shard_map(
        on_device,
        mesh=mesh,
        in_specs=placed,
        out_specs=(P("sec", None, "ctx", "tp"), P("sec", "ctx", None, "tp")),
        check_vma=False,
    )
```

profile of v0, /device:TPU:1, one launch (start us, length us, event | category | flops | bytes accessed | tf_op | source)
XLA Modules:
  0.0 563.2 jit_solution(14204345812215614360)
XLA Ops:
  7.2 4.5 collective-permute-start
  11.8 21.5 %all_gather.27 = bf16[32,4,1,7,128]{4,1,3,2,0:T(4,128)(2,1)S(1)} all-gather(bf16[2,4,1,7,128]{4,1,3,2,0:T(4,128)(2,1)} %bitcast.375), channel_id=1, replica_groups=mesh['sec'=2,'ctx'=16,'tp'=4] {'ctx'}, dimensions={0}, use_global_device_ids=true | all-gather | bytes 243712 | tf_op jit(solution)/shard_map/all_gather | solution.py:124
  36.8 17.3 %while.29 = (s32[]{:T(128)}, f32[32,4,1,7,128]{4,1,3,0,2:T(4,128)S(1)}, f32[32,4,1,7]{3,1,0,2:T(4,128)S(1)}, s32[3,8]{1,0:T(4,128)S(1)}, bf16[3,8,128,128]{3,2,1...) while((s32[]{:T(128)}, ...), condition=%wide.region_12.13_spmd.clone, body=%wide.region_7.12_spmd.clone.sunk | while | flops 14856010 | bytes 1510593 | solution.py:62
  61.0 5.4 all-reduce.3
  67.5 53.6 %all-reduce.2 = bf16[32,4,1,7]{3,1,0,2:T(4,128)(2,1)S(1)} all-reduce(bf16[32,4,1,7]{3,1,0,2:T(4,128)(2,1)S(1)} %convert_element_type.42), channel_id=9, replica_groups=mesh['sec'=2,'ctx'=16,'tp'=4] {'ctx'}, use_global_device_ids=true, to_apply=%region_15.16.clone | all-reduce | flops 896 | bytes 3584
  122.5 25.7 %all-gather.15.cloned.1.call-done = bf16[1,8,512,128]{3,2,1,0:T(8,128)(2,1)} async-done(((bf16[1,8,32,128]{3,2,1,0:T(8,128)(2,1)}), bf16[1,8,512,128]{3,2,1,0:T(8,128)(2,1)}) %all-gather.15.cloned.1.call-update) | async-done | bytes 1048592 | tf_op jit(solution)/shard_map/all_gather | solution.py:122
  148.2 4.5 fusion.49
  152.7 69.3 %all-gather.11.cloned.1.call-done = bf16[1,384,128,128]{3,2,0,1:T(8,128)(2,1)} async-done(((bf16[1,24,128,128]{3,2,0,1:T(8,128)(2,1)}), bf16[1,384,128,128]{3,2,0,1:T(8,128)(2,1)}) %all-gather.11.cloned.1.call-update) | async-done | bytes 12582928 | tf_op jit(solution)/shard_map/all_gather | solution.py:116
  222.0 74.4 %all-gather.13.cloned.1.call-done = bf16[1,384,128,128]{3,2,0,1:T(8,128)(2,1)} async-done(((bf16[1,24,128,128]{3,2,0,1:T(8,128)(2,1)}), bf16[1,384,128,128]{3,2,0,1:T(8,128)(2,1)}) %all-gather.13.cloned.1.call-update) | async-done | bytes 12582928 | tf_op jit(solution)/shard_map/all_gather | solution.py:115
  296.6 198.3 %while.28 = (s32[]{:T(128)}, f32[8,32,1,7,128]{4,1,3,0,2:T(8,128)S(1)}, f32[8,32,1,7]{1,3,0,2:T(8,128)S(1)}, s32[3,128]{1,0:T(4,128)S(1)}, bf16[3,128,128,128]{3...) while((s32[]{:T(128)}, ...), condition=%wide.region_5.6_spmd.clone, body=%wide.region_0.5_spmd.clone.sunk | while | flops 1908446336 | bytes 134738336 | solution.py:62
  296.6 6.5 %gather_fusion = bf16[128,32,7,128]{3,2,1,0:T(8,128)(2,1)} fusion(bf16[8,32,7,128]{3,2,1,0:T(8,128)(2,1)S(1)} %bitcast.356, s32[1024]{0:T(1024)S(1)} %pad_clamp_fusion.4), kind=kCustom, calls=%fused_computation.clone.clone.1 | custom fusion | bytes 14680576 | tf_op jit(solution)/shard_map/while/body/eval_jaxpr/jit(_take)/gather | solution.py:34
  303.2 7.5 %broadcast_select_fusion.2 = bf16[128,32,7,128]{3,2,1,0:T(8,128)(2,1)} fusion(bf16[128,32,7,128]{3,2,1,0:T(8,128)(2,1)} %gather_fusion, pred[128]{0:T(512)(128)(4,1)S(1)} %get-tuple-element.421), kind=kLoop, calls=%fused_computation.14.clone.1 | loop fusion | flops 3670016 | bytes 14680192 | tf_op jit(solution)/shard_map/while/body/eval_jaxpr/jit(_take)/select_n | solution.py:34
  310.8 10.2 %bitcast_reduce_fusion.2 = (f32[128,7,32]{2,1,0:T(8,128)S(1)}, f32[128,128,32,7]{1,2,3,0:T(8,128)}) fusion(pred[128,128]{1,0:T(8,128)(4,1)S(1)} %fusion.124, bf16[128,32,7,128]{3,2,1,0:T(8,128)(2,1)} %broadcast_select_fusion.2, bf16[3,128,128,128]{3,2,1,0:T(8,128)(2,1)} %get-tuple-element.494, s32[]{:T(128)} %get-tuple-element.477), kind=kOutput, calls=%fused_computation.10.clone.1 | convolution fusion | flops 950505472 | bytes 27394560 | tf_op jit(solution)/shard_map/while/body/eval_jaxpr/nqhgd,nkhd->nhgqk/dot_general | solution.py:38
  321.1 14.1 %convolution_bitcast_fusion.6 = f32[128,32,7,128]{3,1,2,0:T(8,128)} fusion(f32[128,128,32,7]{1,2,3,0:T(8,128)} %get-tuple-element.422, pred[128,128]{1,0:T(8,128)(4,1)S(1)} %fusion.124, bf16[3,128,128,128]{3,2,1,0:T(8,128)(2,1)} %get-tuple-element.491, s32[]{:T(128)} %get-tuple-element.477), kind=kOutput, calls=%fused_computation.13.clone.1 | convolution fusion | flops 950534144 | bytes 33571328 | tf_op jit(solution)/shard_map/while/body/eval_jaxpr/nhgqk,nkhd->nqhgd/dot_general | solution.py:45
  335.2 22.4 %scatter_fusion = f32[8,32,7,128]{3,1,2,0:T(8,128)S(1)} fusion(f32[8,32,7,128]{3,1,2,0:T(8,128)S(1)} %bitcast.353, s32[128]{0:T(128)S(1)} %fusion.122, f32[128,32,7,128]{3,1,2,0:T(8,128)} %convolution_bitcast_fusion.6), kind=kCustom, calls=%fused_computation.2.clone.clone.1 | custom fusion | flops 3670016 | bytes 44040704 | tf_op jit(solution)/shard_map/while/body/eval_jaxpr/scatter-add | solution.py:52
  357.6 5.1 scatter_fusion.1
  362.8 6.6 %gather_fusion = bf16[128,32,7,128]{3,2,1,0:T(8,128)(2,1)} fusion(bf16[8,32,7,128]{3,2,1,0:T(8,128)(2,1)S(1)} %bitcast.356, s32[1024]{0:T(1024)S(1)} %pad_clamp_fusion.4), kind=kCustom, calls=%fused_computation.clone.clone.1 | custom fusion | bytes 14680576 | tf_op jit(solution)/shard_map/while/body/eval_jaxpr/jit(_take)/gather | solution.py:34
  369.4 7.5 %broadcast_select_fusion.2 = bf16[128,32,7,128]{3,2,1,0:T(8,128)(2,1)} fusion(bf16[128,32,7,128]{3,2,1,0:T(8,128)(2,1)} %gather_fusion, pred[128]{0:T(512)(128)(4,1)S(1)} %get-tuple-element.421), kind=kLoop, calls=%fused_computation.14.clone.1 | loop fusion | flops 3670016 | bytes 14680192 | tf_op jit(solution)/shard_map/while/body/eval_jaxpr/jit(_take)/select_n | solution.py:34
  377.1 10.2 %bitcast_reduce_fusion.2 = (f32[128,7,32]{2,1,0:T(8,128)S(1)}, f32[128,128,32,7]{1,2,3,0:T(8,128)}) fusion(pred[128,128]{1,0:T(8,128)(4,1)S(1)} %fusion.124, bf16[128,32,7,128]{3,2,1,0:T(8,128)(2,1)} %broadcast_select_fusion.2, bf16[3,128,128,128]{3,2,1,0:T(8,128)(2,1)} %get-tuple-element.494, s32[]{:T(128)} %get-tuple-element.477), kind=kOutput, calls=%fused_computation.10.clone.1 | convolution fusion | flops 950505472 | bytes 27394560 | tf_op jit(solution)/shard_map/while/body/eval_jaxpr/nqhgd,nkhd->nhgqk/dot_general | solution.py:38
  387.2 14.1 %convolution_bitcast_fusion.6 = f32[128,32,7,128]{3,1,2,0:T(8,128)} fusion(f32[128,128,32,7]{1,2,3,0:T(8,128)} %get-tuple-element.422, pred[128,128]{1,0:T(8,128)(4,1)S(1)} %fusion.124, bf16[3,128,128,128]{3,2,1,0:T(8,128)(2,1)} %get-tuple-element.491, s32[]{:T(128)} %get-tuple-element.477), kind=kOutput, calls=%fused_computation.13.clone.1 | convolution fusion | flops 950534144 | bytes 33571328 | tf_op jit(solution)/shard_map/while/body/eval_jaxpr/nhgqk,nkhd->nqhgd/dot_general | solution.py:45
  401.3 22.4 %scatter_fusion = f32[8,32,7,128]{3,1,2,0:T(8,128)S(1)} fusion(f32[8,32,7,128]{3,1,2,0:T(8,128)S(1)} %bitcast.353, s32[128]{0:T(128)S(1)} %fusion.122, f32[128,32,7,128]{3,1,2,0:T(8,128)} %convolution_bitcast_fusion.6), kind=kCustom, calls=%fused_computation.2.clone.clone.1 | custom fusion | flops 3670016 | bytes 44040704 | tf_op jit(solution)/shard_map/while/body/eval_jaxpr/scatter-add | solution.py:52
  423.7 5.1 scatter_fusion.1
  428.9 6.5 %gather_fusion = bf16[128,32,7,128]{3,2,1,0:T(8,128)(2,1)} fusion(bf16[8,32,7,128]{3,2,1,0:T(8,128)(2,1)S(1)} %bitcast.356, s32[1024]{0:T(1024)S(1)} %pad_clamp_fusion.4), kind=kCustom, calls=%fused_computation.clone.clone.1 | custom fusion | bytes 14680576 | tf_op jit(solution)/shard_map/while/body/eval_jaxpr/jit(_take)/gather | solution.py:34
  435.4 7.5 %broadcast_select_fusion.2 = bf16[128,32,7,128]{3,2,1,0:T(8,128)(2,1)} fusion(bf16[128,32,7,128]{3,2,1,0:T(8,128)(2,1)} %gather_fusion, pred[128]{0:T(512)(128)(4,1)S(1)} %get-tuple-element.421), kind=kLoop, calls=%fused_computation.14.clone.1 | loop fusion | flops 3670016 | bytes 14680192 | tf_op jit(solution)/shard_map/while/body/eval_jaxpr/jit(_take)/select_n | solution.py:34
  443.1 10.2 %bitcast_reduce_fusion.2 = (f32[128,7,32]{2,1,0:T(8,128)S(1)}, f32[128,128,32,7]{1,2,3,0:T(8,128)}) fusion(pred[128,128]{1,0:T(8,128)(4,1)S(1)} %fusion.124, bf16[128,32,7,128]{3,2,1,0:T(8,128)(2,1)} %broadcast_select_fusion.2, bf16[3,128,128,128]{3,2,1,0:T(8,128)(2,1)} %get-tuple-element.494, s32[]{:T(128)} %get-tuple-element.477), kind=kOutput, calls=%fused_computation.10.clone.1 | convolution fusion | flops 950505472 | bytes 27394560 | tf_op jit(solution)/shard_map/while/body/eval_jaxpr/nqhgd,nkhd->nhgqk/dot_general | solution.py:38
  453.2 14.1 %convolution_bitcast_fusion.6 = f32[128,32,7,128]{3,1,2,0:T(8,128)} fusion(f32[128,128,32,7]{1,2,3,0:T(8,128)} %get-tuple-element.422, pred[128,128]{1,0:T(8,128)(4,1)S(1)} %fusion.124, bf16[3,128,128,128]{3,2,1,0:T(8,128)(2,1)} %get-tuple-element.491, s32[]{:T(128)} %get-tuple-element.477), kind=kOutput, calls=%fused_computation.13.clone.1 | convolution fusion | flops 950534144 | bytes 33571328 | tf_op jit(solution)/shard_map/while/body/eval_jaxpr/nhgqk,nkhd->nqhgd/dot_general | solution.py:45
  467.3 22.4 %scatter_fusion = f32[8,32,7,128]{3,1,2,0:T(8,128)S(1)} fusion(f32[8,32,7,128]{3,1,2,0:T(8,128)S(1)} %bitcast.353, s32[128]{0:T(128)S(1)} %fusion.122, f32[128,32,7,128]{3,1,2,0:T(8,128)} %convolution_bitcast_fusion.6), kind=kCustom, calls=%fused_computation.2.clone.clone.1 | custom fusion | flops 3670016 | bytes 44040704 | tf_op jit(solution)/shard_map/while/body/eval_jaxpr/scatter-add | solution.py:52
  489.8 5.1 scatter_fusion.1
  494.9 3.1 fusion.78
  498.4 10.4 %convolution_convert_fusion = bf16[264,7168]{1,0:T(8,128)(2,1)} fusion(bf16[896,7168]{1,0:T(8,128)(2,1)} %param.41, bf16[8,896]{1,0:T(8,128)(2,1)S(1)} %bitcast.376, bf16[256,896]{1,0:T(8,128)(2,1)S(1)} %bitcast.371), kind=kOutput, calls=%fused_computation.75 | convolution fusion | flops 3393933312 | bytes 17102848 | tf_op jit(solution)/shard_map/dot_general | solution.py:179
  508.8 44.0 %reduce-scatter.6.cloned.1.call-done = bf16[264,1792]{1,0:T(8,128)(2,1)} async-done(((bf16[264,7168]{1,0:T(8,128)(2,1)}), bf16[264,1792]{1,0:T(8,128)(2,1)}) %reduce-scatter.6.cloned.1.call-update) | async-done | bytes 946192 | tf_op jit(solution)/shard_map/reduce_scatter | solution.py:180
  554.2 2.2 slice.83
  (135 shorter events, 31.0 us)
Async XLA Ops:
  7.2 60.1 %copy-start = (bf16[1,2,4,128]{3,2,1,0:T(4,128)(2,1)S(1)}, bf16[1,2,4,128]{3,2,1,0:T(4,128)(2,1)}, u32[]{:S(2)}) copy-start(bf16[1,2,4,128]{3,2,1,0:T(4,128)(2,1)} %param.35) | copy-start | bytes 6148
  7.2 113.9 %reduce-scatter.4.cloned.1.call-start = ((), (), s32[]{:S(2)}) async-start(), calls=%async_computation.2 | async-start | bytes 278528 | tf_op jit(solution)/shard_map/reduce_scatter | solution.py:155
  7.2 47.1 %collective-permute-start = (bf16[8,32,128]{2,1,0:T(8,128)(2,1)}, bf16[8,32,128]{2,1,0:T(8,128)(2,1)S(1)}, u32[]{:S(2)}, u32[]{:S(2)}) collective-permute-start(bf16[8,32,128]{2,1,0:T(8,128)(2,1)} %bitcast.373), channel_id=1, source_target_pairs={{0,64},{64,0},{1,65},{65,1},{2,66},{66,2},{3,67},{67,3},{4,68},{68... | collective-permute-start | bytes 196616 | tf_op jit(solution)/shard_map/ppermute | solution.py:12
  11.7 42.8 %collective-permute-start.1 = (bf16[8,32,128]{2,1,0:T(8,128)(2,1)}, bf16[8,32,128]{2,1,0:T(8,128)(2,1)S(1)}, u32[]{:S(2)}, u32[]{:S(2)}) collective-permute-start(bf16[8,32,128]{2,1,0:T(8,128)(2,1)} %bitcast.374), channel_id=1, source_target_pairs={{0,64},{64,0},{1,65},{65,1},{2,66},{66,2},{3,67},{67,3},{4,68},{68... | collective-permute-start | bytes 196616 | tf_op jit(solution)/shard_map/ppermute | solution.py:12
  36.8 21.5 %copy-start.2 = (bf16[1,8,32,896]{3,2,1,0:T(8,128)(2,1)S(1)}, bf16[1,8,32,896]{3,2,1,0:T(8,128)(2,1)}, u32[]{:S(2)}) copy-start(bf16[1,8,32,896]{3,2,1,0:T(8,128)(2,1)} %param.25) | copy-start | bytes 1376260
  36.8 22.5 %copy-start.3 = (bf16[1,2,4,896]{3,2,1,0:T(4,128)(2,1)S(1)}, bf16[1,2,4,896]{3,2,1,0:T(4,128)(2,1)}, u32[]{:S(2)}) copy-start(bf16[1,2,4,896]{3,2,1,0:T(4,128)(2,1)} %param.33) | copy-start | bytes 43012
  36.8 22.7 %copy-start.8 = (u32[128]{0:T(128)S(1)}, u32[128]{0:T(128)}, u32[]{:S(2)}) copy-start(u32[128]{0:T(128)} %constant.160) | copy-start | bytes 1540
  36.8 24.0 %copy-start.10 = (s32[1,24]{1,0:T(1,128)S(1)}, s32[1,24]{1,0:T(1,128)}, u32[]{:S(2)}) copy-start(s32[1,24]{1,0:T(1,128)} %param.31) | copy-start | bytes 292
  36.8 24.1 %copy-start.11 = (s32[1,24]{1,0:T(1,128)S(1)}, s32[1,24]{1,0:T(1,128)}, u32[]{:S(2)}) copy-start(s32[1,24]{1,0:T(1,128)} %param.30) | copy-start | bytes 292
  36.8 30.2 %copy-start.9 = (bf16[1,2,4,128]{3,2,1,0:T(4,128)(2,1)S(1)}, bf16[1,2,4,128]{3,2,1,0:T(4,128)(2,1)}, u32[]{:S(2)}) copy-start(bf16[1,2,4,128]{3,2,1,0:T(4,128)(2,1)} %param.34) | copy-start | bytes 6148
  54.2 242.4 %copy-start.12 = (s32[1,8]{1,0:T(1,128)S(1)}, s32[1,8]{1,0:T(1,128)}, u32[]{:S(2)}) copy-start(s32[1,8]{1,0:T(1,128)} %param.32) | copy-start | bytes 100
  55.5 92.7 %all-gather.15.cloned.1.call-start = ((), (), s32[]{:S(2)}) async-start(), calls=%async_computation.6 | async-start | bytes 1114112 | tf_op jit(solution)/shard_map/all_gather | solution.py:122
  56.3 165.7 %all-gather.11.cloned.1.call-start = ((), (), s32[]{:S(2)}) async-start(), calls=%async_computation.4 | async-start | bytes 13369344 | tf_op jit(solution)/shard_map/all_gather | solution.py:116
  57.0 239.4 %all-gather.13.cloned.1.call-start = ((), (), s32[]{:S(2)}) async-start(), calls=%async_computation.5 | async-start | bytes 13369344 | tf_op jit(solution)/shard_map/all_gather | solution.py:115
  57.6 437.4 %all-gather.17.cloned.1.call-start = ((), (), s32[]{:S(2)}) async-start(), calls=%async_computation.7 | async-start | bytes 1114112 | tf_op jit(solution)/shard_map/all_gather | solution.py:123
  58.2 494.6 %reduce-scatter.6.cloned.1.call-start = ((), (), s32[]{:S(2)}) async-start(), calls=%async_computation.3 | async-start | bytes 4730880 | tf_op jit(solution)/shard_map/reduce_scatter | solution.py:180
  59.5 237.0 %copy-start.5 = (pred[32,512]{1,0:T(8,128)(4,1)}, pred[32,512]{1,0:T(8,128)(4,1)S(1)}, u32[]{:S(2)}) copy-start(pred[32,512]{1,0:T(8,128)(4,1)S(1)} %iota_compare_fusion.2) | copy-start | bytes 49156
  296.5 198.3 %copy-start.4 = (f32[8,32,7]{1,2,0:T(8,128)S(1)}, f32[8,32,7]{1,2,0:T(8,128)}, u32[]{:S(2)}) copy-start(f32[8,32,7]{1,2,0:T(8,128)} %get-tuple-element.303) | copy-start | bytes 21508
  296.6 198.4 %copy-start.6 = (pred[32,512]{1,0:T(8,128)(4,1)S(1)}, pred[32,512]{1,0:T(8,128)(4,1)}, u32[]{:S(2)}) copy-start(pred[32,512]{1,0:T(8,128)(4,1)} %copy-done.5) | copy-start | bytes 49156
  494.9 3.5 copy-start.7
  498.4 57.9 %copy-start.1 = (bf16[1,2,4,128]{3,2,1,0:T(4,128)(2,1)S(1)}, bf16[1,2,4,128]{3,2,1,0:T(4,128)(2,1)}, u32[]{:S(2)}) copy-start(bf16[1,2,4,128]{3,2,1,0:T(4,128)(2,1)} %param.35) | copy-start | bytes 6148
Sparse Core Ops, SparseCore 0:
  55.6 55.6 reduce-scatter.3
  113.1 35.0 all-gather.14
  150.0 71.9 all-gather.10
  223.7 72.6 all-gather.12
  298.0 33.2 all-gather.16
  508.9 43.8 reduce-scatter.5
where the time goes:
time: 565 us; the launch traced here: 563 us
  waiting for transfers between devices  216 us (38%)
  other arithmetic  118 us (21%)
  matrix products  99 us (18%)
  blocking collectives  80.4 us (14%)
  local copies, waits for them, and re-layouts  28.8 us (5%)
  between operations  15.8 us (3%)
    all_gather x1, waiting for transfers between devices, on_device(): lax.all_gather(p_cache_k[0], 'ctx', axis=0, tiled=True)  74.4 us
    scatter-add x6, other arithmetic, advance(): numerator = numerator.at[owner_ids].add(products)  69.9 us
    all_gather x1, waiting for transfers between devices, on_device(): lax.all_gather(p_cache_v[0], 'ctx', axis=0, tiled=True)  69.3 us
    unnamed x2, blocking collectives  58.9 us
    dot_general x6, matrix products, advance(): jnp.einsum('nhgqk,nkhd->nqhgd', weights.astype(jnp.bfloat16), value_rows,...  45.7 us
    reduce_scatter x1, waiting for transfers between devices, on_device(): lax.psum_scatter(projected.astype(jnp.bfloat16), 'tp', scatter_dimension=...  44 us
    dot_general x6, matrix products, advance(): jnp.einsum('nqhgd,nkhd->nhgqk', chosen, key_rows, preferred_element_type=...  34.5 us
    all_gather x1, waiting for transfers between devices, on_device(): lax.all_gather(p_key[0], 'ctx', axis=1, tiled=True)  25.7 us
  transfers between devices with their start and end apart: 8, of which 4 were waited for; matrix products, arithmetic and copies ran while one was open for 40% of the time, Pallas kernels for 0%

commit v1 on v0

v1 whole, which is shorter than its diff:
```python
import functools

import jax
import jax.numpy as jnp
from jax import lax
from jax.experimental import pallas as pl
from jax.experimental.pallas import tpu as pltpu
from jax.sharding import PartitionSpec as P

HD = 128
PAGE = 128
BF = jnp.bfloat16
F32 = jnp.float32
NT = (((1,), (1,)), ((), ()))
NB = 4
VM = pl.BlockSpec(memory_space=pltpu.VMEM)
SM = pl.BlockSpec(memory_space=pltpu.SMEM)
HBM = pl.BlockSpec(memory_space=pl.ANY)


def attn_kernel(order, lim, starts, *refs, first, R, heads, half):
    rows=heads*128
    if first:
        bases, q0,q1,q2,q3, ka, kb, va, vb, sk, sv, num, den, ks, vs, qs, dacc, tile, sem = refs
    else:
        q0,q1,q2,q3, ka, kb, va, vb, num_in, den_in, o0,o1,o2,o3, ks, vs, qs, acc, dacc, sem = refs
    cs=[pltpu.make_async_copy(ka, ks.at[pl.ds(0,half)], sem.at[0]),
        pltpu.make_async_copy(kb, ks.at[pl.ds(half,half)], sem.at[1]),
        pltpu.make_async_copy(va, vs.at[pl.ds(0,half)], sem.at[2]),
        pltpu.make_async_copy(vb, vs.at[pl.ds(half,half)], sem.at[3])]
    for c in cs: c.start()
    qr=(q0,q1,q2,q3)
    for r in range(R):
        for h in range(heads):
            for d in range(4):
                qs[r,pl.ds(h*128+d*32,32),:]=qr[d][r,:,pl.ds(h*128,128)]
    if first:
        rowi=lax.broadcasted_iota(jnp.int32,(128,128),0); coli=lax.broadcasted_iota(jnp.int32,(128,128),1)
        def pick(i,b):
            g=i//32
            return jnp.where(g==0,bases[b],jnp.where(g==1,bases[b+1],jnp.where(g==2,bases[b+2],bases[b+3])))+lax.rem(i,32)
        tile[...]=jnp.where(pick(rowi,0)>=pick(coli,4),1.0,0.0)
    for c in cs: c.wait()
    lane1=lax.broadcasted_iota(jnp.int32,(128,128),1)
    lane=lax.broadcasted_iota(jnp.int32,(1,128),1)
    if first: den[...]=jnp.zeros_like(den)
    def request(r,dtile):
        s0=starts[r]; n=starts[r+1]-s0
        nref=num.at[r] if first else acc
        def fetch(i):
            ok=i<n
            s=jnp.where(ok,s0+i,0)
            b=order[s]
            return ks[b],vs[b],jnp.where(ok,lim[s],0)
        def weights(Ks,ms):
            K=jnp.concatenate(Ks,axis=0)
            sc=lax.dot_general(qs[r],K,NT,preferred_element_type=F32)
            w=jnp.exp(sc*HD**-0.5)
            return [m(w[:,j*128:(j+1)*128]) for j,m in enumerate(ms)]
        def keep(l):
            return lambda w: jnp.where(lane<l,w,0.0)
        def causal(w):
            return (w.reshape(heads,128,128)*tile[...][None]).reshape(rows,128)
        def causal_sel(w):
            return jnp.where(tile[...][None]>0.5,w.reshape(heads,128,128),0.0).reshape(rows,128)
        def total(ws):
            t=ws[0]
            for w in ws[1:]: t=t+w
            return t
        def product(ws,Vs):
            return jnp.dot(jnp.concatenate([w.astype(BF) for w in ws],axis=1),jnp.concatenate(Vs,axis=0),preferred_element_type=F32)
        skip=0
        if first:
            f=[fetch(i) for i in range(NB-1)]
            ws=weights([sk[r]]+[x[0] for x in f],[causal_sel]+[keep(x[2]) for x in f])
            dacc[...]=total(ws)
            nref[...]=product(ws,[sv[r]]+[x[1] for x in f])
            skip=NB-1
        else:
            acc[...]=jnp.zeros_like(acc); dacc[...]=jnp.zeros_like(dacc)
        def step(p,_):
            f=[fetch(skip+NB*p+i) for i in range(NB)]
            ws=weights([x[0] for x in f],[keep(x[2]) for x in f])
            dacc[...]+=total(ws)
            nref[...]+=product(ws,[x[1] for x in f])
            return 0
        lax.fori_loop(0,(jnp.maximum(n-skip,0)+NB-1)//NB,step,0)
        upd=dtile
        for h in range(heads):
            col=jnp.sum(dacc[pl.ds(h*128,128),:],axis=1,keepdims=True)
            upd=upd+jnp.where(lane1==r*16+h,col,0.0)
        if not first:
            outs=(o0,o1,o2,o3)
            for h in range(heads):
                for d in range(4):
                    sl=pl.ds(h*128+d*32,32)
                    outs[d][pl.ds(pl.multiple_of(r*32,32),32),pl.ds(h*128,128)]=(num_in[r,sl,:]+acc[sl,:]).astype(BF)
        return upd
    init=jnp.zeros((128,128),F32) if first else den_in[...]
    dl=lax.fori_loop(0,R,request,init)
    if first:
        den[...]=dl
    else:
        outs=(o0,o1,o2,o3)
        hi=dl.astype(BF)
        lo=(dl-hi.astype(F32)).astype(BF)
        for d in range(4):
            z=jnp.zeros((16,128),BF)
            for k,a in enumerate((hi,lo)):
                outs[d][R*32:R*32+16,pl.ds(k*256,128)]=a[d*32:d*32+16]
                outs[d][R*32:R*32+16,pl.ds(k*256+128,128)]=a[d*32+16:d*32+32]
            for k in range(4,heads):
                outs[d][R*32:R*32+16,pl.ds(k*128,128)]=z

def attn(first, order, lim, starts, qs, kv, extra):
    R,T,W=qs[0].shape
    heads=W//HD
    rows=heads*128
    nb=order.shape[0]
    half=nb//2
    anyspec=pl.BlockSpec(memory_space=pl.ANY)
    vm=pl.BlockSpec(memory_space=pltpu.VMEM)
    sm=pl.BlockSpec(memory_space=pltpu.SMEM)
    scr=[pltpu.VMEM((nb,128,128),BF),pltpu.VMEM((nb,128,128),BF),pltpu.VMEM((R,rows,128),BF)]
    cost=pl.CostEstimate(flops=4*nb*rows*128*128,bytes_accessed=12_000_000,transcendentals=nb*rows*128)
    body=functools.partial(attn_kernel,first=first,R=R,heads=heads,half=half)
    cp=pltpu.CompilerParams(vmem_limit_bytes=48<<20)
    if first:
        bases,sk,sv=extra
        return pl.pallas_call(body,in_specs=[sm]*4+[vm]*4+[anyspec]*4+[vm]*2,out_specs=[vm]*2,
            scratch_shapes=scr+[pltpu.VMEM((rows,128),F32),pltpu.VMEM((128,128),F32),pltpu.SemaphoreType.DMA((4,))],
            out_shape=[jax.ShapeDtypeStruct((R,rows,128),F32),jax.ShapeDtypeStruct((128,128),F32)],
            compiler_params=cp,cost_estimate=cost,name="attn_near")(order,lim,starts,bases,*qs,*kv,sk,sv)
    num,den=extra
    return pl.pallas_call(body,in_specs=[sm]*3+[vm]*4+[anyspec]*4+[vm]*2,out_specs=[vm]*4,
        scratch_shapes=scr+[pltpu.VMEM((rows,128),F32),pltpu.VMEM((rows,128),F32),pltpu.SemaphoreType.DMA((4,))],
        out_shape=[jax.ShapeDtypeStruct((R*T+16,W),BF)]*4,compiler_params=cp,cost_estimate=cost,name="attn_far")(order,lim,starts,*qs,*kv,num,den)


def decode_kernel(req, lim, ctx, q, k, v, hk, hv, dk, dv, out, acc, dacc):
    scale = HD ** -0.5
    blocks = k.shape[0]
    handed = hk.shape[0]
    lane = lax.broadcasted_iota(jnp.int32, (1, 128), 1)
    acc[...] = jnp.zeros_like(acc)
    dacc[...] = jnp.zeros_like(dacc)

    def block(i, unused):
        r = req[i]
        s = lax.dot_general(q[r], k[i], NT, preferred_element_type=F32)
        w = jnp.where(lane < lim[i], jnp.exp(s * scale), 0.0)
        dacc[r] += w
        acc[r] += jnp.dot(w.astype(BF), v[i], preferred_element_type=F32)
        return 0

    lax.fori_loop(0, blocks, block, 0, unroll=True)

    def first_lane(w):
        return jnp.where(lane == 0, jnp.sum(w, axis=1, keepdims=True), 0.0)

    for r in range(handed):
        s = lax.dot_general(q[r], hk[r], NT, preferred_element_type=F32)
        w = jnp.exp(s * scale)
        dacc[r] += first_lane(w)
        acc[r] += jnp.dot(w.astype(BF), hv[r], preferred_element_type=F32)
    steps = 4
    for j in range(dk.shape[0]):
        r = ctx[0] * dk.shape[0] + j
        s = lax.dot_general(q[r], dk[j], NT, preferred_element_type=F32)
        row = lax.rem(lax.broadcasted_iota(jnp.int32, s.shape, 0), steps)
        col = lax.broadcasted_iota(jnp.int32, s.shape, 1)
        w = jnp.where(col <= row, jnp.exp(s * scale), 0.0)
        dacc[r] += first_lane(w)
        acc[r] += jnp.dot(w.astype(BF), dv[j], preferred_element_type=F32)
    out[:, :, 0:128] = acc[...].astype(BF)
    den = jnp.sum(dacc[...], axis=2, keepdims=True)
    hi = den.astype(BF)
    lo = (den - hi.astype(F32)).astype(BF)
    out[:, :, 128:256] = jnp.where(lane[None] < 64, hi, lo)


def decode(req, lim, ctx, q, k, v, hk, hv, dk, dv):
    shape = q.shape
    return pl.pallas_call(
        decode_kernel,
        in_specs=[SM] * 3 + [VM] * 7,
        out_specs=VM,
        scratch_shapes=[pltpu.VMEM(shape, F32), pltpu.VMEM(shape, F32)],
        out_shape=jax.ShapeDtypeStruct((shape[0], shape[1], 256), BF),
        compiler_params=pltpu.CompilerParams(vmem_limit_bytes=16 << 20),
        cost_estimate=pl.CostEstimate(flops=10**8, bytes_accessed=3_000_000, transcendentals=10**5),
        name="decode_terms",
    )(req, lim, ctx, q, k, v, hk, hv, dk, dv)


def combine_kernel(o0, o1, o2, o3, dec, out, small):
    rows = o0.shape[0] - 16
    heads = o0.shape[1] // HD
    reqs = rows // 32
    refs = (o0, o1, o2, o3)

    def total(*at):
        t = refs[0][at].astype(F32)
        for ref in refs[1:]:
            t = t + ref[at].astype(F32)
        return t

    tail = total(pl.ds(rows, 16), pl.ds(0, 512))
    tail = tail[:, :256] + tail[:, 256:]
    den = jnp.concatenate([tail[:, :128], tail[:, 128:]], axis=0)
    for r in range(reqs):
        for h in range(heads):
            at = (pl.ds(r * 32, 32), pl.ds(h * 128, 128))
            out[at] = (total(*at) / den[:, r * 16 + h : r * 16 + h + 1]).astype(BF)
    sums = jnp.sum(dec[...].astype(F32), axis=0)
    reqs = sums.shape[0]
    dden = sums[:, :, 128:129] + sums[:, :, 192:193]
    live = lax.broadcasted_iota(jnp.int32, (1, 32, 1), 1) < heads * 4
    att = sums[:, :, :128] / jnp.where(live, dden, 1.0)
    small[...] = jnp.zeros_like(small)
    for j in range(reqs):
        for h in range(heads):
            small[j * 4 : j * 4 + 4, h * 128 : h * 128 + 128] = att[j, h * 4 : h * 4 + 4]
    out[rows : rows + 16] = small[...].astype(BF)


def combine(os, dec):
    shape = os[0].shape
    return pl.pallas_call(
        combine_kernel,
        in_specs=[VM] * 5,
        out_specs=VM,
        scratch_shapes=[pltpu.VMEM((16, shape[1]), F32)],
        out_shape=jax.ShapeDtypeStruct(shape, BF),
        compiler_params=pltpu.CompilerParams(vmem_limit_bytes=16 << 20),
        cost_estimate=pl.CostEstimate(flops=10**6, bytes_accessed=2_500_000, transcendentals=0),
        name="combine",
    )(*os, dec)


def project_kernel(at, x, w, o):
    o[...] = jnp.dot(x[...], w[...], preferred_element_type=F32)[: o.shape[0]].astype(BF)


def project_last_kernel(at, x, w, a, b, c, op, od):
    y = jnp.dot(x[...], w[...], preferred_element_type=F32)[: a.shape[0]]
    y = y + a[...].astype(F32) + b[...].astype(F32) + c[...].astype(F32)
    rows = op.shape[0]
    op[...] = y[:rows].astype(BF)
    od[...] = y[rows:].astype(BF)


def project(column, x, w, rows, parts, others=None):
    depth = x.shape[1]
    width = w.shape[1] // parts
    tile = 896
    tiles = width // tile
    xs = pl.BlockSpec(x.shape, lambda t, at: (0, 0))
    ws = pl.BlockSpec((depth, tile), lambda t, at: (0, at[0] * tiles + t))
    os = lambda n: pl.BlockSpec((n, tile), lambda t, at: (0, t))
    params = pltpu.CompilerParams(vmem_limit_bytes=32 << 20)
    cost = pl.CostEstimate(flops=2 * rows * depth * width, bytes_accessed=4_500_000, transcendentals=0)
    if others is None:
        spec = pltpu.PrefetchScalarGridSpec(
            num_scalar_prefetch=1, grid=(tiles,), in_specs=[xs, ws], out_specs=os(rows)
        )
        return pl.pallas_call(
            project_kernel, grid_spec=spec, out_shape=jax.ShapeDtypeStruct((rows, width), BF),
            compiler_params=params, cost_estimate=cost, name="project",
        )(column, x, w)
    main = rows - 8
    spec = pltpu.PrefetchScalarGridSpec(
        num_scalar_prefetch=1, grid=(tiles,), in_specs=[xs, ws] + [os(rows)] * 3, out_specs=[os(main), os(8)]
    )
    return pl.pallas_call(
        project_last_kernel, grid_spec=spec,
        out_shape=[jax.ShapeDtypeStruct((main, width), BF), jax.ShapeDtypeStruct((8, width), BF)],
        compiler_params=params, cost_estimate=cost, name="project_last",
    )(column, x, w, *others)


def sorted_tables(codes):
    index = jnp.arange(codes.shape[0], dtype=jnp.int32)
    rank = jnp.sum((codes[None, :] < codes[:, None]).astype(jnp.int32), axis=1)
    hit = rank[None, :] == index[:, None]
    order = jnp.sum(jnp.where(hit, index[None, :], 0), axis=1)
    lim = jnp.sum(jnp.where(hit, codes[None, :] & 255, 0), axis=1)
    owners = codes >> 16
    starts = jnp.sum((owners[None, :] < jnp.arange(9, dtype=jnp.int32)[:, None]).astype(jnp.int32), axis=1)
    return order, lim, starts


def visible_tokens(req, blk, bounds):
    count = bounds.shape[0]
    hit = req[:, None] == jnp.arange(count, dtype=jnp.int32)[None, :]
    bound = jnp.sum(jnp.where(hit, bounds[None, :], 0), axis=1)
    return jnp.clip(bound - blk * PAGE, 0, PAGE)


def on_device(
    p_query, p_key, p_value, p_cache_k, p_cache_v, p_slot_req, p_slot_blk, p_offsets,
    d_query, d_key, d_value, d_cache_k, d_cache_v, d_slot_req, d_slot_blk, d_lengths, out_weight,
):
    me = lax.axis_index("ctx")
    column = lax.axis_index("tp")
    ctx = lax.axis_size("ctx")
    tp = lax.axis_size("tp")

    def along_y(x, d):
        return lax.ppermute(x, "ctx", [(i, (i + 4 * d) % ctx) for i in range(ctx)])

    def across(x, bit):
        return lax.ppermute(x, "ctx", [(i, i ^ bit) for i in range(ctx)])

    def along_x(x, d):
        return lax.ppermute(x, "tp", [(i, (i + d) % tp) for i in range(tp)])

    heads = p_query.shape[3] // HD
    q0, k0, v0 = p_query[0], p_cache_k[0], p_cache_v[0]
    codes = (p_slot_req[0] * 256 + p_slot_blk[0]) * 256 + visible_tokens(
        p_slot_req[0], p_slot_blk[0], p_offsets[0]
    )
    qs = [q0, along_y(q0, 1), along_y(q0, -1), along_y(q0, 2)]
    k2, v2 = across(k0, 2), across(v0, 2)
    k1, v1 = across(k0, 1), across(v0, 1)
    span = jnp.stack([p_key[0], p_value[0]])
    spans = [span, across(span, 1), across(span, 2), across(span, 3)]
    handed = lax.ppermute(span, "sec", [(0, 1), (1, 0)])
    c1, c2, c3 = across(codes, 1), across(codes, 2), across(codes, 3)

    steps = d_query.shape[2]
    dq = d_query[0].reshape(2, steps, heads, HD).transpose(0, 2, 1, 3).reshape(2, steps * heads, HD)
    dq = jnp.pad(dq, ((0, 0), (0, 32 - steps * heads), (0, 0)))
    dq_all = lax.all_to_all(jnp.broadcast_to(dq[None], (ctx,) + dq.shape), "ctx", 0, 0)
    dq_all = dq_all.reshape(ctx * 2, 32, HD)
    pad = ((0, 0), (0, 16 - steps), (0, 0))
    dec = decode(
        d_slot_req[0],
        visible_tokens(d_slot_req[0], d_slot_blk[0], d_lengths[0]),
        me.reshape(1),
        dq_all,
        d_cache_k[0],
        d_cache_v[0],
        handed[0],
        handed[1],
        jnp.pad(d_key[0], pad),
        jnp.pad(d_value[0], pad),
    )
    dec = lax.all_to_all(dec.reshape(ctx, 2, 32, 256), "ctx", 0, 0)

    sources = jnp.stack([me, me - 4 + ctx, me + 4, me + 8]) % ctx
    bases = jnp.concatenate([sources, me ^ jnp.arange(4, dtype=jnp.int32)]).astype(jnp.int32) * 32
    joined_span = jnp.concatenate(spans, axis=2)
    near = attn(
        True, *sorted_tables(jnp.concatenate([codes, c1])), qs, (k0, k1, v0, v1),
        (bases, joined_span[0], joined_span[1]),
    )
    k3, v3 = across(k2, 1), across(v2, 1)
    o0, o1, o2, o3 = attn(False, *sorted_tables(jnp.concatenate([c2, c3])), qs, (k2, k3, v2, v3), near)
    parts = [o0, along_y(o1, -1), along_y(o2, 1), along_y(o3, 2)]
    joined = combine(parts, dec)

    rows = joined.shape[0] - 8
    share = lambda d: project(((column + d) % tp).reshape(1), joined, out_weight, rows, tp)
    far = along_x(share(2), 2)
    up = along_x(share(1), 1)
    down = along_x(share(3), -1)
    prefill_out, decode_out = project(column.reshape(1), joined, out_weight, rows, tp, (up, down, far))
    width = prefill_out.shape[1]
    return (
        prefill_out.reshape(1, p_query.shape[1], p_query.shape[2], width),
        decode_out.reshape(1, 2, steps, width),
    )


def solution(mesh):
    placed = (
        P("sec", None, "ctx", "tp"),
        P("sec", None, "ctx", "tp"),
        P("sec", None, "ctx", "tp"),
        P("sec", "ctx", None, "tp"),
        P("sec", "ctx", None, "tp"),
        P("sec", "ctx"),
        P("sec", "ctx"),
        P("sec", None),
        P("sec", "ctx", None, "tp"),
        P("sec", "ctx", None, "tp"),
        P("sec", "ctx", None, "tp"),
        P("sec", "ctx", None, "tp"),
        P("sec", "ctx", None, "tp"),
        P("sec", "ctx"),
        P("sec", "ctx"),
        P("sec", None),
        P("tp", None),
    )
    return jax.shard_map(
        on_device,
        mesh=mesh,
        in_specs=placed,
        out_specs=(P("sec", None, "ctx", "tp"), P("sec", "ctx", None, "tp")),
        check_vma=False,
    )
```

time: 565 us -> 220 us (0.39)
  waiting for transfers between devices: 216 us -> 95 us
  other arithmetic: 118 us -> 5.76 us
  matrix products: 99 us -> 0 us
  blocking collectives: 80.4 us -> 0 us
  Pallas kernels: 0 us -> 51.6 us
  starting transfers between devices: 4.83 us -> 36.8 us
  between operations: 15.8 us -> 0.88 us
    all_gather x4 -> x0, waiting for transfers between devices: 169 us -> none  [the longest x1 74.4 us: on_device(): lax.all_gather(p_cache_k[0], 'ctx', axis=0, tiled=True)]
    dot_general x19 -> x0, matrix products: 99 us -> none  [the longest x6 45.7 us: advance(): jnp.einsum('nhgqk,nkhd->nqhgd', weights.astype(jnp.bfloat16), value_rows,...]
    ppermute x2 -> x22, waiting for transfers between devices: 0.01 us -> 95 us  [the longest x3 36.9 us: along_x(): return lax.ppermute(x, 'tp', [(i, (i + d) % tp) for i in range(tp)])]
    scatter-add x13 -> x0, other arithmetic: 87.6 us -> none  [the longest x6 69.9 us: advance(): numerator = numerator.at[owner_ids].add(products)]
    unnamed x2 -> x0, blocking collectives: 58.9 us -> none
    pallas_call x0 -> x8, Pallas kernels: none -> 51.6 us  [the longest x1 18.5 us: attn(): pl.pallas_call(body, in_specs=[sm] * 4 + [vm] * 4 + [anyspec] * 4 + [vm]...]
    reduce_scatter x2 -> x0, waiting for transfers between devices: 44 us -> none  [the longest x1 44 us: on_device(): lax.psum_scatter(projected.astype(jnp.bfloat16), 'tp', scatter_dimension=...]
    ppermute x2 -> x22, starting transfers between devices: 4.6 us -> 28.1 us  [the longest x6 10.5 us: along_y(): return lax.ppermute(x, 'ctx', [(i, (i + 4 * d) % ctx) for i in range(ctx)])]
  transfers between devices with their start and end apart: 8 -> 24, of which waited for: 4 -> 7; matrix products, arithmetic and copies ran while one was open for 40% -> 4% of each run, Pallas kernels for 0% -> 21%
where the time goes in v1:
time: 220 us; the launch traced here: 217 us
  waiting for transfers between devices  95 us (43%)
  Pallas kernels  51.6 us (23%)
  starting transfers between devices  36.8 us (17%)
  local copies, waits for them, and re-layouts  27.4 us (12%)
  other arithmetic  5.76 us (3%)
    ppermute x3, waiting for transfers between devices, along_x(): return lax.ppermute(x, 'tp', [(i, (i + d) % tp) for i in range(tp)])  36.9 us
    ppermute x12, waiting for transfers between devices, across(): return lax.ppermute(x, 'ctx', [(i, i ^ bit) for i in range(ctx)])  33.4 us
    unnamed x40, local copies, waits for them, and re-layouts  23 us
    ppermute x6, waiting for transfers between devices, along_y(): return lax.ppermute(x, 'ctx', [(i, (i + 4 * d) % ctx) for i in range(ctx)])  21.3 us
    pallas_call x1, Pallas kernels, attn(): pl.pallas_call(body, in_specs=[sm] * 4 + [vm] * 4 + [anyspec] * 4 + [vm]...  18.5 us
    pallas_call x1, Pallas kernels, attn(): pl.pallas_call(body, in_specs=[sm] * 3 + [vm] * 4 + [anyspec] * 4 + [vm]...  17.4 us
    ppermute x6, starting transfers between devices, along_y(): return lax.ppermute(x, 'ctx', [(i, (i + 4 * d) % ctx) for i in range(ctx)])  10.5 us
    ppermute x12, starting transfers between devices, across(): return lax.ppermute(x, 'ctx', [(i, i ^ bit) for i in range(ctx)])  10.5 us
  transfers between devices with their start and end apart: 24, of which 7 were waited for; matrix products, arithmetic and copies ran while one was open for 4% of the time, Pallas kernels for 21%

profile of v1, /device:TPU:1, one launch (start us, length us, event | category | flops | bytes accessed | tf_op | source)
XLA Modules:
  0.0 217.4 jit_solution(6183635822872744528)
XLA Ops:
  2.3 1.5 collective-permute-start.12
  3.8 1.7 collective-permute-start.13
  7.4 1.8 collective-permute-start.1
  10.7 4.6 %all-to-all-start = ((bf16[16,2,32,128]{3,2,1,0:T(8,128)(2,1)}), bf16[16,2,32,128]{3,2,1,0:T(8,128)(2,1)S(1)}, u32[]{:S(2)}, u32[]{:S(2)}) async-start(bf16[16,2,32,128]{3,2,1,0:T(8,128)(2,1)} %broadcast_in_dim.93), calls=%async_computation | async-start | bytes 524288 | tf_op jit(solution)/shard_map/all_to_all | solution.py:334
  19.0 1.4 collective-permute-start.2
  20.4 1.2 collective-permute-start.5
  22.1 2.3 %collective-permute-start.14 = (bf16[2,8,32,128]{3,2,1,0:T(8,128)(2,1)S(1)}, bf16[2,8,32,128]{3,2,1,0:T(8,128)(2,1)S(1)}, u32[]{:S(2)}, u32[]{:S(2)}) collective-permute-start(bf16[2,8,32,128]{3,2,1,0:T(8,128)(2,1)S(1)} %constant_dynamic-update-slice_fusion), channel_id=1, source_target_pairs={{0,12},{4,8},{8,4},{12,0},{16,28},{20,24},{24,20},{28,16},{32,44},... | collective-permute-start | bytes 393224 | tf_op jit(solution)/shard_map/ppermute | solution.py:313
  24.6 1.6 collective-permute-start.3
  26.2 33.3 %collective-permute-done.14 = bf16[2,8,32,128]{3,2,1,0:T(8,128)(2,1)S(1)} collective-permute-done((bf16[2,8,32,128]{3,2,1,0:T(8,128)(2,1)S(1)}, bf16[2,8,32,128]{3,2,1,0:T(8,128)(2,1)S(1)}, u32[]{:S(2)}, u32[]{:S(2)}) %collective-permute-start.14) | collective-permute-done | bytes 131104 | tf_op jit(solution)/shard_map/ppermute | solution.py:313
  59.6 3.3 %collective-permute-start.18 = (bf16[2,8,32,128]{3,2,1,0:T(8,128)(2,1)S(1)}, bf16[2,8,32,128]{3,2,1,0:T(8,128)(2,1)S(1)}, u32[]{:S(2)}, u32[]{:S(2)}) collective-permute-start(bf16[2,8,32,128]{3,2,1,0:T(8,128)(2,1)S(1)} %constant_dynamic-update-slice_fusion), channel_id=1, source_target_pairs={{0,64},{64,0},{1,65},{65,1},{2,66},{66,2},{3,67},{67,3},{4,68},{68... | collective-permute-start | bytes 393224 | tf_op jit(solution)/shard_map/ppermute | solution.py:328
  63.1 3.5 %collective-permute-done.18 = bf16[2,8,32,128]{3,2,1,0:T(8,128)(2,1)S(1)} collective-permute-done((bf16[2,8,32,128]{3,2,1,0:T(8,128)(2,1)S(1)}, bf16[2,8,32,128]{3,2,1,0:T(8,128)(2,1)S(1)}, u32[]{:S(2)}, u32[]{:S(2)}) %collective-permute-start.18) | collective-permute-done | bytes 131104 | tf_op jit(solution)/shard_map/ppermute | solution.py:328
  68.9 2.4 %collective-permute-start.4 = (bf16[8,32,896]{2,1,0:T(8,128)(2,1)}, bf16[8,32,896]{2,1,0:T(8,128)(2,1)}, u32[]{:S(2)}, u32[]{:S(2)}) collective-permute-start(bf16[8,32,896]{2,1,0:T(8,128)(2,1)} %bitcast.75), channel_id=1, source_target_pairs={{0,32},{4,36},{8,40},{12,44},{16,48},{20,52},{24,56},{28,60},{32,0... | collective-permute-start | bytes 1376264 | tf_op jit(solution)/shard_map/ppermute | solution.py:310
  74.3 1.1 copy-done.3
  76.1 6.6 %decode_terms.1 = bf16[32,32,256]{2,1,0:T(8,128)(2,1)} custom-call(s32[24]{0:T(128)S(1)} %bitcast.66, s32[24]{0:T(128)S(1)} %fusion.1.lim, s32[1]{0:T(128)} %bitcast.9.ctx, bf16[32,32,128]{2,1,0:T(8,128)(2,1)S(1)} %bitcast.62, bf16[24,128,128]{2,1,0:T(8,128)(2,1)S(1)} %bitcast.63, bf16[24,128,128]{2,1,0:T(8,128)(2,1)S(1)} %bitcast.64, ...), custom_call_target="tpu_custom_call" | custom-call | flops 100000000 | bytes 3000000 | tf_op jit(solution)/shard_map/decode_terms/pallas_call | solution.py:184
  82.7 4.0 %all-to-all-start.1 = ((bf16[16,2,32,256]{3,2,1,0:T(8,128)(2,1)}), bf16[16,2,32,256]{3,2,1,0:T(8,128)(2,1)S(1)}, u32[]{:S(2)}, u32[]{:S(2)}) async-start(bf16[16,2,32,256]{3,2,1,0:T(8,128)(2,1)} %bitcast.27), calls=%async_computation.1 | async-start | bytes 1048576 | tf_op jit(solution)/shard_map/all_to_all | solution.py:349
  87.9 1.1 copy-done.6
  92.1 18.5 %attn_near.1 = (f32[8,896,128]{2,1,0:T(8,128)}, f32[128,128]{1,0:T(8,128)S(1)}) custom-call(s32[48]{0:T(128)S(1)} %get-tuple-element.19.order, s32[48]{0:T(128)S(1)} %get-tuple-element.18.lim, s32[9]{0:T(128)S(1)} %convert_reduce_fusion.2.starts, s32[8]{0:T(128)S(1)} %add_multiply_fusion.refs_0_, bf16[8,32,896]{2,1,0:T(8,128)(2,1)S(1)} %bitcast.76, ...), custom_call_target="tpu_custom_call" | custom-call | flops 2818572288 | bytes 12000000 | tf_op jit(solution)/shard_map/attn_near/pallas_call | solution.py:130
  113.7 17.4 %attn_far.1 = (bf16[272,896]{1,0:T(8,128)(2,1)S(1)}, bf16[272,896]{1,0:T(8,128)(2,1)}, bf16[272,896]{1,0:T(8,128)(2,1)}, bf16[272,896]{1,0:T(8,128)(2,1)S(1)}) custom-call(s32[48]{0:T(128)S(1)} %get-tuple-element.21.order, s32[48]{0:T(128)S(1)} %get-tuple-element.20.lim, s32[9]{0:T(128)S(1)} %convert_reduce_fusion.3.starts, ...), custom_call_target="tpu_custom_call" | custom-call | flops 2818572288 | bytes 12000000 | tf_op jit(solution)/shard_map/attn_far/pallas_call | solution.py:135
  131.0 3.4 %collective-permute-start.15 = (bf16[272,896]{1,0:T(8,128)(2,1)}, bf16[272,896]{1,0:T(8,128)(2,1)S(1)}, u32[]{:S(2)}, u32[]{:S(2)}) collective-permute-start(bf16[272,896]{1,0:T(8,128)(2,1)} %get-tuple-element.13), channel_id=1, source_target_pairs={{0,48},{4,52},{8,56},{12,60},{16,0},{20,4},{24,8},{28,12},{32,16},... | collective-permute-start | bytes 1462280 | tf_op jit(solution)/shard_map/ppermute | solution.py:310
  134.5 1.8 collective-permute-start.17
  136.2 19.0 %collective-permute-done.15.o1 = bf16[272,896]{1,0:T(8,128)(2,1)S(1)} collective-permute-done((bf16[272,896]{1,0:T(8,128)(2,1)}, bf16[272,896]{1,0:T(8,128)(2,1)S(1)}, u32[]{:S(2)}, u32[]{:S(2)}) %collective-permute-start.15) | collective-permute-done | bytes 487456 | tf_op jit(solution)/shard_map/ppermute | solution.py:310
  155.2 2.3 %collective-permute-done.17.o3 = bf16[272,896]{1,0:T(8,128)(2,1)S(1)} collective-permute-done((bf16[272,896]{1,0:T(8,128)(2,1)S(1)}, bf16[272,896]{1,0:T(8,128)(2,1)S(1)}, u32[]{:S(2)}, u32[]{:S(2)}) %collective-permute-start.17) | collective-permute-done | bytes 487456 | tf_op jit(solution)/shard_map/ppermute | solution.py:310
  158.1 4.6 %copy-done = bf16[896,7168]{1,0:T(8,128)(2,1)S(1)} copy-done((bf16[896,7168]{1,0:T(8,128)(2,1)S(1)}, bf16[896,7168]{1,0:T(8,128)(2,1)}, u32[]{:S(2)}) %copy-start) | copy-done | bytes 12845080
  162.7 1.9 project.4
  164.6 2.6 %collective-permute-start.20 = (bf16[264,1792]{1,0:T(8,128)(2,1)S(1)}, bf16[264,1792]{1,0:T(8,128)(2,1)S(1)}, u32[]{:S(2)}, u32[]{:S(2)}) collective-permute-start(bf16[264,1792]{1,0:T(8,128)(2,1)S(1)} %project.4), channel_id=1, source_target_pairs={{0,3},{1,0},{2,1},{3,2},{4,7},{5,4},{6,5},{7,6},{8,11},{9,8},{10,9... | collective-permute-start | bytes 2838536 | tf_op jit(solution)/shard_map/ppermute | solution.py:316
  167.1 1.9 project.5
  169.6 4.6 %copy-done.1 = bf16[896,7168]{1,0:T(8,128)(2,1)S(1)} copy-done((bf16[896,7168]{1,0:T(8,128)(2,1)S(1)}, bf16[896,7168]{1,0:T(8,128)(2,1)}, u32[]{:S(2)}) %copy-start.1) | copy-done | bytes 12845080
  174.3 1.9 project.3
  176.8 9.0 %collective-permute-done.20.b = bf16[264,1792]{1,0:T(8,128)(2,1)S(1)} collective-permute-done((bf16[264,1792]{1,0:T(8,128)(2,1)S(1)}, bf16[264,1792]{1,0:T(8,128)(2,1)S(1)}, u32[]{:S(2)}, u32[]{:S(2)}) %collective-permute-start.20) | collective-permute-done | bytes 946208 | tf_op jit(solution)/shard_map/ppermute | solution.py:316
  185.8 4.6 %collective-permute-done.21.c = bf16[264,1792]{1,0:T(8,128)(2,1)S(1)} collective-permute-done((bf16[264,1792]{1,0:T(8,128)(2,1)S(1)}, bf16[264,1792]{1,0:T(8,128)(2,1)S(1)}, u32[]{:S(2)}, u32[]{:S(2)}) %collective-permute-start.21) | collective-permute-done | bytes 946208 | tf_op jit(solution)/shard_map/ppermute | solution.py:316
  190.4 23.3 %collective-permute-done.19.a = bf16[264,1792]{1,0:T(8,128)(2,1)S(1)} collective-permute-done((bf16[264,1792]{1,0:T(8,128)(2,1)S(1)}, bf16[264,1792]{1,0:T(8,128)(2,1)S(1)}, u32[]{:S(2)}, u32[]{:S(2)}) %collective-permute-start.19) | collective-permute-done | bytes 946208 | tf_op jit(solution)/shard_map/ppermute | solution.py:316
  213.8 3.0 %project_last.1 = (bf16[256,1792]{1,0:T(8,128)(2,1)}, bf16[8,1792]{1,0:T(8,128)(2,1)S(1)}) custom-call(s32[1]{0:T(128)} %bitcast.at, bf16[272,896]{1,0:T(8,128)(2,1)S(1)} %combine.1.x, bf16[896,7168]{1,0:T(8,128)(2,1)S(1)} %bitcast.61, bf16[264,1792]{1,0:T(8,128)(2,1)S(1)} %collective-permute-done.19.a, bf16[264,1792]{1,0:T(8,128)(2,1)S(1)} %collective-permute-done.20.b, ...), custom_call_target="tpu_custom_call" | custom-call | flops 847773696 | bytes 4500000 | tf_op jit(solution)/shard_map/project_last/pallas_call | solution.py:275
  (93 shorter events, 25.4 us)
Async XLA Ops:
  2.3 19.8 %collective-permute-start.12 = (bf16[2,8,32,128]{3,2,1,0:T(8,128)(2,1)S(1)}, bf16[2,8,32,128]{3,2,1,0:T(8,128)(2,1)}, u32[]{:S(2)}, u32[]{:S(2)}) collective-permute-start(bf16[2,8,32,128]{3,2,1,0:T(8,128)(2,1)S(1)} %constant_dynamic-update-slice_fusion), channel_id=1, source_target_pairs={{0,4},{4,0},{8,12},{12,8},{16,20},{20,16},{24,28},{28,24},{32,36},... | collective-permute-start | bytes 393224 | tf_op jit(solution)/shard_map/ppermute | solution.py:313
  3.8 20.7 %collective-permute-start.13 = (bf16[2,8,32,128]{3,2,1,0:T(8,128)(2,1)S(1)}, bf16[2,8,32,128]{3,2,1,0:T(8,128)(2,1)}, u32[]{:S(2)}, u32[]{:S(2)}) collective-permute-start(bf16[2,8,32,128]{3,2,1,0:T(8,128)(2,1)S(1)} %constant_dynamic-update-slice_fusion), channel_id=1, source_target_pairs={{0,8},{4,12},{8,0},{12,4},{16,24},{20,28},{24,16},{28,20},{32,40},... | collective-permute-start | bytes 393224 | tf_op jit(solution)/shard_map/ppermute | solution.py:313
  7.0 14.7 %collective-permute-start.9 = (s32[24]{0:T(128)S(1)}, s32[24]{0:T(128)S(1)}, u32[]{:S(2)}, u32[]{:S(2)}) collective-permute-start(s32[24]{0:T(128)S(1)} %fusion.5), channel_id=1, source_target_pairs={{0,4},{4,0},{8,12},{12,8},{16,20},{20,16},{24,28},{28,24},{32,36},... | collective-permute-start | bytes 296 | tf_op jit(solution)/shard_map/ppermute | solution.py:313
  7.4 11.7 %collective-permute-start = (s32[24]{0:T(128)S(1)}, s32[24]{0:T(128)S(1)}, u32[]{:S(2)}, u32[]{:S(2)}) collective-permute-start(s32[24]{0:T(128)S(1)} %fusion.5), channel_id=1, source_target_pairs={{0,8},{4,12},{8,0},{12,4},{16,24},{20,28},{24,16},{28,20},{32,40},... | collective-permute-start | bytes 296 | tf_op jit(solution)/shard_map/ppermute | solution.py:313
  7.4 13.1 %collective-permute-start.1 = (s32[24]{0:T(128)S(1)}, s32[24]{0:T(128)S(1)}, u32[]{:S(2)}, u32[]{:S(2)}) collective-permute-start(s32[24]{0:T(128)S(1)} %fusion.5), channel_id=1, source_target_pairs={{0,12},{4,8},{8,4},{12,0},{16,28},{20,24},{24,20},{28,16},{32,44},... | collective-permute-start | bytes 296 | tf_op jit(solution)/shard_map/ppermute | solution.py:313
  10.7 62.5 %all-to-all-start = ((bf16[16,2,32,128]{3,2,1,0:T(8,128)(2,1)}), bf16[16,2,32,128]{3,2,1,0:T(8,128)(2,1)S(1)}, u32[]{:S(2)}, u32[]{:S(2)}) async-start(bf16[16,2,32,128]{3,2,1,0:T(8,128)(2,1)} %broadcast_in_dim.93), calls=%async_computation | async-start | bytes 524288 | tf_op jit(solution)/shard_map/all_to_all | solution.py:334
  19.0 48.0 %collective-permute-start.2 = (bf16[8,32,896]{2,1,0:T(8,128)(2,1)}, bf16[8,32,896]{2,1,0:T(8,128)(2,1)S(1)}, u32[]{:S(2)}, u32[]{:S(2)}) collective-permute-start(bf16[8,32,896]{2,1,0:T(8,128)(2,1)} %bitcast.73), channel_id=1, source_target_pairs={{0,16},{4,20},{8,24},{12,28},{16,32},{20,36},{24,40},{28,44},{32,4... | collective-permute-start | bytes 1376264 | tf_op jit(solution)/shard_map/ppermute | solution.py:310
  20.4 50.9 %collective-permute-start.5 = (bf16[24,128,128]{2,1,0:T(8,128)(2,1)}, bf16[24,128,128]{2,1,0:T(8,128)(2,1)S(1)}, u32[]{:S(2)}, u32[]{:S(2)}) collective-permute-start(bf16[24,128,128]{2,1,0:T(8,128)(2,1)} %bitcast.67), channel_id=1, source_target_pairs={{0,8},{4,12},{8,0},{12,4},{16,24},{20,28},{24,16},{28,20},{32,40},... | collective-permute-start | bytes 2359304 | tf_op jit(solution)/shard_map/ppermute | solution.py:313
  21.7 50.3 %collective-permute-start.7 = (bf16[24,128,128]{2,1,0:T(8,128)(2,1)}, bf16[24,128,128]{2,1,0:T(8,128)(2,1)S(1)}, u32[]{:S(2)}, u32[]{:S(2)}) collective-permute-start(bf16[24,128,128]{2,1,0:T(8,128)(2,1)} %bitcast.70), channel_id=1, source_target_pairs={{0,8},{4,12},{8,0},{12,4},{16,24},{20,28},{24,16},{28,20},{32,40},... | collective-permute-start | bytes 2359304 | tf_op jit(solution)/shard_map/ppermute | solution.py:313
  22.1 37.5 %collective-permute-start.14 = (bf16[2,8,32,128]{3,2,1,0:T(8,128)(2,1)S(1)}, bf16[2,8,32,128]{3,2,1,0:T(8,128)(2,1)S(1)}, u32[]{:S(2)}, u32[]{:S(2)}) collective-permute-start(bf16[2,8,32,128]{3,2,1,0:T(8,128)(2,1)S(1)} %constant_dynamic-update-slice_fusion), channel_id=1, source_target_pairs={{0,12},{4,8},{8,4},{12,0},{16,28},{20,24},{24,20},{28,16},{32,44},... | collective-permute-start | bytes 393224 | tf_op jit(solution)/shard_map/ppermute | solution.py:313
  24.6 43.6 %collective-permute-start.3 = (bf16[8,32,896]{2,1,0:T(8,128)(2,1)}, bf16[8,32,896]{2,1,0:T(8,128)(2,1)S(1)}, u32[]{:S(2)}, u32[]{:S(2)}) collective-permute-start(bf16[8,32,896]{2,1,0:T(8,128)(2,1)} %bitcast.74), channel_id=1, source_target_pairs={{0,48},{4,52},{8,56},{12,60},{16,0},{20,4},{24,8},{28,12},{32,16},... | collective-permute-start | bytes 1376264 | tf_op jit(solution)/shard_map/ppermute | solution.py:310
  59.6 7.1 %collective-permute-start.18 = (bf16[2,8,32,128]{3,2,1,0:T(8,128)(2,1)S(1)}, bf16[2,8,32,128]{3,2,1,0:T(8,128)(2,1)S(1)}, u32[]{:S(2)}, u32[]{:S(2)}) collective-permute-start(bf16[2,8,32,128]{3,2,1,0:T(8,128)(2,1)S(1)} %constant_dynamic-update-slice_fusion), channel_id=1, source_target_pairs={{0,64},{64,0},{1,65},{65,1},{2,66},{66,2},{3,67},{67,3},{4,68},{68... | collective-permute-start | bytes 393224 | tf_op jit(solution)/shard_map/ppermute | solution.py:328
  66.6 20.2 %collective-permute-start.10 = (bf16[24,128,128]{2,1,0:T(8,128)(2,1)}, bf16[24,128,128]{2,1,0:T(8,128)(2,1)S(1)}, u32[]{:S(2)}, u32[]{:S(2)}) collective-permute-start(bf16[24,128,128]{2,1,0:T(8,128)(2,1)} %bitcast.68), channel_id=1, source_target_pairs={{0,4},{4,0},{8,12},{12,8},{16,20},{20,16},{24,28},{28,24},{32,36},... | collective-permute-start | bytes 2359304 | tf_op jit(solution)/shard_map/ppermute | solution.py:313
  67.8 19.0 %collective-permute-start.11 = (bf16[24,128,128]{2,1,0:T(8,128)(2,1)}, bf16[24,128,128]{2,1,0:T(8,128)(2,1)}, u32[]{:S(2)}, u32[]{:S(2)}) collective-permute-start(bf16[24,128,128]{2,1,0:T(8,128)(2,1)} %bitcast.71), channel_id=1, source_target_pairs={{0,4},{4,0},{8,12},{12,8},{16,20},{20,16},{24,28},{28,24},{32,36},... | collective-permute-start | bytes 2359304 | tf_op jit(solution)/shard_map/ppermute | solution.py:313
  68.9 17.9 %collective-permute-start.4 = (bf16[8,32,896]{2,1,0:T(8,128)(2,1)}, bf16[8,32,896]{2,1,0:T(8,128)(2,1)}, u32[]{:S(2)}, u32[]{:S(2)}) collective-permute-start(bf16[8,32,896]{2,1,0:T(8,128)(2,1)} %bitcast.75), channel_id=1, source_target_pairs={{0,32},{4,36},{8,40},{12,44},{16,48},{20,52},{24,56},{28,60},{32,0... | collective-permute-start | bytes 1376264 | tf_op jit(solution)/shard_map/ppermute | solution.py:310
  71.3 39.3 %collective-permute-start.6 = (bf16[24,128,128]{2,1,0:T(8,128)(2,1)S(1)}, bf16[24,128,128]{2,1,0:T(8,128)(2,1)}, u32[]{:S(2)}, u32[]{:S(2)}) collective-permute-start(bf16[24,128,128]{2,1,0:T(8,128)(2,1)S(1)} %collective-permute-done.5.refs_4_), channel_id=1, source_target_pairs={{0,4},{4,0},{8,12},{12,8},{16,20},{20,16},{24,28},{28,24},{32,36},... | collective-permute-start | bytes 2359304 | tf_op jit(solution)/shard_map/ppermute | solution.py:313
  72.0 38.6 %collective-permute-start.8 = (bf16[24,128,128]{2,1,0:T(8,128)(2,1)S(1)}, bf16[24,128,128]{2,1,0:T(8,128)(2,1)}, u32[]{:S(2)}, u32[]{:S(2)}) collective-permute-start(bf16[24,128,128]{2,1,0:T(8,128)(2,1)S(1)} %collective-permute-done.7.refs_6_), channel_id=1, source_target_pairs={{0,4},{4,0},{8,12},{12,8},{16,20},{20,16},{24,28},{28,24},{32,36},... | collective-permute-start | bytes 2359304 | tf_op jit(solution)/shard_map/ppermute | solution.py:313
  73.2 1.1 copy-start.2
  82.7 53.5 %all-to-all-start.1 = ((bf16[16,2,32,256]{3,2,1,0:T(8,128)(2,1)}), bf16[16,2,32,256]{3,2,1,0:T(8,128)(2,1)S(1)}, u32[]{:S(2)}, u32[]{:S(2)}) async-start(bf16[16,2,32,256]{3,2,1,0:T(8,128)(2,1)} %bitcast.27), calls=%async_computation.1 | async-start | bytes 1048576 | tf_op jit(solution)/shard_map/all_to_all | solution.py:349
  86.8 1.1 copy-start.5
  131.0 24.2 %collective-permute-start.15 = (bf16[272,896]{1,0:T(8,128)(2,1)}, bf16[272,896]{1,0:T(8,128)(2,1)S(1)}, u32[]{:S(2)}, u32[]{:S(2)}) collective-permute-start(bf16[272,896]{1,0:T(8,128)(2,1)} %get-tuple-element.13), channel_id=1, source_target_pairs={{0,48},{4,52},{8,56},{12,60},{16,0},{20,4},{24,8},{28,12},{32,16},... | collective-permute-start | bytes 1462280 | tf_op jit(solution)/shard_map/ppermute | solution.py:310
  134.5 20.8 %collective-permute-start.16 = (bf16[272,896]{1,0:T(8,128)(2,1)}, bf16[272,896]{1,0:T(8,128)(2,1)S(1)}, u32[]{:S(2)}, u32[]{:S(2)}) collective-permute-start(bf16[272,896]{1,0:T(8,128)(2,1)} %get-tuple-element.14), channel_id=1, source_target_pairs={{0,16},{4,20},{8,24},{12,28},{16,32},{20,36},{24,40},{28,44},{32,4... | collective-permute-start | bytes 1462280 | tf_op jit(solution)/shard_map/ppermute | solution.py:310
  134.5 23.0 %collective-permute-start.17 = (bf16[272,896]{1,0:T(8,128)(2,1)S(1)}, bf16[272,896]{1,0:T(8,128)(2,1)S(1)}, u32[]{:S(2)}, u32[]{:S(2)}) collective-permute-start(bf16[272,896]{1,0:T(8,128)(2,1)S(1)} %get-tuple-element.15), channel_id=1, source_target_pairs={{0,32},{4,36},{8,40},{12,44},{16,48},{20,52},{24,56},{28,60},{32,0... | collective-permute-start | bytes 1462280 | tf_op jit(solution)/shard_map/ppermute | solution.py:310
  158.0 4.7 %copy-start = (bf16[896,7168]{1,0:T(8,128)(2,1)S(1)}, bf16[896,7168]{1,0:T(8,128)(2,1)}, u32[]{:S(2)}) copy-start(bf16[896,7168]{1,0:T(8,128)(2,1)} %w.7) | copy-start | bytes 38535172
  162.7 51.1 %slice-start = ((s8[12845056]{0:T(1024)(128)(4,1)}), s8[4194304]{0:T(1024)(128)(4,1)S(1)}, s32[]{:S(2)}) async-start(s8[12845056]{0:T(1024)(128)(4,1)} %bitcast.60), calls=%async_computation.2 | async-start | bytes 8388608
  162.7 51.1 %slice-start.1 = ((s8[12845056]{0:T(1024)(128)(4,1)}), s8[4194304]{0:T(1024)(128)(4,1)S(1)}, s32[]{:S(2)}) async-start(s8[12845056]{0:T(1024)(128)(4,1)} %bitcast.60), calls=%async_computation.3 | async-start | bytes 8388608
  164.6 21.2 %collective-permute-start.20 = (bf16[264,1792]{1,0:T(8,128)(2,1)S(1)}, bf16[264,1792]{1,0:T(8,128)(2,1)S(1)}, u32[]{:S(2)}, u32[]{:S(2)}) collective-permute-start(bf16[264,1792]{1,0:T(8,128)(2,1)S(1)} %project.4), channel_id=1, source_target_pairs={{0,3},{1,0},{2,1},{3,2},{4,7},{5,4},{6,5},{7,6},{8,11},{9,8},{10,9... | collective-permute-start | bytes 2838536 | tf_op jit(solution)/shard_map/ppermute | solution.py:316
  167.1 46.6 %slice-start.2 = ((s8[12845056]{0:T(1024)(128)(4,1)}), s8[4194304]{0:T(1024)(128)(4,1)S(1)}, s32[]{:S(2)}) async-start(s8[12845056]{0:T(1024)(128)(4,1)} %bitcast.60), calls=%async_computation.4 | async-start | bytes 8388608
  169.0 21.4 %collective-permute-start.21 = (bf16[264,1792]{1,0:T(8,128)(2,1)S(1)}, bf16[264,1792]{1,0:T(8,128)(2,1)S(1)}, u32[]{:S(2)}, u32[]{:S(2)}) collective-permute-start(bf16[264,1792]{1,0:T(8,128)(2,1)S(1)} %project.5), channel_id=1, source_target_pairs={{0,2},{1,3},{2,0},{3,1},{4,6},{5,7},{6,4},{7,5},{8,10},{9,11},{10,... | collective-permute-start | bytes 2838536 | tf_op jit(solution)/shard_map/ppermute | solution.py:316
  169.6 4.7 %copy-start.1 = (bf16[896,7168]{1,0:T(8,128)(2,1)S(1)}, bf16[896,7168]{1,0:T(8,128)(2,1)}, u32[]{:S(2)}) copy-start(bf16[896,7168]{1,0:T(8,128)(2,1)} %w.7) | copy-start | bytes 38535172
  174.3 39.5 %slice-start.3 = ((s8[12845056]{0:T(1024)(128)(4,1)}), s8[262144]{0:T(1024)(128)(4,1)S(1)}, s32[]{:S(2)}) async-start(s8[12845056]{0:T(1024)(128)(4,1)} %bitcast.60), calls=%async_computation.5 | async-start | bytes 524288
  176.2 37.6 %collective-permute-start.19 = (bf16[264,1792]{1,0:T(8,128)(2,1)S(1)}, bf16[264,1792]{1,0:T(8,128)(2,1)S(1)}, u32[]{:S(2)}, u32[]{:S(2)}) collective-permute-start(bf16[264,1792]{1,0:T(8,128)(2,1)S(1)} %project.3), channel_id=1, source_target_pairs={{0,1},{1,2},{2,3},{3,0},{4,5},{5,6},{6,7},{7,4},{8,9},{9,10},{10,1... | collective-permute-start | bytes 2838536 | tf_op jit(solution)/shard_map/ppermute | solution.py:316
  (11 other events, 10.6 us)

commit v2 on v1

v2 whole, which is shorter than its diff:
```python
import functools

import jax
import jax.numpy as jnp
from jax import lax
from jax.experimental import pallas as pl
from jax.experimental.pallas import tpu as pltpu
from jax.sharding import PartitionSpec as P

HD = 128
PAGE = 128
BF = jnp.bfloat16
F32 = jnp.float32
NT = (((1,), (1,)), ((), ()))
NB = 4
VM = pl.BlockSpec(memory_space=pltpu.VMEM)
SM = pl.BlockSpec(memory_space=pltpu.SMEM)
HBM = pl.BlockSpec(memory_space=pl.ANY)


def attn_kernel(order, lim, starts, *refs, first, r0, R, heads, half):
    rows = heads * 128
    if first:
        (bases, q0, q1, q2, q3, ka, kb, va, vb, span, num_a, num_b, qs_out, den,
         qv, qs, ks, vs, sk, num, dacc, tile, sem) = refs
    else:
        (qs_in, ka, kb, va, vb, num_in, den_in, o0, o1, o2, o3, qs, ks, vs, num, acc, dacc, sem) = refs
    cs = []

    def copy(src, dst, i):
        c = pltpu.make_async_copy(src, dst, sem.at[i])
        c.start()
        return c

    if first:
        qc = [copy(q, qv.at[d], 4 + d) for d, q in enumerate((q0, q1, q2, q3))]
        cs = [copy(span, sk, 8)]
    else:
        cs = [copy(qs_in.at[pl.ds(r0, R)], qs, 4)]
    cs += [
        copy(ka, ks.at[pl.ds(0, half)], 0),
        copy(kb, ks.at[pl.ds(half, half)], 1),
        copy(va, vs.at[pl.ds(0, half)], 2),
        copy(vb, vs.at[pl.ds(half, half)], 3),
    ]
    if not first:
        num_copy = copy(num_in, num, 5)
    if first:
        rowi = lax.broadcasted_iota(jnp.int32, (128, 128), 0)
        coli = lax.broadcasted_iota(jnp.int32, (128, 128), 1)

        def pick(i, b):
            g = i // 32
            base = jnp.where(g == 0, bases[b], jnp.where(g == 1, bases[b + 1], jnp.where(g == 2, bases[b + 2], bases[b + 3])))
            return base + lax.rem(i, 32)

        tile[...] = jnp.where(pick(rowi, 0) >= pick(coli, 4), 1.0, 0.0)
        for d in range(4):
            qc[d].wait()
            for r in range(R):
                for h in range(heads):
                    qs[r, pl.ds(h * 128 + d * 32, 32), :] = qv[d, r, :, pl.ds(h * 128, 128)]
        qs_copy = copy(qs, qs_out, 4)
    for c in cs:
        c.wait()
    lane1 = lax.broadcasted_iota(jnp.int32, (128, 128), 1)
    lane = lax.broadcasted_iota(jnp.int32, (1, 128), 1)
    if not first:
        num_copy.wait()

    def request(r, dtile):
        s0 = starts[r0 + r]
        n = starts[r0 + r + 1] - s0
        nref = num.at[r] if first else acc

        def fetch(i):
            ok = i < n
            s = jnp.where(ok, s0 + i, 0)
            b = order[s]
            return ks[b], vs[b], jnp.where(ok, lim[s], 0)

        def weights(Ks, ms):
            K = jnp.concatenate(Ks, axis=0)
            sc = lax.dot_general(qs[r], K, NT, preferred_element_type=F32)
            w = jnp.exp(sc * HD ** -0.5)
            return [m(w[:, j * 128 : (j + 1) * 128]) for j, m in enumerate(ms)]

        def keep(l):
            return lambda w: jnp.where(lane < l, w, 0.0)

        def causal(w):
            return jnp.where(tile[...][None] > 0.5, w.reshape(heads, 128, 128), 0.0).reshape(rows, 128)

        def total(ws):
            t = ws[0]
            for w in ws[1:]:
                t = t + w
            return t

        def product(ws, Vs):
            return jnp.dot(
                jnp.concatenate([w.astype(BF) for w in ws], axis=1),
                jnp.concatenate(Vs, axis=0),
                preferred_element_type=F32,
            )

        skip = 0
        if first:
            f = [fetch(i) for i in range(NB - 1)]
            ws = weights([sk[0, r]] + [x[0] for x in f], [causal] + [keep(x[2]) for x in f])
            dacc[...] = total(ws)
            nref[...] = product(ws, [sk[1, r]] + [x[1] for x in f])
            skip = NB - 1
        else:
            acc[...] = jnp.zeros_like(acc)
            dacc[...] = jnp.zeros_like(dacc)

        def step(p, unused):
            f = [fetch(skip + NB * p + i) for i in range(NB)]
            ws = weights([x[0] for x in f], [keep(x[2]) for x in f])
            dacc[...] += total(ws)
            nref[...] += product(ws, [x[1] for x in f])
            return 0

        lax.fori_loop(0, (jnp.maximum(n - skip, 0) + NB - 1) // NB, step, 0)
        upd = dtile
        for h in range(heads):
            col = jnp.sum(dacc[pl.ds(h * 128, 128), :], axis=1, keepdims=True)
            upd = upd + jnp.where(lane1 == (r0 + r) * 16 + h, col, 0.0)
        if not first:
            outs = (o0, o1, o2, o3)
            for h in range(heads):
                for d in range(4):
                    sl = pl.ds(h * 128 + d * 32, 32)
                    outs[d][pl.ds(pl.multiple_of(r * 32, 32), 32), pl.ds(h * 128, 128)] = (
                        num[r, sl, :] + acc[sl, :]
                    ).astype(BF)
        return upd

    init = jnp.zeros((128, 128), F32) if first else den_in[...]
    dl = lax.fori_loop(0, R, request, init)
    if first:
        den[...] = dl
        na = copy(num.at[pl.ds(0, R // 2)], num_a, 0)
        nb = copy(num.at[pl.ds(R // 2, R // 2)], num_b, 1)
        na.wait()
        nb.wait()
        qs_copy.wait()
    else:
        outs = (o0, o1, o2, o3)
        dl = dl[:, r0 * 16 : r0 * 16 + 64]
        hi = dl.astype(BF).astype(F32)
        both = jnp.concatenate([hi, dl - hi], axis=1).astype(BF)
        z = jnp.zeros((16, (heads - 2) * 128), BF)
        for d in range(4):
            outs[d][R * 32 : R * 32 + 16, 0:128] = both[d * 32 : d * 32 + 16]
            outs[d][R * 32 : R * 32 + 16, 128:256] = both[d * 32 + 16 : d * 32 + 32]
            outs[d][R * 32 : R * 32 + 16, 256:] = z


def attn_near(order, lim, starts, bases, qs, kv, span):
    R, T, W = qs[0].shape
    heads = W // HD
    rows = heads * 128
    nb = order.shape[0]
    body = functools.partial(attn_kernel, first=True, r0=0, R=R, heads=heads, half=nb // 2)
    return pl.pallas_call(
        body,
        in_specs=[SM] * 4 + [HBM] * 9,
        out_specs=[HBM, HBM, HBM, VM],
        scratch_shapes=[
            pltpu.VMEM((4, R, T, W), BF),
            pltpu.VMEM((R, rows, 128), BF),
            pltpu.VMEM((nb, 128, 128), BF),
            pltpu.VMEM((nb, 128, 128), BF),
            pltpu.VMEM(span.shape, BF),
            pltpu.VMEM((R, rows, 128), F32),
            pltpu.VMEM((rows, 128), F32),
            pltpu.VMEM((128, 128), F32),
            pltpu.SemaphoreType.DMA((9,)),
        ],
        out_shape=[
            jax.ShapeDtypeStruct((R // 2, rows, 128), F32),
            jax.ShapeDtypeStruct((R // 2, rows, 128), F32),
            jax.ShapeDtypeStruct((R, rows, 128), BF),
            jax.ShapeDtypeStruct((128, 128), F32),
        ],
        compiler_params=pltpu.CompilerParams(vmem_limit_bytes=48 << 20),
        cost_estimate=pl.CostEstimate(flops=4 * nb * rows * 128 * 128, bytes_accessed=12_000_000, transcendentals=nb * rows * 128),
        name="attn_near",
    )(order, lim, starts, bases, *qs, *kv, span)


def attn_far(order, lim, starts, r0, qs, kv, num, den, T, W):
    R = num.shape[0]
    heads = W // HD
    rows = heads * 128
    nb = order.shape[0]
    body = functools.partial(attn_kernel, first=False, r0=r0, R=R, heads=heads, half=nb // 2)
    return pl.pallas_call(
        body,
        in_specs=[SM] * 3 + [HBM] * 6 + [VM],
        out_specs=[VM] * 4,
        scratch_shapes=[
            pltpu.VMEM((R, rows, 128), BF),
            pltpu.VMEM((nb, 128, 128), BF),
            pltpu.VMEM((nb, 128, 128), BF),
            pltpu.VMEM((R, rows, 128), F32),
            pltpu.VMEM((rows, 128), F32),
            pltpu.VMEM((rows, 128), F32),
            pltpu.SemaphoreType.DMA((6,)),
        ],
        out_shape=[jax.ShapeDtypeStruct((R * T + 16, W), BF)] * 4,
        compiler_params=pltpu.CompilerParams(vmem_limit_bytes=48 << 20),
        cost_estimate=pl.CostEstimate(flops=2 * nb * rows * 128 * 128, bytes_accessed=12_000_000, transcendentals=nb * rows * 64),
        name="attn_far",
    )(order, lim, starts, qs, *kv, num, den)


def decode_kernel(req, lim, ctx, q, k, v, hk, hv, dk, dv, out, acc, dacc):
    scale = HD ** -0.5
    blocks = k.shape[0]
    handed = hk.shape[0]
    lane = lax.broadcasted_iota(jnp.int32, (1, 128), 1)
    acc[...] = jnp.zeros_like(acc)
    dacc[...] = jnp.zeros_like(dacc)

    def block(i, unused):
        r = req[i]
        s = lax.dot_general(q[r], k[i], NT, preferred_element_type=F32)
        w = jnp.where(lane < lim[i], jnp.exp(s * scale), 0.0)
        dacc[r] += w
        acc[r] += jnp.dot(w.astype(BF), v[i], preferred_element_type=F32)
        return 0

    lax.fori_loop(0, blocks, block, 0, unroll=True)

    def first_lane(w):
        return jnp.where(lane == 0, jnp.sum(w, axis=1, keepdims=True), 0.0)

    for r in range(handed):
        s = lax.dot_general(q[r], hk[r], NT, preferred_element_type=F32)
        w = jnp.exp(s * scale)
        dacc[r] += first_lane(w)
        acc[r] += jnp.dot(w.astype(BF), hv[r], preferred_element_type=F32)
    steps = 4
    for j in range(dk.shape[0]):
        r = ctx[0] * dk.shape[0] + j
        s = lax.dot_general(q[r], dk[j], NT, preferred_element_type=F32)
        row = lax.rem(lax.broadcasted_iota(jnp.int32, s.shape, 0), steps)
        col = lax.broadcasted_iota(jnp.int32, s.shape, 1)
        w = jnp.where(col <= row, jnp.exp(s * scale), 0.0)
        dacc[r] += first_lane(w)
        acc[r] += jnp.dot(w.astype(BF), dv[j], preferred_element_type=F32)
    out[:, :, 0:128] = acc[...].astype(BF)
    den = jnp.sum(dacc[...], axis=2, keepdims=True)
    hi = den.astype(BF)
    lo = (den - hi.astype(F32)).astype(BF)
    out[:, :, 128:256] = jnp.where(lane[None] < 64, hi, lo)


def decode(req, lim, ctx, q, k, v, hk, hv, dk, dv):
    shape = q.shape
    return pl.pallas_call(
        decode_kernel,
        in_specs=[SM] * 3 + [VM] * 7,
        out_specs=VM,
        scratch_shapes=[pltpu.VMEM(shape, F32), pltpu.VMEM(shape, F32)],
        out_shape=jax.ShapeDtypeStruct((shape[0], shape[1], 256), BF),
        compiler_params=pltpu.CompilerParams(vmem_limit_bytes=16 << 20),
        cost_estimate=pl.CostEstimate(flops=10**8, bytes_accessed=3_000_000, transcendentals=10**5),
        name="decode_terms",
    )(req, lim, ctx, q, k, v, hk, hv, dk, dv)


def combine_kernel(*refs, decode_rows):
    if decode_rows:
        o0, o1, o2, o3, dec, out, small = refs
    else:
        o0, o1, o2, o3, out = refs
    rows = o0.shape[0] - 16
    heads = o0.shape[1] // HD
    parts = (o0, o1, o2, o3)

    def total(*at):
        t = parts[0][at].astype(F32)
        for ref in parts[1:]:
            t = t + ref[at].astype(F32)
        return t

    tail = total(pl.ds(rows, 16), pl.ds(0, 256))
    den = jnp.concatenate([tail[:, :128], tail[:, 128:]], axis=0)
    den = den[:, :64] + den[:, 64:]
    for r in range(rows // 32):
        for h in range(heads):
            at = (pl.ds(r * 32, 32), pl.ds(h * 128, 128))
            out[at] = (total(*at) / den[:, r * 16 + h : r * 16 + h + 1]).astype(BF)
    if not decode_rows:
        return
    sums = jnp.sum(dec[...].astype(F32), axis=0)
    reqs = sums.shape[0]
    dden = sums[:, :, 128:129] + sums[:, :, 192:193]
    att = sums[:, :, :128] / dden
    small[...] = jnp.zeros_like(small)
    for j in range(reqs):
        for h in range(heads):
            small[j * 4 : j * 4 + 4, h * 128 : h * 128 + 128] = att[j, h * 4 : h * 4 + 4]
    out[rows : rows + 16] = small[...].astype(BF)


def combine(os, dec=None):
    rows, width = os[0].shape
    more = [] if dec is None else [dec]
    out_rows = rows if more else rows - 16
    return pl.pallas_call(
        functools.partial(combine_kernel, decode_rows=len(more)),
        in_specs=[VM] * (4 + len(more)),
        out_specs=VM,
        scratch_shapes=[pltpu.VMEM((16, width), F32)] * len(more),
        out_shape=jax.ShapeDtypeStruct((out_rows, width), BF),
        compiler_params=pltpu.CompilerParams(vmem_limit_bytes=16 << 20),
        cost_estimate=pl.CostEstimate(flops=10**6, bytes_accessed=2_500_000, transcendentals=0),
        name="combine",
    )(*os, *more)


def project_kernel(own, other, x0, x1, x2, x3, w0, a1, a2, a3, b1, b2, b3, *outs):
    def run(ws):
        y = jnp.dot(x0[...], w0[...], preferred_element_type=F32)
        for x, w in zip((x1, x2, x3), ws):
            y = y + jnp.dot(x[...], w[...], preferred_element_type=F32)
        rows = outs[0].shape[0]
        outs[0][...] = y[:rows].astype(BF)
        if len(outs) > 1:
            outs[1][...] = y[rows : rows + outs[1].shape[0]].astype(BF)

    @pl.when(pl.program_id(0) == 0)
    def _():
        run((a1, a2, a3))

    @pl.when(pl.program_id(0) == 1)
    def _():
        run((b1, b2, b3))


def project(own, other, xs, w, mine, theirs, small):
    rows, depth = xs[0].shape
    half = mine[0].shape[1]
    full = lambda a: pl.BlockSpec(a.shape, lambda t, o, q: (0, 0))
    side = lambda t, o, q: jnp.where(t == 0, o[0], q[0])
    main = rows - (16 if small else 0)
    shapes = [jax.ShapeDtypeStruct((main, 2 * half), BF)]
    out_specs = [pl.BlockSpec((main, half), lambda t, o, q: (0, lax.rem(side(t, o, q), 2)))]
    if small:
        shapes.append(jax.ShapeDtypeStruct((small, 2 * half), BF))
        out_specs.append(pl.BlockSpec((small, half), lambda t, o, q: (0, lax.rem(side(t, o, q), 2))))
    spec = pltpu.PrefetchScalarGridSpec(
        num_scalar_prefetch=2,
        grid=(2,),
        in_specs=[full(x) for x in xs]
        + [pl.BlockSpec((depth, half), lambda t, o, q: (0, side(t, o, q)))]
        + [full(a) for a in mine + theirs],
        out_specs=out_specs,
    )
    return pl.pallas_call(
        project_kernel,
        grid_spec=spec,
        out_shape=shapes,
        compiler_params=pltpu.CompilerParams(vmem_limit_bytes=48 << 20),
        cost_estimate=pl.CostEstimate(flops=8 * rows * depth * 2 * half, bytes_accessed=14_000_000, transcendentals=0),
        name="project",
    )(own, other, *xs, w, *mine, *theirs)


def sorted_tables(req, lim):
    index = jnp.arange(req.shape[0], dtype=jnp.int32)
    key = req * 256 + index
    rank = jnp.sum((key[None, :] < key[:, None]).astype(jnp.int32), axis=1)
    hit = rank[None, :] == index[:, None]
    order = jnp.sum(jnp.where(hit, index[None, :], 0), axis=1)
    lims = jnp.sum(jnp.where(hit, lim[None, :], 0), axis=1)
    starts = jnp.sum((req[None, :] < jnp.arange(9, dtype=jnp.int32)[:, None]).astype(jnp.int32), axis=1)
    return order, lims, starts


def visible_tokens(req, blk, bounds):
    count = bounds.shape[0]
    hit = req[:, None] == jnp.arange(count, dtype=jnp.int32)[None, :]
    bound = jnp.sum(jnp.where(hit, bounds[None, :], 0), axis=1)
    return jnp.clip(bound - blk * PAGE, 0, PAGE)


def on_device(
    p_query, p_key, p_value, p_cache_k, p_cache_v, p_slot_req, p_slot_blk, p_offsets,
    d_query, d_key, d_value, d_cache_k, d_cache_v, d_slot_req, d_slot_blk, d_lengths, out_weight,
):
    me = lax.axis_index("ctx")
    column = lax.axis_index("tp")
    core = me % 2
    ctx = lax.axis_size("ctx")
    tp = lax.axis_size("tp")

    def along_y(x, d):
        return lax.ppermute(x, "ctx", [(i, (i + 4 * d) % ctx) for i in range(ctx)])

    def across(x, bit):
        return lax.ppermute(x, "ctx", [(i, i ^ bit) for i in range(ctx)])

    def along_x(x, d):
        return lax.ppermute(x, "tp", [(i, (i + d) % tp) for i in range(tp)])

    heads = p_query.shape[3] // HD
    reqs, span_len = p_query.shape[1:3]
    slots = p_slot_req.shape[1]
    steps = d_query.shape[2]
    width = heads * HD
    q0, k0, v0 = p_query[0], p_cache_k[0], p_cache_v[0]

    k2, v2 = across(k0, 2), across(v0, 2)
    k1, v1 = across(k0, 1), across(v0, 1)
    qs = [q0, along_y(q0, 1), along_y(q0, -1), along_y(q0, 2)]
    lim0 = visible_tokens(p_slot_req[0], p_slot_blk[0], p_offsets[0])
    table = jnp.pad(jnp.stack([p_slot_req[0], lim0]), ((0, 14), (0, HD - slots))).astype(BF)
    note = jnp.concatenate(
        [p_key[0].reshape(-1, HD), p_value[0].reshape(-1, HD), table], axis=0
    )
    notes = [note, across(note, 1), across(note, 2), across(note, 3)]
    handed = lax.ppermute(note, "sec", [(0, 1), (1, 0)])[: 2 * reqs * span_len]
    handed = handed.reshape(2, reqs, span_len, HD)
    spans = [n[: 2 * reqs * span_len].reshape(2, reqs, span_len, HD) for n in notes]
    reqs_of = [n[2 * reqs * span_len, :slots].astype(jnp.int32) for n in notes]
    lims_of = [n[2 * reqs * span_len + 1, :slots].astype(jnp.int32) for n in notes]

    half = out_weight.shape[1] // (2 * tp)
    block = lambda d: lax.dynamic_slice(
        out_weight, (0, (((column + d) % tp) * 2 + core) * half), (out_weight.shape[0], half)
    )
    mine = [along_x(block(1), 1), along_x(block(3), -1), along_x(block(2), 2)]
    theirs = [across(w, 1) for w in mine]

    dq = d_query[0].reshape(2, steps, heads, HD).transpose(0, 2, 1, 3).reshape(2, steps * heads, HD)
    dq = jnp.pad(dq, ((0, 0), (0, 32 - steps * heads), (0, 0)))
    dq_all = lax.all_to_all(jnp.broadcast_to(dq[None], (ctx,) + dq.shape), "ctx", 0, 0)
    dq_all = dq_all.reshape(ctx * 2, 32, HD)
    pad = ((0, 0), (0, 16 - steps), (0, 0))
    dec = decode(
        d_slot_req[0],
        visible_tokens(d_slot_req[0], d_slot_blk[0], d_lengths[0]),
        me.reshape(1),
        dq_all,
        d_cache_k[0],
        d_cache_v[0],
        handed[0],
        handed[1],
        jnp.pad(d_key[0], pad),
        jnp.pad(d_value[0], pad),
    )
    dec = lax.all_to_all(dec.reshape(ctx, 2, 32, 256), "ctx", 0, 0)

    sources = jnp.stack([me, me - 4 + ctx, me + 4, me + 8]) % ctx
    bases = jnp.concatenate([sources, me ^ jnp.arange(4, dtype=jnp.int32)]).astype(jnp.int32) * span_len
    near_tables = sorted_tables(jnp.concatenate(reqs_of[:2]), jnp.concatenate(lims_of[:2]))
    far_tables = sorted_tables(jnp.concatenate(reqs_of[2:]), jnp.concatenate(lims_of[2:]))
    num_a, num_b, queries, den = attn_near(
        *near_tables, bases, qs, (k0, k1, v0, v1), jnp.concatenate(spans, axis=2)
    )
    k2, v2, num_a, num_b, queries, den = lax.optimization_barrier((k2, v2, num_a, num_b, queries, den))
    k3, v3 = across(k2, 1), across(v2, 1)
    kv = (k2, k3, v2, v3)
    oa = attn_far(*far_tables, 0, queries, kv, num_a, den, span_len, width)
    sent_a = [oa[0], along_y(oa[1], -1), along_y(oa[2], 1), along_y(oa[3], 2)]
    ob = attn_far(*far_tables, reqs // 2, queries, kv, num_b, den, span_len, width)
    sent_b = [ob[0], along_y(ob[1], -1), along_y(ob[2], 1), along_y(ob[3], 2)]

    def gathered(x):
        return [x, along_x(x, 1), along_x(x, -1), along_x(x, 2)]

    xa = gathered(combine(sent_a, dec))
    xb = gathered(combine(sent_b))
    own = (column * 2 + core).reshape(1)
    other = (column * 2 + 1 - core).reshape(1)
    pa, decode_out = project(own, other, xa, out_weight, mine, theirs, 2 * steps)
    (pb,) = project(own, other, xb, out_weight, mine, theirs, 0)
    width = pa.shape[1]
    prefill_out = jnp.concatenate(
        [p.reshape(1, reqs // 2, span_len, width) for p in (pa, pb)], axis=1
    )
    return prefill_out, decode_out.reshape(1, 2, steps, width)


def solution(mesh):
    placed = (
        P("sec", None, "ctx", "tp"),
        P("sec", None, "ctx", "tp"),
        P("sec", None, "ctx", "tp"),
        P("sec", "ctx", None, "tp"),
        P("sec", "ctx", None, "tp"),
        P("sec", "ctx"),
        P("sec", "ctx"),
        P("sec", None),
        P("sec", "ctx", None, "tp"),
        P("sec", "ctx", None, "tp"),
        P("sec", "ctx", None, "tp"),
        P("sec", "ctx", None, "tp"),
        P("sec", "ctx", None, "tp"),
        P("sec", "ctx"),
        P("sec", "ctx"),
        P("sec", None),
        P("tp", None),
    )
    return jax.shard_map(
        on_device,
        mesh=mesh,
        in_specs=placed,
        out_specs=(P("sec", None, "ctx", "tp"), P("sec", "ctx", None, "tp")),
        check_vma=False,
    )
```

time: 220 us -> 211 us (0.959)
  the two profiles are of different devices: /device:TPU:1 before, /device:TPU:24 now
where the time goes in v2:
time: 211 us; the launch traced here: 207 us
  Pallas kernels  61.5 us (29%)
  waiting for transfers between devices  58 us (27%)
  starting transfers between devices  50.9 us (24%)
  local copies, waits for them, and re-layouts  29.3 us (14%)
  other arithmetic  6.39 us (3%)
    ppermute x9, waiting for transfers between devices, along_x(): return lax.ppermute(x, 'tp', [(i, (i + d) % tp) for i in range(tp)])  31.6 us
    ppermute x9, waiting for transfers between devices, along_y(): return lax.ppermute(x, 'ctx', [(i, (i + 4 * d) % ctx) for i in range(ctx)])  25.9 us
    unnamed x91, local copies, waits for them, and re-layouts  21.3 us
    pallas_call x2, Pallas kernels, attn_far(): pl.pallas_call(body, in_specs=[SM] * 3 + [HBM] * 6 + [VM], out_specs=[VM]...  20.4 us
    pallas_call x1, Pallas kernels, attn_near(): pl.pallas_call(body, in_specs=[SM] * 4 + [HBM] * 9, out_specs=[HBM, HBM,...  19.2 us
    ppermute x9, starting transfers between devices, along_x(): return lax.ppermute(x, 'tp', [(i, (i + d) % tp) for i in range(tp)])  14.5 us
    pallas_call x2, Pallas kernels, project(): pl.pallas_call(project_kernel, grid_spec=spec, out_shape=shapes, compiler...  14.1 us
    ppermute x9, starting transfers between devices, along_y(): return lax.ppermute(x, 'ctx', [(i, (i + 4 * d) % ctx) for i in range(ctx)])  11.4 us
  transfers between devices with their start and end apart: 33, of which 9 were waited for; matrix products, arithmetic and copies ran while one was open for 5% of the time, Pallas kernels for 26%

profile of v2, /device:TPU:24, one launch (start us, length us, event | category | flops | bytes accessed | tf_op | source)
XLA Modules:
  0.0 207.2 jit_solution(9155463264364391979)
XLA Ops:
  3.1 2.0 collective-permute-start.1
  6.7 6.1 %all-to-all-start = ((bf16[16,2,32,128]{3,2,1,0:T(8,128)(2,1)}), bf16[16,2,32,128]{3,2,1,0:T(8,128)(2,1)S(1)}, u32[]{:S(2)}, u32[]{:S(2)}) async-start(bf16[16,2,32,128]{3,2,1,0:T(8,128)(2,1)} %broadcast_in_dim.93), calls=%async_computation | async-start | bytes 524288 | tf_op jit(solution)/shard_map/all_to_all | solution.py:443
  13.3 1.5 pad_maximum_fusion.3
  14.9 2.9 %constant_dynamic-slice_fusion = (bf16[896,896]{1,0:T(8,128)(2,1)S(1)}, bf16[896,896]{1,0:T(8,128)(2,1)S(1)}, bf16[896,896]{1,0:T(8,128)(2,1)S(1)}) fusion(bf16[896,7168]{1,0:T(8,128)(2,1)} %w0.3, s32[]{:T(128)S(6)} %select_n.68, s32[]{:T(128)S(6)} %select_n.66, s32[]{:T(128)S(6)} %select_n.64), kind=kLoop, calls=%fused_computation.31 | loop fusion | bytes 9633804 | tf_op jit(solution)/shard_map/dynamic_slice | solution.py:435
  18.0 1.5 collective-permute-start.7
  19.7 3.3 %collective-permute-start.5 = (bf16[8,32,896]{2,1,0:T(8,128)(2,1)S(1)}, bf16[8,32,896]{2,1,0:T(8,128)(2,1)S(1)}, u32[]{:S(2)}, u32[]{:S(2)}) collective-permute-start(bf16[8,32,896]{2,1,0:T(8,128)(2,1)S(1)} %bitcast.74), channel_id=1, source_target_pairs={{0,16},{4,20},{8,24},{12,28},{16,32},{20,36},{24,40},{28,44},{32,4... | collective-permute-start | bytes 1376264 | tf_op jit(solution)/shard_map/ppermute | solution.py:404
  23.3 9.6 %collective-permute-done.7.refs_4_ = bf16[8,32,896]{2,1,0:T(8,128)(2,1)S(1)} collective-permute-done((bf16[8,32,896]{2,1,0:T(8,128)(2,1)S(1)}, bf16[8,32,896]{2,1,0:T(8,128)(2,1)S(1)}, u32[]{:S(2)}, u32[]{:S(2)}) %collective-permute-start.7) | collective-permute-done | bytes 458784 | tf_op jit(solution)/shard_map/ppermute | solution.py:404
  34.4 7.5 %collective-permute-done.6.refs_3_ = bf16[8,32,896]{2,1,0:T(8,128)(2,1)S(1)} collective-permute-done((bf16[8,32,896]{2,1,0:T(8,128)(2,1)S(1)}, bf16[8,32,896]{2,1,0:T(8,128)(2,1)S(1)}, u32[]{:S(2)}, u32[]{:S(2)}) %collective-permute-start.6) | collective-permute-done | bytes 458784 | tf_op jit(solution)/shard_map/ppermute | solution.py:404
  43.4 3.1 %collective-permute-start.21 = (bf16[896,896]{1,0:T(8,128)(2,1)S(1)}, bf16[896,896]{1,0:T(8,128)(2,1)S(1)}, u32[]{:S(2)}, u32[]{:S(2)}) collective-permute-start(bf16[896,896]{1,0:T(8,128)(2,1)S(1)} %get-tuple-element.50), channel_id=1, source_target_pairs={{0,2},{1,3},{2,0},{3,1},{4,6},{5,7},{6,4},{7,5},{8,10},{9,11},{10,... | collective-permute-start | bytes 4816904 | tf_op jit(solution)/shard_map/ppermute | solution.py:410
  49.7 19.2 %attn_near.1 = (f32[4,896,128]{2,1,0:T(8,128)}, f32[4,896,128]{2,1,0:T(8,128)}, bf16[8,896,128]{2,1,0:T(8,128)(2,1)}, f32[128,128]{1,0:T(8,128)S(1)}) custom-call(s32[48]{0:T(128)S(1)} %get-tuple-element.43.order, s32[48]{0:T(128)S(1)} %get-tuple-element.42.lim, s32[9]{0:T(128)S(1)} %convert_reduce_fusion.2.starts, s32[8]{0:T(128)S(1)} %add_multiply_fusion.refs_0_, ...), custom_call_target="tpu_custom_call" | custom-call | flops 2818572288 | bytes 12000000 | tf_op jit(solution)/shard_map/attn_near/pallas_call | solution.py:167
  71.3 5.1 %collective-permute-start.15 = (bf16[528,128]{1,0:T(8,128)(2,1)S(1)}, bf16[528,128]{1,0:T(8,128)(2,1)S(1)}, u32[]{:S(2)}, u32[]{:S(2)}) collective-permute-start(bf16[528,128]{1,0:T(8,128)(2,1)S(1)} %copy-done.38), channel_id=1, source_target_pairs={{0,64},{64,0},{1,65},{65,1},{2,66},{66,2},{3,67},{67,3},{4,68},{68... | collective-permute-start | bytes 405512 | tf_op jit(solution)/shard_map/ppermute | solution.py:428
  76.4 6.6 %collective-permute-done.21.a3 = bf16[896,896]{1,0:T(8,128)(2,1)S(1)} collective-permute-done((bf16[896,896]{1,0:T(8,128)(2,1)S(1)}, bf16[896,896]{1,0:T(8,128)(2,1)S(1)}, u32[]{:S(2)}, u32[]{:S(2)}) %collective-permute-start.21) | collective-permute-done | bytes 1605664 | tf_op jit(solution)/shard_map/ppermute | solution.py:410
  83.1 2.4 %copy-done = bf16[8,896,128]{2,1,0:T(8,128)(2,1)S(1)} copy-done((bf16[8,896,128]{2,1,0:T(8,128)(2,1)S(1)}, bf16[8,896,128]{2,1,0:T(8,128)(2,1)}, u32[]{:S(2)}) %copy-start) | copy-done | bytes 1835032
  85.5 11.3 %attn_far.2 = (bf16[144,896]{1,0:T(8,128)(2,1)S(1)}, bf16[144,896]{1,0:T(8,128)(2,1)S(1)}, bf16[144,896]{1,0:T(8,128)(2,1)}, bf16[144,896]{1,0:T(8,128)(2,1)}) custom-call(s32[48]{0:T(128)S(1)} %get-tuple-element.45.order, s32[48]{0:T(128)S(1)} %get-tuple-element.44.lim, s32[9]{0:T(128)S(1)} %convert_reduce_fusion.3.starts, ...), custom_call_target="tpu_custom_call" | custom-call | flops 1409286144 | bytes 12000000 | tf_op jit(solution)/shard_map/attn_far/pallas_call | solution.py:200
  97.6 1.6 collective-permute-start.12
  99.1 17.3 %collective-permute-done.20.a2 = bf16[896,896]{1,0:T(8,128)(2,1)} collective-permute-done((bf16[896,896]{1,0:T(8,128)(2,1)S(1)}, bf16[896,896]{1,0:T(8,128)(2,1)}, u32[]{:S(2)}, u32[]{:S(2)}) %collective-permute-start.20) | collective-permute-done | bytes 1605664 | tf_op jit(solution)/shard_map/ppermute | solution.py:410
  117.3 1.7 collective-permute-start.14
  125.3 5.8 %decode_terms.1 = bf16[32,32,256]{2,1,0:T(8,128)(2,1)S(1)} custom-call(s32[24]{0:T(128)S(1)} %bitcast.65, s32[24]{0:T(128)S(1)} %fusion.7.lim, s32[1]{0:T(128)} %bitcast.17.ctx, bf16[32,32,128]{2,1,0:T(8,128)(2,1)S(1)} %bitcast.58, bf16[24,128,128]{2,1,0:T(8,128)(2,1)S(1)} %bitcast.59, bf16[24,128,128]{2,1,0:T(8,128)(2,1)S(1)} %bitcast.60, ...), custom_call_target="tpu_custom_call" | custom-call | flops 100000000 | bytes 3000000 | tf_op jit(solution)/shard_map/decode_terms/pallas_call | solution.py:264
  131.9 7.0 %all-to-all-start.1 = ((bf16[16,2,32,256]{3,2,1,0:T(8,128)(2,1)}), bf16[16,2,32,256]{3,2,1,0:T(8,128)(2,1)}, u32[]{:S(2)}, u32[]{:S(2)}) async-start(bf16[16,2,32,256]{3,2,1,0:T(8,128)(2,1)} %bitcast.56), calls=%async_computation.1 | async-start | bytes 1048576 | tf_op jit(solution)/shard_map/all_to_all | solution.py:458
  143.5 9.0 %attn_far.3 = (bf16[144,896]{1,0:T(8,128)(2,1)S(1)}, bf16[144,896]{1,0:T(8,128)(2,1)}, bf16[144,896]{1,0:T(8,128)(2,1)}, bf16[144,896]{1,0:T(8,128)(2,1)S(1)}) custom-call(s32[48]{0:T(128)S(1)} %get-tuple-element.45.order, s32[48]{0:T(128)S(1)} %get-tuple-element.44.lim, s32[9]{0:T(128)S(1)} %convert_reduce_fusion.3.starts, ...), custom_call_target="tpu_custom_call" | custom-call | flops 1409286144 | bytes 12000000 | tf_op jit(solution)/shard_map/attn_far/pallas_call | solution.py:200
  154.0 3.2 %collective-permute-start.26 = (bf16[144,896]{1,0:T(8,128)(2,1)}, bf16[144,896]{1,0:T(8,128)(2,1)S(1)}, u32[]{:S(2)}, u32[]{:S(2)}) collective-permute-start(bf16[144,896]{1,0:T(8,128)(2,1)} %get-tuple-element.39), channel_id=1, source_target_pairs={{0,16},{4,20},{8,24},{12,28},{16,32},{20,36},{24,40},{28,44},{32,4... | collective-permute-start | bytes 774152 | tf_op jit(solution)/shard_map/ppermute | solution.py:404
  159.1 1.7 combine.2.x0
  160.8 2.8 %collective-permute-done.25.refs_1_ = bf16[144,896]{1,0:T(8,128)(2,1)S(1)} collective-permute-done((bf16[144,896]{1,0:T(8,128)(2,1)}, bf16[144,896]{1,0:T(8,128)(2,1)S(1)}, u32[]{:S(2)}, u32[]{:S(2)}) %collective-permute-start.25) | collective-permute-done | bytes 258080 | tf_op jit(solution)/shard_map/ppermute | solution.py:404
  165.0 2.4 %collective-permute-start.18 = (bf16[144,896]{1,0:T(8,128)(2,1)S(1)}, bf16[144,896]{1,0:T(8,128)(2,1)S(1)}, u32[]{:S(2)}, u32[]{:S(2)}) collective-permute-start(bf16[144,896]{1,0:T(8,128)(2,1)S(1)} %combine.2.x0), channel_id=1, source_target_pairs={{0,2},{1,3},{2,0},{3,1},{4,6},{5,7},{6,4},{7,5},{8,10},{9,11},{10,... | collective-permute-start | bytes 774152 | tf_op jit(solution)/shard_map/ppermute | solution.py:410
  167.4 5.8 %collective-permute-done.27.refs_3_ = bf16[144,896]{1,0:T(8,128)(2,1)S(1)} collective-permute-done((bf16[144,896]{1,0:T(8,128)(2,1)S(1)}, bf16[144,896]{1,0:T(8,128)(2,1)S(1)}, u32[]{:S(2)}, u32[]{:S(2)}) %collective-permute-start.27) | collective-permute-done | bytes 258080 | tf_op jit(solution)/shard_map/ppermute | solution.py:404
  173.3 2.6 %collective-permute-start.17 = (bf16[144,896]{1,0:T(8,128)(2,1)S(1)}, bf16[144,896]{1,0:T(8,128)(2,1)S(1)}, u32[]{:S(2)}, u32[]{:S(2)}) collective-permute-start(bf16[144,896]{1,0:T(8,128)(2,1)S(1)} %combine.2.x0), channel_id=1, source_target_pairs={{0,3},{1,0},{2,1},{3,2},{4,7},{5,4},{6,5},{7,6},{8,11},{9,8},{10,9... | collective-permute-start | bytes 774152 | tf_op jit(solution)/shard_map/ppermute | solution.py:410
  178.1 1.8 collective-permute-done.17.x2
  179.9 2.3 %collective-permute-start.30 = (bf16[128,896]{1,0:T(8,128)(2,1)S(1)}, bf16[128,896]{1,0:T(8,128)(2,1)S(1)}, u32[]{:S(2)}, u32[]{:S(2)}) collective-permute-start(bf16[128,896]{1,0:T(8,128)(2,1)S(1)} %combine.3.x0), channel_id=1, source_target_pairs={{0,2},{1,3},{2,0},{3,1},{4,6},{5,7},{6,4},{7,5},{8,10},{9,11},{10,... | collective-permute-start | bytes 688136 | tf_op jit(solution)/shard_map/ppermute | solution.py:410
  182.2 5.9 %collective-permute-done.16.x1 = bf16[144,896]{1,0:T(8,128)(2,1)S(1)} collective-permute-done((bf16[144,896]{1,0:T(8,128)(2,1)S(1)}, bf16[144,896]{1,0:T(8,128)(2,1)S(1)}, u32[]{:S(2)}, u32[]{:S(2)}) %collective-permute-start.16) | collective-permute-done | bytes 258080 | tf_op jit(solution)/shard_map/ppermute | solution.py:410
  188.1 2.0 collective-permute-start.28
  190.2 7.4 %project.2 = (bf16[128,1792]{1,0:T(8,128)(2,1)S(1)}, bf16[8,1792]{1,0:T(8,128)(2,1)S(1)}) custom-call(s32[1]{0:T(128)} %bitcast.own, s32[1]{0:T(128)} %bitcast.1.other, bf16[144,896]{1,0:T(8,128)(2,1)S(1)} %combine.2.x0, bf16[144,896]{1,0:T(8,128)(2,1)S(1)} %collective-permute-done.16.x1, bf16[144,896]{1,0:T(8,128)(2,1)S(1)} %collective-permute-done.17.x2, ...), custom_call_target="tpu_custom_call" | custom-call | flops 1849688064 | bytes 14000000 | tf_op jit(solution)/shard_map/project/pallas_call | solution.py:365
  199.5 6.7 %project.3 = bf16[128,1792]{1,0:T(8,128)(2,1)S(1)} custom-call(s32[1]{0:T(128)} %bitcast.own, s32[1]{0:T(128)} %bitcast.1.other, bf16[128,896]{1,0:T(8,128)(2,1)S(1)} %combine.3.x0, bf16[128,896]{1,0:T(8,128)(2,1)} %collective-permute-done.28.x1, bf16[128,896]{1,0:T(8,128)(2,1)} %collective-permute-done.29.x2, ...), custom_call_target="tpu_custom_call" | custom-call | flops 1644167168 | bytes 14000000 | tf_op jit(solution)/shard_map/project/pallas_call | solution.py:365
  (170 shorter events, 36.7 us)
Async XLA Ops:
  3.0 15.0 %collective-permute-start.4 = (bf16[528,128]{1,0:T(8,128)(2,1)S(1)}, bf16[528,128]{1,0:T(8,128)(2,1)S(1)}, u32[]{:S(2)}, u32[]{:S(2)}) collective-permute-start(bf16[528,128]{1,0:T(8,128)(2,1)S(1)} %pad_maximum_fusion.2), channel_id=1, source_target_pairs={{0,4},{4,0},{8,12},{12,8},{16,20},{20,16},{24,28},{28,24},{32,36},... | collective-permute-start | bytes 405512 | tf_op jit(solution)/shard_map/ppermute | solution.py:407
  3.1 16.4 %collective-permute-start.1 = (bf16[528,128]{1,0:T(8,128)(2,1)S(1)}, bf16[528,128]{1,0:T(8,128)(2,1)S(1)}, u32[]{:S(2)}, u32[]{:S(2)}) collective-permute-start(bf16[528,128]{1,0:T(8,128)(2,1)S(1)} %pad_maximum_fusion.2), channel_id=1, source_target_pairs={{0,12},{4,8},{8,4},{12,0},{16,28},{20,24},{24,20},{28,16},{32,44},... | collective-permute-start | bytes 405512 | tf_op jit(solution)/shard_map/ppermute | solution.py:407
  5.1 14.5 %collective-permute-start = (bf16[528,128]{1,0:T(8,128)(2,1)S(1)}, bf16[528,128]{1,0:T(8,128)(2,1)S(1)}, u32[]{:S(2)}, u32[]{:S(2)}) collective-permute-start(bf16[528,128]{1,0:T(8,128)(2,1)S(1)} %pad_maximum_fusion.2), channel_id=1, source_target_pairs={{0,8},{4,12},{8,0},{12,4},{16,24},{20,28},{24,16},{28,20},{32,40},... | collective-permute-start | bytes 405512 | tf_op jit(solution)/shard_map/ppermute | solution.py:407
  6.7 112.9 %all-to-all-start = ((bf16[16,2,32,128]{3,2,1,0:T(8,128)(2,1)}), bf16[16,2,32,128]{3,2,1,0:T(8,128)(2,1)S(1)}, u32[]{:S(2)}, u32[]{:S(2)}) async-start(bf16[16,2,32,128]{3,2,1,0:T(8,128)(2,1)} %broadcast_in_dim.93), calls=%async_computation | async-start | bytes 524288 | tf_op jit(solution)/shard_map/all_to_all | solution.py:443
  12.8 33.8 %collective-permute-start.8 = (bf16[24,128,128]{2,1,0:T(8,128)(2,1)}, bf16[24,128,128]{2,1,0:T(8,128)(2,1)S(1)}, u32[]{:S(2)}, u32[]{:S(2)}) collective-permute-start(bf16[24,128,128]{2,1,0:T(8,128)(2,1)} %bitcast.66), channel_id=1, source_target_pairs={{0,4},{4,0},{8,12},{12,8},{16,20},{20,16},{24,28},{28,24},{32,36},... | collective-permute-start | bytes 2359304 | tf_op jit(solution)/shard_map/ppermute | solution.py:407
  13.0 34.9 %collective-permute-start.9 = (bf16[24,128,128]{2,1,0:T(8,128)(2,1)}, bf16[24,128,128]{2,1,0:T(8,128)(2,1)}, u32[]{:S(2)}, u32[]{:S(2)}) collective-permute-start(bf16[24,128,128]{2,1,0:T(8,128)(2,1)} %bitcast.69), channel_id=1, source_target_pairs={{0,4},{4,0},{8,12},{12,8},{16,20},{20,16},{24,28},{28,24},{32,36},... | collective-permute-start | bytes 2359304 | tf_op jit(solution)/shard_map/ppermute | solution.py:407
  18.0 15.0 %collective-permute-start.7 = (bf16[8,32,896]{2,1,0:T(8,128)(2,1)S(1)}, bf16[8,32,896]{2,1,0:T(8,128)(2,1)S(1)}, u32[]{:S(2)}, u32[]{:S(2)}) collective-permute-start(bf16[8,32,896]{2,1,0:T(8,128)(2,1)S(1)} %bitcast.72), channel_id=1, source_target_pairs={{0,32},{4,36},{8,40},{12,44},{16,48},{20,52},{24,56},{28,60},{32,0... | collective-permute-start | bytes 1376264 | tf_op jit(solution)/shard_map/ppermute | solution.py:404
  19.5 22.4 %collective-permute-start.6 = (bf16[8,32,896]{2,1,0:T(8,128)(2,1)S(1)}, bf16[8,32,896]{2,1,0:T(8,128)(2,1)S(1)}, u32[]{:S(2)}, u32[]{:S(2)}) collective-permute-start(bf16[8,32,896]{2,1,0:T(8,128)(2,1)S(1)} %bitcast.73), channel_id=1, source_target_pairs={{0,48},{4,52},{8,56},{12,60},{16,0},{20,4},{24,8},{28,12},{32,16},... | collective-permute-start | bytes 1376264 | tf_op jit(solution)/shard_map/ppermute | solution.py:404
  19.7 23.8 %collective-permute-start.5 = (bf16[8,32,896]{2,1,0:T(8,128)(2,1)S(1)}, bf16[8,32,896]{2,1,0:T(8,128)(2,1)S(1)}, u32[]{:S(2)}, u32[]{:S(2)}) collective-permute-start(bf16[8,32,896]{2,1,0:T(8,128)(2,1)S(1)} %bitcast.74), channel_id=1, source_target_pairs={{0,16},{4,20},{8,24},{12,28},{16,32},{20,36},{24,40},{28,44},{32,4... | collective-permute-start | bytes 1376264 | tf_op jit(solution)/shard_map/ppermute | solution.py:404
  33.0 36.0 %collective-permute-start.2 = (bf16[24,128,128]{2,1,0:T(8,128)(2,1)S(1)}, bf16[24,128,128]{2,1,0:T(8,128)(2,1)S(1)}, u32[]{:S(2)}, u32[]{:S(2)}) collective-permute-start(bf16[24,128,128]{2,1,0:T(8,128)(2,1)S(1)} %bitcast.67), channel_id=1, source_target_pairs={{0,8},{4,12},{8,0},{12,4},{16,24},{20,28},{24,16},{28,20},{32,40},... | collective-permute-start | bytes 2359304 | tf_op jit(solution)/shard_map/ppermute | solution.py:407
  41.9 27.0 %collective-permute-start.3 = (bf16[24,128,128]{2,1,0:T(8,128)(2,1)S(1)}, bf16[24,128,128]{2,1,0:T(8,128)(2,1)S(1)}, u32[]{:S(2)}, u32[]{:S(2)}) collective-permute-start(bf16[24,128,128]{2,1,0:T(8,128)(2,1)S(1)} %bitcast.70), channel_id=1, source_target_pairs={{0,8},{4,12},{8,0},{12,4},{16,24},{20,28},{24,16},{28,20},{32,40},... | collective-permute-start | bytes 2359304 | tf_op jit(solution)/shard_map/ppermute | solution.py:407
  43.4 39.6 %collective-permute-start.21 = (bf16[896,896]{1,0:T(8,128)(2,1)S(1)}, bf16[896,896]{1,0:T(8,128)(2,1)S(1)}, u32[]{:S(2)}, u32[]{:S(2)}) collective-permute-start(bf16[896,896]{1,0:T(8,128)(2,1)S(1)} %get-tuple-element.50), channel_id=1, source_target_pairs={{0,2},{1,3},{2,0},{3,1},{4,6},{5,7},{6,4},{7,5},{8,10},{9,11},{10,... | collective-permute-start | bytes 4816904 | tf_op jit(solution)/shard_map/ppermute | solution.py:410
  46.6 69.7 %collective-permute-start.20 = (bf16[896,896]{1,0:T(8,128)(2,1)S(1)}, bf16[896,896]{1,0:T(8,128)(2,1)}, u32[]{:S(2)}, u32[]{:S(2)}) collective-permute-start(bf16[896,896]{1,0:T(8,128)(2,1)S(1)} %get-tuple-element.51), channel_id=1, source_target_pairs={{0,3},{1,0},{2,1},{3,2},{4,7},{5,4},{6,5},{7,6},{8,11},{9,8},{10,9... | collective-permute-start | bytes 4816904 | tf_op jit(solution)/shard_map/ppermute | solution.py:410
  47.9 68.5 %collective-permute-start.19 = (bf16[896,896]{1,0:T(8,128)(2,1)S(1)}, bf16[896,896]{1,0:T(8,128)(2,1)}, u32[]{:S(2)}, u32[]{:S(2)}) collective-permute-start(bf16[896,896]{1,0:T(8,128)(2,1)S(1)} %get-tuple-element.52), channel_id=1, source_target_pairs={{0,1},{1,2},{2,3},{3,0},{4,5},{5,6},{6,7},{7,4},{8,9},{9,10},{10,1... | collective-permute-start | bytes 4816904 | tf_op jit(solution)/shard_map/ppermute | solution.py:410
  69.1 14.0 %collective-permute-start.11 = (bf16[24,128,128]{2,1,0:T(8,128)(2,1)S(1)}, bf16[24,128,128]{2,1,0:T(8,128)(2,1)S(1)}, u32[]{:S(2)}, u32[]{:S(2)}) collective-permute-start(bf16[24,128,128]{2,1,0:T(8,128)(2,1)S(1)} %collective-permute-done.3.refs_3_), channel_id=1, source_target_pairs={{0,4},{4,0},{8,12},{12,8},{16,20},{20,16},{24,28},{28,24},{32,36},... | collective-permute-start | bytes 2359304 | tf_op jit(solution)/shard_map/ppermute | solution.py:407
  71.3 45.8 %collective-permute-start.15 = (bf16[528,128]{1,0:T(8,128)(2,1)S(1)}, bf16[528,128]{1,0:T(8,128)(2,1)S(1)}, u32[]{:S(2)}, u32[]{:S(2)}) collective-permute-start(bf16[528,128]{1,0:T(8,128)(2,1)S(1)} %copy-done.38), channel_id=1, source_target_pairs={{0,64},{64,0},{1,65},{65,1},{2,66},{66,2},{3,67},{67,3},{4,68},{68... | collective-permute-start | bytes 405512 | tf_op jit(solution)/shard_map/ppermute | solution.py:428
  83.1 105.1 %collective-permute-start.24 = (bf16[896,896]{1,0:T(8,128)(2,1)S(1)}, bf16[896,896]{1,0:T(8,128)(2,1)}, u32[]{:S(2)}, u32[]{:S(2)}) collective-permute-start(bf16[896,896]{1,0:T(8,128)(2,1)S(1)} %collective-permute-done.21.a3), channel_id=1, source_target_pairs={{0,4},{4,0},{8,12},{12,8},{16,20},{20,16},{24,28},{28,24},{32,36},... | collective-permute-start | bytes 4816904 | tf_op jit(solution)/shard_map/ppermute | solution.py:407
  97.6 19.7 %collective-permute-start.12 = (bf16[144,896]{1,0:T(8,128)(2,1)S(1)}, bf16[144,896]{1,0:T(8,128)(2,1)S(1)}, u32[]{:S(2)}, u32[]{:S(2)}) collective-permute-start(bf16[144,896]{1,0:T(8,128)(2,1)S(1)} %get-tuple-element.32), channel_id=1, source_target_pairs={{0,48},{4,52},{8,56},{12,60},{16,0},{20,4},{24,8},{28,12},{32,16},... | collective-permute-start | bytes 774152 | tf_op jit(solution)/shard_map/ppermute | solution.py:404
  116.4 73.8 %collective-permute-start.23 = (bf16[896,896]{1,0:T(8,128)(2,1)}, bf16[896,896]{1,0:T(8,128)(2,1)}, u32[]{:S(2)}, u32[]{:S(2)}) collective-permute-start(bf16[896,896]{1,0:T(8,128)(2,1)} %collective-permute-done.20.a2), channel_id=1, source_target_pairs={{0,4},{4,0},{8,12},{12,8},{16,20},{20,16},{24,28},{28,24},{32,36},... | collective-permute-start | bytes 4816904 | tf_op jit(solution)/shard_map/ppermute | solution.py:407
  116.4 73.8 %collective-permute-start.22 = (bf16[896,896]{1,0:T(8,128)(2,1)}, bf16[896,896]{1,0:T(8,128)(2,1)}, u32[]{:S(2)}, u32[]{:S(2)}) collective-permute-start(bf16[896,896]{1,0:T(8,128)(2,1)} %collective-permute-done.19.a1), channel_id=1, source_target_pairs={{0,4},{4,0},{8,12},{12,8},{16,20},{20,16},{24,28},{28,24},{32,36},... | collective-permute-start | bytes 4816904 | tf_op jit(solution)/shard_map/ppermute | solution.py:407
  117.2 36.7 %collective-permute-start.13 = (bf16[144,896]{1,0:T(8,128)(2,1)}, bf16[144,896]{1,0:T(8,128)(2,1)}, u32[]{:S(2)}, u32[]{:S(2)}) collective-permute-start(bf16[144,896]{1,0:T(8,128)(2,1)} %get-tuple-element.33), channel_id=1, source_target_pairs={{0,16},{4,20},{8,24},{12,28},{16,32},{20,36},{24,40},{28,44},{32,4... | collective-permute-start | bytes 774152 | tf_op jit(solution)/shard_map/ppermute | solution.py:404
  117.3 36.7 %collective-permute-start.14 = (bf16[144,896]{1,0:T(8,128)(2,1)}, bf16[144,896]{1,0:T(8,128)(2,1)}, u32[]{:S(2)}, u32[]{:S(2)}) collective-permute-start(bf16[144,896]{1,0:T(8,128)(2,1)} %get-tuple-element.34), channel_id=1, source_target_pairs={{0,32},{4,36},{8,40},{12,44},{16,48},{20,52},{24,56},{28,60},{32,0... | collective-permute-start | bytes 774152 | tf_op jit(solution)/shard_map/ppermute | solution.py:404
  131.9 25.3 %all-to-all-start.1 = ((bf16[16,2,32,256]{3,2,1,0:T(8,128)(2,1)}), bf16[16,2,32,256]{3,2,1,0:T(8,128)(2,1)}, u32[]{:S(2)}, u32[]{:S(2)}) async-start(bf16[16,2,32,256]{3,2,1,0:T(8,128)(2,1)} %bitcast.56), calls=%async_computation.1 | async-start | bytes 1048576 | tf_op jit(solution)/shard_map/all_to_all | solution.py:458
  153.9 9.7 %collective-permute-start.25 = (bf16[144,896]{1,0:T(8,128)(2,1)}, bf16[144,896]{1,0:T(8,128)(2,1)S(1)}, u32[]{:S(2)}, u32[]{:S(2)}) collective-permute-start(bf16[144,896]{1,0:T(8,128)(2,1)} %get-tuple-element.38), channel_id=1, source_target_pairs={{0,48},{4,52},{8,56},{12,60},{16,0},{20,4},{24,8},{28,12},{32,16},... | collective-permute-start | bytes 774152 | tf_op jit(solution)/shard_map/ppermute | solution.py:404
  154.0 10.3 %collective-permute-start.26 = (bf16[144,896]{1,0:T(8,128)(2,1)}, bf16[144,896]{1,0:T(8,128)(2,1)S(1)}, u32[]{:S(2)}, u32[]{:S(2)}) collective-permute-start(bf16[144,896]{1,0:T(8,128)(2,1)} %get-tuple-element.39), channel_id=1, source_target_pairs={{0,16},{4,20},{8,24},{12,28},{16,32},{20,36},{24,40},{28,44},{32,4... | collective-permute-start | bytes 774152 | tf_op jit(solution)/shard_map/ppermute | solution.py:404
  164.3 9.0 %collective-permute-start.27 = (bf16[144,896]{1,0:T(8,128)(2,1)S(1)}, bf16[144,896]{1,0:T(8,128)(2,1)S(1)}, u32[]{:S(2)}, u32[]{:S(2)}) collective-permute-start(bf16[144,896]{1,0:T(8,128)(2,1)S(1)} %copy-done.35), channel_id=1, source_target_pairs={{0,32},{4,36},{8,40},{12,44},{16,48},{20,52},{24,56},{28,60},{32,0... | collective-permute-start | bytes 774152 | tf_op jit(solution)/shard_map/ppermute | solution.py:404
  165.0 10.9 %collective-permute-start.18 = (bf16[144,896]{1,0:T(8,128)(2,1)S(1)}, bf16[144,896]{1,0:T(8,128)(2,1)S(1)}, u32[]{:S(2)}, u32[]{:S(2)}) collective-permute-start(bf16[144,896]{1,0:T(8,128)(2,1)S(1)} %combine.2.x0), channel_id=1, source_target_pairs={{0,2},{1,3},{2,0},{3,1},{4,6},{5,7},{6,4},{7,5},{8,10},{9,11},{10,... | collective-permute-start | bytes 774152 | tf_op jit(solution)/shard_map/ppermute | solution.py:410
  173.3 6.7 %collective-permute-start.17 = (bf16[144,896]{1,0:T(8,128)(2,1)S(1)}, bf16[144,896]{1,0:T(8,128)(2,1)S(1)}, u32[]{:S(2)}, u32[]{:S(2)}) collective-permute-start(bf16[144,896]{1,0:T(8,128)(2,1)S(1)} %combine.2.x0), channel_id=1, source_target_pairs={{0,3},{1,0},{2,1},{3,2},{4,7},{5,4},{6,5},{7,6},{8,11},{9,8},{10,9... | collective-permute-start | bytes 774152 | tf_op jit(solution)/shard_map/ppermute | solution.py:410
  175.9 12.2 %collective-permute-start.16 = (bf16[144,896]{1,0:T(8,128)(2,1)S(1)}, bf16[144,896]{1,0:T(8,128)(2,1)S(1)}, u32[]{:S(2)}, u32[]{:S(2)}) collective-permute-start(bf16[144,896]{1,0:T(8,128)(2,1)S(1)} %combine.2.x0), channel_id=1, source_target_pairs={{0,1},{1,2},{2,3},{3,0},{4,5},{5,6},{6,7},{7,4},{8,9},{9,10},{10,1... | collective-permute-start | bytes 774152 | tf_op jit(solution)/shard_map/ppermute | solution.py:410
  179.9 19.6 %collective-permute-start.30 = (bf16[128,896]{1,0:T(8,128)(2,1)S(1)}, bf16[128,896]{1,0:T(8,128)(2,1)S(1)}, u32[]{:S(2)}, u32[]{:S(2)}) collective-permute-start(bf16[128,896]{1,0:T(8,128)(2,1)S(1)} %combine.3.x0), channel_id=1, source_target_pairs={{0,2},{1,3},{2,0},{3,1},{4,6},{5,7},{6,4},{7,5},{8,10},{9,11},{10,... | collective-permute-start | bytes 688136 | tf_op jit(solution)/shard_map/ppermute | solution.py:410
  188.1 11.4 %collective-permute-start.29 = (bf16[128,896]{1,0:T(8,128)(2,1)S(1)}, bf16[128,896]{1,0:T(8,128)(2,1)}, u32[]{:S(2)}, u32[]{:S(2)}) collective-permute-start(bf16[128,896]{1,0:T(8,128)(2,1)S(1)} %combine.3.x0), channel_id=1, source_target_pairs={{0,3},{1,0},{2,1},{3,2},{4,7},{5,4},{6,5},{7,6},{8,11},{9,8},{10,9... | collective-permute-start | bytes 688136 | tf_op jit(solution)/shard_map/ppermute | solution.py:410
  188.1 11.4 %collective-permute-start.28 = (bf16[128,896]{1,0:T(8,128)(2,1)S(1)}, bf16[128,896]{1,0:T(8,128)(2,1)}, u32[]{:S(2)}, u32[]{:S(2)}) collective-permute-start(bf16[128,896]{1,0:T(8,128)(2,1)S(1)} %combine.3.x0), channel_id=1, source_target_pairs={{0,1},{1,2},{2,3},{3,0},{4,5},{5,6},{6,7},{7,4},{8,9},{9,10},{10,1... | collective-permute-start | bytes 688136 | tf_op jit(solution)/shard_map/ppermute | solution.py:410
  (46 other events, 505.1 us)

commit v3 on v2

v3 whole, which is shorter than its diff:
```python
import functools

import jax
import jax.numpy as jnp
from jax import lax
from jax.experimental import pallas as pl
from jax.experimental.pallas import tpu as pltpu
from jax.sharding import PartitionSpec as P

HD = 128
PAGE = 128
BF = jnp.bfloat16
F32 = jnp.float32
NT = (((1,), (1,)), ((), ()))
VM = pl.BlockSpec(memory_space=pltpu.VMEM)
SM = pl.BlockSpec(memory_space=pltpu.SMEM)
HBM = pl.BlockSpec(memory_space=pl.ANY)


def attn_kernel(table, *refs, first, r0, R, heads, nb):
    rows = heads * 128
    half = nb // 2
    if first:
        rel, q_all, ma, mb, num_out, qs_out, den, qv, qs, ks, vs, acc, dacc, p0, p1, sem = refs
    else:
        (bases, qs_in, ma, mb, mc, md, num_in, den_in, o0, o1, o2, o3,
         qs, ks, vs, acc, dacc, p0, p1, tile, sem) = refs
    cs = []

    def copy(src, dst, i):
        c = pltpu.make_async_copy(src, dst, sem.at[i])
        c.start()
        return c

    if first:
        qc = [copy(q_all.at[rel[d]], qv.at[d], 4 + d) for d in range(4)]
        sets = (ma, mb)
    else:
        cs = [copy(qs_in.at[pl.ds(r0, R)], qs, 4), copy(num_in.at[pl.ds(r0, R)], acc, 5)]
        sets = (mc, md)
    for i, m in enumerate(sets):
        cs.append(copy(m.at[pl.ds(0, half)], ks.at[pl.ds(i * half, half)], 2 * i))
        cs.append(copy(m.at[pl.ds(half, half)], vs.at[pl.ds(i * half, half)], 2 * i + 1))
    if not first:
        for i, m in enumerate((ma, mb, mc, md)):
            for j, dst in enumerate((ks, vs)):
                for r in range(R):
                    at = nb + j * 2 + (r0 + r) // 4
                    c = pltpu.make_async_copy(
                        m.at[at, pl.ds((r0 + r) % 4 * 32, 32)],
                        dst.at[nb + r, pl.ds(i * 32, 32)],
                        sem.at[6 + (i * 2 + j) * R + r],
                    )
                    c.start()
                    cs.append(c)
    dacc[...] = jnp.zeros_like(dacc)
    p1[...] = jnp.zeros_like(p1)
    if first:
        acc[...] = jnp.zeros_like(acc)
        for d in range(4):
            qc[d].wait()
            for r in range(R):
                for h in range(heads):
                    qs[r, pl.ds(h * 128 + d * 32, 32), :] = qv[d, r, :, pl.ds(h * 128, 128)]
        qs_copy = copy(qs, qs_out, 4)
    else:
        rowi = lax.broadcasted_iota(jnp.int32, (128, 128), 0)
        coli = lax.broadcasted_iota(jnp.int32, (128, 128), 1)

        def pick(i, b):
            g = i // 32
            base = jnp.where(
                g == 0, bases[b], jnp.where(g == 1, bases[b + 1], jnp.where(g == 2, bases[b + 2], bases[b + 3]))
            )
            return base + lax.rem(i, 32)

        tile[...] = jnp.where(pick(rowi, 0) >= pick(coli, 4), coli + 1, 0)
    for c in cs:
        c.wait()
    lane = lax.broadcasted_iota(jnp.int32, (1, 128), 1)
    begin, end = table[3, r0], table[3, r0 + R]

    def pair(p):
        ok = jnp.logical_and(p >= begin, p < end)
        i = jnp.where(ok, 2 * p, 0)
        r = jnp.where(ok, table[2, jnp.where(ok, p, 0)] - r0, 0)
        slots = table[0, i], table[0, i + 1]
        lims = jnp.where(ok, table[1, i], 0), jnp.where(ok, table[1, i + 1], 0)
        return r, slots, lims

    def scores(p, dst):
        r, slots, lims = pair(p)
        if not first:
            slots = [jnp.where(l == 200, nb + r, s) for s, l in zip(slots, lims)]
        K = jnp.concatenate([ks[slots[0]], ks[slots[1]]], axis=0)
        s = lax.dot_general(qs[r], K, NT, preferred_element_type=F32)
        w = jnp.exp(s * HD ** -0.5)
        t = None
        for j in range(2):
            limit = lims[j]
            if first or j:
                keep = (lane < limit)[None]
            else:
                keep = (lane < jnp.where(limit == 200, tile[...], limit))[None]
            one = w[:, j * 128 : (j + 1) * 128].reshape(heads, 128, 128)
            one = jnp.where(keep, one, 0.0).reshape(rows, 128)
            dst[:, j * 128 : (j + 1) * 128] = one.astype(BF)
            t = one if t is None else t + one
        dacc[r] += t

    def products(p, src):
        r, slots, lims = pair(p)
        if not first:
            slots = [jnp.where(l == 200, nb + r, s) for s, l in zip(slots, lims)]
        V = jnp.concatenate([vs[slots[0]], vs[slots[1]]], axis=0)
        acc[r] += jnp.dot(src[...], V, preferred_element_type=F32)

    def step(i, unused):
        p = begin + 2 * i
        products(p - 1, p1)
        scores(p, p0)
        products(p, p0)
        scores(p + 1, p1)
        return 0

    steps = (end - begin + 1) // 2
    lax.fori_loop(0, steps, step, 0)
    products(begin + 2 * steps - 1, p1)

    lane1 = lax.broadcasted_iota(jnp.int32, (128, 128), 1)
    dl = jnp.zeros((128, 128), F32) if first else den_in[...]
    if first:
        num_copy = copy(acc, num_out, 0)
    for r in range(R):
        for h in range(heads):
            col = jnp.sum(dacc[r, pl.ds(h * 128, 128), :], axis=1, keepdims=True)
            dl = dl + jnp.where(lane1 == (r0 + r) * 16 + h, col, 0.0)
    if first:
        den[...] = dl
        num_copy.wait()
        qs_copy.wait()
        return
    outs = (o0, o1, o2, o3)
    for r in range(R):
        for h in range(heads):
            for d in range(4):
                outs[d][r * 32 : r * 32 + 32, h * 128 : h * 128 + 128] = acc[
                    r, h * 128 + d * 32 : h * 128 + d * 32 + 32, :
                ].astype(BF)
    dl = dl[:, r0 * 16 : r0 * 16 + 64]
    hi = dl.astype(BF).astype(F32)
    both = jnp.concatenate([hi, dl - hi], axis=1).astype(BF)
    z = jnp.zeros((16, (heads - 2) * 128), BF)
    for d in range(4):
        outs[d][R * 32 : R * 32 + 16, 0:128] = both[d * 32 : d * 32 + 16]
        outs[d][R * 32 : R * 32 + 16, 128:256] = both[d * 32 + 16 : d * 32 + 32]
        outs[d][R * 32 : R * 32 + 16, 256:] = z


def attn_near(table, rel, qs, sets, slots):
    R, T, W = qs.shape[1:]
    heads = W // HD
    rows = heads * 128
    nb = 2 * slots
    body = functools.partial(attn_kernel, first=True, r0=0, R=R, heads=heads, nb=nb)
    return pl.pallas_call(
        body,
        in_specs=[SM] * 2 + [HBM] * 3,
        out_specs=[HBM, HBM, VM],
        scratch_shapes=[
            pltpu.VMEM((4, R, T, W), BF),
            pltpu.VMEM((R, rows, 128), BF),
            pltpu.VMEM((nb, 128, 128), BF),
            pltpu.VMEM((nb, 128, 128), BF),
            pltpu.VMEM((R, rows, 128), F32),
            pltpu.VMEM((R, rows, 128), F32),
            pltpu.VMEM((rows, 256), BF),
            pltpu.VMEM((rows, 256), BF),
            pltpu.SemaphoreType.DMA((8,)),
        ],
        out_shape=[
            jax.ShapeDtypeStruct((R, rows, 128), F32),
            jax.ShapeDtypeStruct((R, rows, 128), BF),
            jax.ShapeDtypeStruct((128, 128), F32),
        ],
        compiler_params=pltpu.CompilerParams(vmem_limit_bytes=48 << 20),
        cost_estimate=pl.CostEstimate(
            flops=4 * nb * rows * 128 * 128, bytes_accessed=12_000_000, transcendentals=nb * rows * 128
        ),
        name="attn_near",
    )(table, rel, qs, *sets)


def attn_far(table, bases, r0, R, qs, sets, slots, num, den, T, W):
    heads = W // HD
    rows = heads * 128
    nb = 2 * slots
    body = functools.partial(attn_kernel, first=False, r0=r0, R=R, heads=heads, nb=nb)
    return pl.pallas_call(
        body,
        in_specs=[SM] * 2 + [HBM] * 6 + [VM],
        out_specs=[VM] * 4,
        scratch_shapes=[
            pltpu.VMEM((R, rows, 128), BF),
            pltpu.VMEM((nb + R, 128, 128), BF),
            pltpu.VMEM((nb + R, 128, 128), BF),
            pltpu.VMEM((R, rows, 128), F32),
            pltpu.VMEM((R, rows, 128), F32),
            pltpu.VMEM((rows, 256), BF),
            pltpu.VMEM((rows, 256), BF),
            pltpu.VMEM((128, 128), jnp.int32),
            pltpu.SemaphoreType.DMA((6 + 8 * R,)),
        ],
        out_shape=[jax.ShapeDtypeStruct((R * T + 16, W), BF)] * 4,
        compiler_params=pltpu.CompilerParams(vmem_limit_bytes=48 << 20),
        cost_estimate=pl.CostEstimate(
            flops=2 * nb * rows * 128 * 128, bytes_accessed=12_000_000, transcendentals=nb * rows * 64
        ),
        name="attn_far",
    )(table, bases, qs, *sets, num, den)


def pair_table(req, lim, slot, count):
    n = req.shape[0]
    size = n + count + 2
    places = jnp.arange(size, dtype=jnp.int32)
    ids = jnp.arange(count + 1, dtype=jnp.int32)
    index = jnp.arange(n, dtype=jnp.int32)
    counts = jnp.sum((req[None, :] == ids[:, None]).astype(jnp.int32), axis=1)
    pairs = (counts + 1) // 2
    first = jnp.sum(jnp.where(ids[None, :] < ids[:, None], pairs[None, :], 0), axis=1)
    before = jnp.logical_and(req[None, :] == req[:, None], index[None, :] < index[:, None])
    rank = jnp.sum(before.astype(jnp.int32), axis=1)
    base = jnp.sum(jnp.where(req[:, None] == ids[None, :], first[None, :], 0), axis=1)
    place = 2 * base + rank
    hit = place[None, :] == places[:, None]
    slots = jnp.sum(jnp.where(hit, slot[None, :], 0), axis=1)
    lims = jnp.sum(jnp.where(hit, lim[None, :], 0), axis=1)
    owner = jnp.sum((first[None, 1:] <= places[:, None]).astype(jnp.int32), axis=1)
    owner = jnp.minimum(owner, count - 1)
    firsts = jnp.pad(first, (0, size - count - 1))
    return jnp.stack([slots, lims, owner, firsts])


def decode_kernel(req, lim, ctx, q, k_hbm, v_hbm, hand, dk, dv, out, k, v, acc, dacc, sem):
    k_copy = pltpu.make_async_copy(k_hbm, k, sem.at[0])
    v_copy = pltpu.make_async_copy(v_hbm, v, sem.at[1])
    k_copy.start()
    v_copy.start()
    scale = HD ** -0.5
    blocks = k.shape[0]
    handed = hand.shape[1]
    lane = lax.broadcasted_iota(jnp.int32, (1, 128), 1)
    acc[...] = jnp.zeros_like(acc)
    dacc[...] = jnp.zeros_like(dacc)
    k_copy.wait()
    v_copy.wait()

    def block(i, unused):
        r = req[i]
        s = lax.dot_general(q[r], k[i], NT, preferred_element_type=F32)
        w = jnp.where(lane < lim[i], jnp.exp(s * scale), 0.0)
        dacc[r] += w
        acc[r] += jnp.dot(w.astype(BF), v[i], preferred_element_type=F32)
        return 0

    lax.fori_loop(0, blocks, block, 0, unroll=True)

    def first_lane(w):
        return jnp.where(lane == 0, jnp.sum(w, axis=1, keepdims=True), 0.0)

    for r in range(handed):
        s = lax.dot_general(q[r], hand[0, r], NT, preferred_element_type=F32)
        w = jnp.exp(s * scale)
        dacc[r] += first_lane(w)
        acc[r] += jnp.dot(w.astype(BF), hand[1, r], preferred_element_type=F32)
    steps = 4
    for j in range(dk.shape[0]):
        r = ctx[0] * dk.shape[0] + j
        s = lax.dot_general(q[r], dk[j], NT, preferred_element_type=F32)
        row = lax.rem(lax.broadcasted_iota(jnp.int32, s.shape, 0), steps)
        col = lax.broadcasted_iota(jnp.int32, s.shape, 1)
        w = jnp.where(col <= row, jnp.exp(s * scale), 0.0)
        dacc[r] += first_lane(w)
        acc[r] += jnp.dot(w.astype(BF), dv[j], preferred_element_type=F32)
    out[:, :, 0:128] = acc[...].astype(BF)
    den = jnp.sum(dacc[...], axis=2, keepdims=True)
    hi = den.astype(BF)
    lo = (den - hi.astype(F32)).astype(BF)
    out[:, :, 128:256] = jnp.where(lane[None] < 64, hi, lo)


def decode(req, lim, ctx, q, k, v, hand, dk, dv):
    shape = q.shape
    return pl.pallas_call(
        decode_kernel,
        in_specs=[SM] * 3 + [VM] + [HBM] * 2 + [VM] * 3,
        out_specs=VM,
        scratch_shapes=[pltpu.VMEM(k.shape, BF), pltpu.VMEM(v.shape, BF), pltpu.VMEM(shape, F32), pltpu.VMEM(shape, F32), pltpu.SemaphoreType.DMA((2,))],
        out_shape=jax.ShapeDtypeStruct((shape[0], shape[1], 256), BF),
        compiler_params=pltpu.CompilerParams(vmem_limit_bytes=16 << 20),
        cost_estimate=pl.CostEstimate(flops=10**8, bytes_accessed=3_000_000, transcendentals=10**5),
        name="decode_terms",
    )(req, lim, ctx, q, k, v, hand, dk, dv)


def combine_kernel(*refs, decode_rows):
    if decode_rows:
        h0, h1, h2, h3, dec, out, parts, small, sem = refs
    else:
        h0, h1, h2, h3, out, parts, sem = refs
    copies = [pltpu.make_async_copy(h, parts.at[i], sem.at[i]) for i, h in enumerate((h0, h1, h2, h3))]
    for c in copies:
        c.start()
    rows = parts.shape[1] - 16
    heads = parts.shape[2] // HD
    if decode_rows:
        sums = jnp.sum(dec[...].astype(F32), axis=0)
        reqs = sums.shape[0]
        dden = sums[:, :, 128:129] + sums[:, :, 192:193]
        att = sums[:, :, :128] / dden
        small[...] = jnp.zeros_like(small)
        for j in range(reqs):
            for h in range(heads):
                small[j * 4 : j * 4 + 4, h * 128 : h * 128 + 128] = att[j, h * 4 : h * 4 + 4]
        out[rows : rows + small.shape[0]] = small[...].astype(BF)
    for c in copies:
        c.wait()

    def total(*at):
        t = parts[(0,) + at].astype(F32)
        for i in range(1, 4):
            t = t + parts[(i,) + at].astype(F32)
        return t

    tail = total(pl.ds(rows, 16), pl.ds(0, 256))
    den = jnp.concatenate([tail[:, :128], tail[:, 128:]], axis=0)
    inv = 1.0 / (den[:, :64] + den[:, 64:])
    for r in range(rows // 32):
        for h in range(heads):
            at = (pl.ds(r * 32, 32), pl.ds(h * 128, 128))
            out[at] = (total(*at) * inv[:, r * 16 + h : r * 16 + h + 1]).astype(BF)


def combine(os, dec=None):
    rows, width = os[0].shape
    more = [] if dec is None else [dec]
    out_rows = rows + 16 if more else rows - 16
    return pl.pallas_call(
        functools.partial(combine_kernel, decode_rows=len(more)),
        in_specs=[HBM] * 4 + [VM] * len(more),
        out_specs=VM,
        scratch_shapes=[pltpu.VMEM((4, rows, width), BF)]
        + [pltpu.VMEM((32, width), F32)] * len(more)
        + [pltpu.SemaphoreType.DMA((4,))],
        out_shape=jax.ShapeDtypeStruct((out_rows, width), BF),
        compiler_params=pltpu.CompilerParams(vmem_limit_bytes=24 << 20),
        cost_estimate=pl.CostEstimate(flops=10**6, bytes_accessed=2_500_000, transcendentals=0),
        name="combine",
    )(*os, *more)


def project_kernel(at, *refs, row0, gathered):
    if gathered:
        x, refs = refs[0], refs[1:]
        xs = [x.at[at[3 + d]] for d in range(4)]
    else:
        xs, refs = refs[:4], refs[4:]
    w, a1, a2, a3, b1, b2, b3 = refs[:7]
    refs = refs[7:]
    if row0 == 0:
        out, small, ws, stage, sem = refs
    else:
        _, out, ws, stage, sem = refs
    half = stage.shape[2]
    rows = stage.shape[1]
    copies = []
    for t, got in enumerate(((a1, a2, a3), (b1, b2, b3))):
        col = pl.multiple_of(at[t] * half, half)
        for d, part in enumerate([w.at[:, pl.ds(col, half)]] + list(got)):
            c = pltpu.make_async_copy(part, ws.at[t * 4 + d], sem.at[t * 4 + d])
            c.start()
            copies.append(c)
    outs = []
    for t in range(2):
        y = None
        for d in range(4):
            copies[t * 4 + d].wait()
            one = jnp.dot(xs[d][...], ws[t * 4 + d], preferred_element_type=F32)
            y = one if y is None else y + one
        side = at[2] if t == 0 else 1 - at[2]
        cols = pl.ds(pl.multiple_of(side * half, half), half)
        stage[t] = y[:rows].astype(BF)
        if row0 == 0:
            small[:, cols] = y[rows : rows + 16].astype(BF)
        c = pltpu.make_async_copy(stage.at[t], out.at[pl.ds(row0, rows), cols], sem.at[8 + t])
        c.start()
        outs.append(c)
    for c in outs:
        c.wait()


def project(at, xs, w, mine, theirs, total, out=None):
    rows, depth = xs[0].shape[-2:]
    half = mine[0].shape[1]
    first = out is None
    rows = rows - (32 if first else 0)
    row0 = 0 if first else total - rows
    shape = jax.ShapeDtypeStruct((total, 2 * half), BF)
    more = [] if first else [out]
    return pl.pallas_call(
        functools.partial(project_kernel, row0=row0, gathered=len(xs) == 1),
        in_specs=[SM] + [VM] * len(xs) + [HBM] * (7 + len(more)),
        out_specs=[HBM, VM] if first else HBM,
        out_shape=[shape, jax.ShapeDtypeStruct((16, 2 * half), BF)] if first else shape,
        scratch_shapes=[
            pltpu.VMEM((8, depth, half), BF),
            pltpu.VMEM((2, rows, half), BF),
            pltpu.SemaphoreType.DMA((10,)),
        ],
        input_output_aliases={} if first else {8 + len(xs): 0},
        compiler_params=pltpu.CompilerParams(vmem_limit_bytes=48 << 20),
        cost_estimate=pl.CostEstimate(
            flops=16 * rows * depth * half, bytes_accessed=14_000_000, transcendentals=0
        ),
        name="project",
    )(at, *xs, w, *mine, *theirs, *more)


def visible_tokens(req, blk, bounds):
    count = bounds.shape[0]
    hit = req[:, None] == jnp.arange(count, dtype=jnp.int32)[None, :]
    bound = jnp.sum(jnp.where(hit, bounds[None, :], 0), axis=1)
    return jnp.clip(bound - blk * PAGE, 0, PAGE)


def on_device(
    p_query, p_key, p_value, p_cache_k, p_cache_v, p_slot_req, p_slot_blk, p_offsets,
    d_query, d_key, d_value, d_cache_k, d_cache_v, d_slot_req, d_slot_blk, d_lengths, out_weight,
):
    me = lax.axis_index("ctx")
    column = lax.axis_index("tp")
    core = me % 2
    ctx = lax.axis_size("ctx")
    tp = lax.axis_size("tp")

    def along_y(x, d):
        return lax.ppermute(x, "ctx", [(i, (i + 4 * d) % ctx) for i in range(ctx)])

    def across(x, bit):
        return lax.ppermute(x, "ctx", [(i, i ^ bit) for i in range(ctx)])

    def along_x(x, d):
        return lax.ppermute(x, "tp", [(i, (i + d) % tp) for i in range(tp)])

    heads = p_query.shape[3] // HD
    reqs, span_len = p_query.shape[1:3]
    slots = p_slot_req.shape[1]
    steps = d_query.shape[2]
    width = heads * HD

    rings = [[z + 4 * y for y in range(ctx // 4)] for z in range(4)]
    qs = lax.all_gather(p_query, "ctx", axis_index_groups=rings, tiled=True)
    span = jnp.concatenate([p_key[0].reshape(-1, PAGE, HD), p_value[0].reshape(-1, PAGE, HD)], axis=0)
    m0 = jnp.concatenate([p_cache_k[0], p_cache_v[0], span], axis=0)
    half = out_weight.shape[1] // (2 * tp)
    block = lambda d: lax.dynamic_slice(
        out_weight, (0, (((column + d) % tp) * 2 + core) * half), (out_weight.shape[0], half)
    )
    m0, w1, w3, p_slot_req, d_query, span = lax.optimization_barrier(
        (m0, block(1), block(3), p_slot_req, d_query, span)
    )
    m2 = across(m0, 2)
    w1, w3 = along_x(w1, 1), along_x(w3, -1)
    m1 = across(m0, 1)

    lim0 = visible_tokens(p_slot_req[0], p_slot_blk[0], p_offsets[0])
    note = jnp.pad(jnp.stack([p_slot_req[0], lim0]), ((0, 6), (0, HD - slots)))
    notes = [note, across(note, 1), across(note, 2), across(note, 3)]
    handed = lax.ppermute(span, "sec", [(0, 1), (1, 0)]).reshape(2, reqs, span_len, HD)

    dq = d_query[0].reshape(2, steps, heads, HD).transpose(0, 2, 1, 3).reshape(2, steps * heads, HD)
    dq = jnp.pad(dq, ((0, 0), (0, 32 - steps * heads), (0, 0)))
    dq_all = lax.all_to_all(jnp.broadcast_to(dq[None], (ctx,) + dq.shape), "ctx", 0, 0)

    index = jnp.arange(slots, dtype=jnp.int32)
    ids = jnp.arange(reqs, dtype=jnp.int32)
    near_table = pair_table(
        jnp.concatenate([n[0, :slots] for n in notes[:2]]),
        jnp.concatenate([n[1, :slots] for n in notes[:2]]),
        jnp.concatenate([index, index + slots]),
        reqs,
    )
    far_table = pair_table(
        jnp.concatenate([ids] + [n[0, :slots] for n in notes[2:]]),
        jnp.concatenate([jnp.full_like(ids, 200)] + [n[1, :slots] for n in notes[2:]]),
        jnp.concatenate([jnp.zeros_like(ids), index, index + slots]),
        reqs,
    )
    ring = (me // 4 + jnp.array([0, 3, 1, 2], dtype=jnp.int32)) % (ctx // 4)
    bases = jnp.concatenate([ring * 4 + me % 4, me ^ jnp.arange(4, dtype=jnp.int32)]).astype(jnp.int32) * span_len

    num, queries, den = attn_near(near_table, ring.astype(jnp.int32), qs, (m0, m1), slots)
    m2, w1, w3, out_weight, num, queries, den, dq_all, handed = lax.optimization_barrier(
        (m2, w1, w3, out_weight, num, queries, den, dq_all, handed)
    )
    m3 = across(m2, 1)
    w2 = along_x(
        lax.dynamic_slice(out_weight, (0, (((column + 2) % tp) * 2 + core) * half), (out_weight.shape[0], half)), 2
    )
    pad = ((0, 0), (0, 16 - steps), (0, 0))
    dec = decode(
        d_slot_req[0],
        visible_tokens(d_slot_req[0], d_slot_blk[0], d_lengths[0]),
        me.reshape(1),
        dq_all.reshape(ctx * 2, 32, HD),
        d_cache_k[0],
        d_cache_v[0],
        handed,
        jnp.pad(d_key[0], pad),
        jnp.pad(d_value[0], pad),
    )
    dec, far_table = lax.optimization_barrier((dec, far_table))
    dec = lax.all_to_all(dec.reshape(ctx, 2, 32, 256), "ctx", 0, 0)
    sets = (m0, m1, m2, m3)
    hr = reqs // 2
    oa = attn_far(far_table, bases, 0, hr, queries, sets, slots, num, den, span_len, width)
    oa, w1, den = lax.optimization_barrier((oa, w1, den))
    sent_a = [oa[0], along_y(oa[1], -1), along_y(oa[2], 1), along_y(oa[3], 2)]
    b1 = across(w1, 1)
    ob = attn_far(far_table, bases, hr, hr, queries, sets, slots, num, den, span_len, width)
    ob, w3, sent_a = lax.optimization_barrier((ob, w3, sent_a))
    sent_b = [ob[0], along_y(ob[1], -1), along_y(ob[2], 1), along_y(ob[3], 2)]
    b3 = across(w3, 1)
    xa = combine(sent_a, dec)
    xa, w2 = lax.optimization_barrier((xa, w2))
    xa = lax.all_gather(xa, "tp")
    b2 = across(w2, 1)
    xb = combine(sent_b)
    xb = [xb, along_x(xb, 1), along_x(xb, -1), along_x(xb, 2)]
    mine, theirs = (w1, w3, w2), (b1, b3, b2)
    at = jnp.stack(
        [column * 2 + core, column * 2 + 1 - core, core, column]
        + [(column + d) % tp for d in (3, 1, 2)]
    ).astype(jnp.int32)
    total = reqs * span_len
    out, small = project(at, [xa], out_weight, mine, theirs, total)
    out = project(at, xb, out_weight, mine, theirs, total, out)
    width = out.shape[1]
    return out.reshape(1, reqs, span_len, width), small[: 2 * steps].reshape(1, 2, steps, width)


def solution(mesh):
    placed = (
        P("sec", None, "ctx", "tp"),
        P("sec", None, "ctx", "tp"),
        P("sec", None, "ctx", "tp"),
        P("sec", "ctx", None, "tp"),
        P("sec", "ctx", None, "tp"),
        P("sec", "ctx"),
        P("sec", "ctx"),
        P("sec", None),
        P("sec", "ctx", None, "tp"),
        P("sec", "ctx", None, "tp"),
        P("sec", "ctx", None, "tp"),
        P("sec", "ctx", None, "tp"),
        P("sec", "ctx", None, "tp"),
        P("sec", "ctx"),
        P("sec", "ctx"),
        P("sec", None),
        P("tp", None),
    )
    return jax.shard_map(
        on_device,
        mesh=mesh,
        in_specs=placed,
        out_specs=(P("sec", None, "ctx", "tp"), P("sec", "ctx", None, "tp")),
        check_vma=False,
    )
```

time: 211 us -> 170 us (0.81)
  the two profiles are of different devices: /device:TPU:24 before, /device:TPU:1 now
where the time goes in v3:
time: 170 us; the launch traced here: 169 us
  Pallas kernels  58.2 us (34%)
  starting transfers between devices  36.7 us (22%)
  waiting for transfers between devices  31.4 us (18%)
  local copies, waits for them, and re-layouts  22.1 us (13%)
  between operations  14.6 us (9%)
  other arithmetic  5.57 us (3%)
    pallas_call x2, Pallas kernels, attn_far(): pl.pallas_call(body, in_specs=[SM] * 2 + [HBM] * 6 + [VM], out_specs=[VM]...  18.5 us
    all_gather x1, waiting for transfers between devices, on_device(): qs = lax.all_gather(p_query, 'ctx', axis_index_groups=rings, tiled=True)  17.2 us
    ppermute x6, waiting for transfers between devices, along_y(): return lax.ppermute(x, 'ctx', [(i, (i + 4 * d) % ctx) for i in range(ctx)])  14.2 us
    pallas_call x1, Pallas kernels, attn_near(): pl.pallas_call(body, in_specs=[SM] * 2 + [HBM] * 3, out_specs=[HBM, HBM,...  14 us
    pallas_call x2, Pallas kernels, project(): pl.pallas_call(functools.partial(project_kernel, row0=row0, gathered=len(...  13.8 us
    unnamed x65, local copies, waits for them, and re-layouts  13.8 us
    ppermute x9, starting transfers between devices, across(): return lax.ppermute(x, 'ctx', [(i, i ^ bit) for i in range(ctx)])  9.05 us
    ppermute x6, starting transfers between devices, along_x(): return lax.ppermute(x, 'tp', [(i, (i + d) % tp) for i in range(tp)])  8.25 us
  transfers between devices with their start and end apart: 26, of which 4 were waited for; matrix products, arithmetic and copies ran while one was open for 4% of the time, Pallas kernels for 31%

profile of v3, /device:TPU:1, one launch (start us, length us, event | category | flops | bytes accessed | tf_op | source)
XLA Modules:
  0.0 168.5 jit_solution(11945542379085131667)
XLA Ops:
  7.3 1.6 pad_maximum_fusion.1
  8.8 1.7 %pad_maximum_fusion.refs_2_ = bf16[52,128,128]{2,1,0:T(8,128)(2,1)S(1)} fusion(bf16[2,128,128]{2,1,0:T(8,128)(2,1)} %bitcast.70, bf16[2,128,128]{2,1,0:T(8,128)(2,1)} %bitcast.72, bf16[24,128,128]{2,1,0:T(8,128)(2,1)} %bitcast.67, bf16[24,128,128]{2,1,0:T(8,128)(2,1)} %bitcast.68), kind=kLoop, calls=%fused_computation | loop fusion | flops 2555904 | bytes 3407872 | tf_op jit(solution)/shard_map/concatenate | solution.py:465
  10.7 3.9 %constant_dynamic-slice_fusion.1 = (bf16[896,896]{1,0:T(8,128)(2,1)}, bf16[896,896]{1,0:T(8,128)(2,1)}) fusion(bf16[896,7168]{1,0:T(8,128)(2,1)} %refs_4_, s32[]{:T(128)S(6)} %select_n.107, s32[]{:T(128)S(6)} %select_n.106), kind=kLoop, calls=%fused_computation.48 | loop fusion | bytes 6422536 | tf_op jit(solution)/shard_map/dynamic_slice | solution.py:467
  14.7 3.1 %collective-permute-start.7 = (s32[8,128]{1,0:T(8,128)S(1)}, s32[8,128]{1,0:T(8,128)S(1)}, u32[]{:S(2)}, u32[]{:S(2)}) collective-permute-start(s32[8,128]{1,0:T(8,128)S(1)} %pad.23), channel_id=1, source_target_pairs={{0,12},{4,8},{8,4},{12,0},{16,28},{20,24},{24,20},{28,16},{32,44},... | collective-permute-start | bytes 12296 | tf_op jit(solution)/shard_map/ppermute | solution.py:451
  18.3 1.1 collective-permute-start
  20.9 4.6 %all-to-all-start = ((bf16[16,2,32,128]{3,2,1,0:T(8,128)(2,1)}), bf16[16,2,32,128]{3,2,1,0:T(8,128)(2,1)}, u32[]{:S(2)}, u32[]{:S(2)}) async-start(bf16[16,2,32,128]{3,2,1,0:T(8,128)(2,1)} %broadcast_in_dim.163), calls=%async_computation | async-start | bytes 524288 | tf_op jit(solution)/shard_map/all_to_all | solution.py:484
  26.0 1.3 collective-permute-start.1
  27.2 1.5 collective-permute-start.2
  28.9 3.4 %collective-permute-start.5 = (bf16[4,128,128]{2,1,0:T(8,128)(2,1)}, bf16[4,128,128]{2,1,0:T(8,128)(2,1)}, u32[]{:S(2)}, u32[]{:S(2)}) collective-permute-start(bf16[4,128,128]{2,1,0:T(8,128)(2,1)} %pad_maximum_fusion.1), channel_id=1, source_target_pairs={{0,64},{64,0},{1,65},{65,1},{2,66},{66,2},{3,67},{67,3},{4,68},{68... | collective-permute-start | bytes 393224 | tf_op jit(solution)/shard_map/ppermute | solution.py:480
  33.3 17.2 %all-gather.4.cloned.1.call-done.refs_1_ = bf16[4,8,32,896]{3,2,1,0:T(8,128)(2,1)} async-done(((bf16[1,8,32,896]{3,2,1,0:T(8,128)(2,1)}), bf16[4,8,32,896]{3,2,1,0:T(8,128)(2,1)}) %all-gather.4.cloned.1.call-update) | async-done | bytes 1835024 | tf_op jit(solution)/shard_map/all_gather | solution.py:463
  50.4 14.0 %attn_near.1 = (f32[8,896,128]{2,1,0:T(8,128)}, bf16[8,896,128]{2,1,0:T(8,128)(2,1)S(1)}, f32[128,128]{1,0:T(8,128)S(1)}) custom-call(s32[4,58]{1,0:T(4,128)S(1)} %pad_add_fusion.table, s32[4]{0:T(128)S(1)} %get-tuple-element.101.refs_0_, bf16[4,8,32,896]{3,2,1,0:T(8,128)(2,1)} %all-gather.4.cloned.1.call-done.refs_1_, ...), custom_call_target="tpu_custom_call" | custom-call | flops 2818572288 | bytes 12000000 | tf_op jit(solution)/shard_map/attn_near/pallas_call | solution.py:166
  64.5 1.2 copy-done
  67.0 2.7 %constant_dynamic-slice_fusion = bf16[896,896]{1,0:T(8,128)(2,1)} fusion(bf16[896,7168]{1,0:T(8,128)(2,1)} %refs_4_, s32[]{:T(128)S(6)} %select_n.122), kind=kLoop, calls=%fused_computation.47 | loop fusion | bytes 3211268 | tf_op jit(solution)/shard_map/dynamic_slice | solution.py:509
  69.7 2.8 %collective-permute-start.18 = (bf16[896,896]{1,0:T(8,128)(2,1)}, bf16[896,896]{1,0:T(8,128)(2,1)}, u32[]{:S(2)}, u32[]{:S(2)}) collective-permute-start(bf16[896,896]{1,0:T(8,128)(2,1)} %constant_dynamic-slice_fusion), channel_id=1, source_target_pairs={{0,2},{1,3},{2,0},{3,1},{4,6},{5,7},{6,4},{7,5},{8,10},{9,11},{10,... | collective-permute-start | bytes 4816904 | tf_op jit(solution)/shard_map/ppermute | solution.py:454
  73.0 6.5 %decode_terms.1 = bf16[32,32,256]{2,1,0:T(8,128)(2,1)S(1)} custom-call(s32[24]{0:T(128)S(1)} %bitcast.65, s32[24]{0:T(128)S(1)} %fusion.4.lim, s32[1]{0:T(128)} %bitcast.10.ctx, bf16[32,32,128]{2,1,0:T(8,128)(2,1)} %bitcast.28.q, bf16[24,128,128]{2,1,0:T(8,128)(2,1)S(1)} %bitcast.62, bf16[24,128,128]{2,1,0:T(8,128)(2,1)S(1)} %bitcast.63, ...), custom_call_target="tpu_custom_call" | custom-call | flops 100000000 | bytes 3000000 | tf_op jit(solution)/shard_map/decode_terms/pallas_call | solution.py:295
  80.3 4.8 %all-to-all-start.1 = ((bf16[16,2,32,256]{3,2,1,0:T(8,128)(2,1)}), bf16[16,2,32,256]{3,2,1,0:T(8,128)(2,1)}, u32[]{:S(2)}, u32[]{:S(2)}) async-start(bf16[16,2,32,256]{3,2,1,0:T(8,128)(2,1)} %bitcast.60), calls=%async_computation.1 | async-start | bytes 1048576 | tf_op jit(solution)/shard_map/all_to_all | solution.py:524
  85.3 10.6 %attn_far.2 = (bf16[144,896]{1,0:T(8,128)(2,1)S(1)}, bf16[144,896]{1,0:T(8,128)(2,1)S(1)}, bf16[144,896]{1,0:T(8,128)(2,1)S(1)}, bf16[144,896]{1,0:T(8,128)(2,1)S(1)}) custom-call(s32[4,66]{1,0:T(4,128)S(1)} %pad_add_fusion.1.table, s32[8]{0:T(128)S(1)} %add_multiply_fusion.refs_0_, bf16[8,896,128]{2,1,0:T(8,128)(2,1)} %copy-done, ...), custom_call_target="tpu_custom_call" | custom-call | flops 1409286144 | bytes 12000000 | tf_op jit(solution)/shard_map/attn_far/pallas_call | solution.py:199
  96.6 1.9 %collective-permute-start.9 = (bf16[144,896]{1,0:T(8,128)(2,1)S(1)}, bf16[144,896]{1,0:T(8,128)(2,1)S(1)}, u32[]{:S(2)}, u32[]{:S(2)}) collective-permute-start(bf16[144,896]{1,0:T(8,128)(2,1)S(1)} %get-tuple-element.77), channel_id=1, source_target_pairs={{0,48},{4,52},{8,56},{12,60},{16,0},{20,4},{24,8},{28,12},{32,16},... | collective-permute-start | bytes 774152 | tf_op jit(solution)/shard_map/ppermute | solution.py:448
  98.5 1.8 %collective-permute-start.11 = (bf16[144,896]{1,0:T(8,128)(2,1)S(1)}, bf16[144,896]{1,0:T(8,128)(2,1)S(1)}, u32[]{:S(2)}, u32[]{:S(2)}) collective-permute-start(bf16[144,896]{1,0:T(8,128)(2,1)S(1)} %get-tuple-element.79), channel_id=1, source_target_pairs={{0,32},{4,36},{8,40},{12,44},{16,48},{20,52},{24,56},{28,60},{32,0... | collective-permute-start | bytes 774152 | tf_op jit(solution)/shard_map/ppermute | solution.py:448
  100.3 7.9 %attn_far.3 = (bf16[144,896]{1,0:T(8,128)(2,1)S(1)}, bf16[144,896]{1,0:T(8,128)(2,1)S(1)}, bf16[144,896]{1,0:T(8,128)(2,1)S(1)}, bf16[144,896]{1,0:T(8,128)(2,1)S(1)}) custom-call(s32[4,66]{1,0:T(4,128)S(1)} %pad_add_fusion.1.table, s32[8]{0:T(128)S(1)} %add_multiply_fusion.refs_0_, bf16[8,896,128]{2,1,0:T(8,128)(2,1)} %copy-done, ...), custom_call_target="tpu_custom_call" | custom-call | flops 1409286144 | bytes 12000000 | tf_op jit(solution)/shard_map/attn_far/pallas_call | solution.py:199
  113.1 0.9 copy-done.8
  116.9 3.7 %combine.3 = bf16[160,896]{1,0:T(8,128)(2,1)} custom-call(bf16[144,896]{1,0:T(8,128)(2,1)S(1)} %copy-done.8, bf16[144,896]{1,0:T(8,128)(2,1)S(1)} %copy-done.10, bf16[144,896]{1,0:T(8,128)(2,1)S(1)} %copy-done.12, bf16[144,896]{1,0:T(8,128)(2,1)S(1)} %copy-done.14, bf16[16,2,32,256]{3,2,1,0:T(8,128)(2,1)} %all-to-all-done.1.refs_4_), custom_call_target="tpu_custom_call" | custom-call | flops 1000000 | bytes 2500000 | tf_op jit(solution)/shard_map/combine/pallas_call | solution.py:349
  120.6 2.3 %collective-permute-start.19 = (bf16[896,896]{1,0:T(8,128)(2,1)}, bf16[896,896]{1,0:T(8,128)(2,1)S(1)}, u32[]{:S(2)}, u32[]{:S(2)}) collective-permute-start(bf16[896,896]{1,0:T(8,128)(2,1)} %collective-permute-done.1.refs_2_.refs_5_), channel_id=1, source_target_pairs={{0,4},{4,0},{8,12},{12,8},{16,20},{20,16},{24,28},{28,24},{32,36},... | collective-permute-start | bytes 4816904 | tf_op jit(solution)/shard_map/ppermute | solution.py:451
  124.2 1.2 collective-permute-start.13
  125.4 6.4 %collective-permute-done.12.refs_1_ = bf16[144,896]{1,0:T(8,128)(2,1)S(1)} collective-permute-done((bf16[144,896]{1,0:T(8,128)(2,1)S(1)}, bf16[144,896]{1,0:T(8,128)(2,1)S(1)}, u32[]{:S(2)}, u32[]{:S(2)}) %collective-permute-start.12) | collective-permute-done | bytes 258080 | tf_op jit(solution)/shard_map/ppermute | solution.py:448
  132.8 7.5 %collective-permute-done.14.refs_3_ = bf16[144,896]{1,0:T(8,128)(2,1)S(1)} collective-permute-done((bf16[144,896]{1,0:T(8,128)(2,1)S(1)}, bf16[144,896]{1,0:T(8,128)(2,1)S(1)}, u32[]{:S(2)}, u32[]{:S(2)}) %collective-permute-start.14) | collective-permute-done | bytes 258080 | tf_op jit(solution)/shard_map/ppermute | solution.py:448
  140.4 1.7 combine.2.refs_0_
  142.4 2.4 %collective-permute-start.16 = (bf16[128,896]{1,0:T(8,128)(2,1)S(1)}, bf16[128,896]{1,0:T(8,128)(2,1)S(1)}, u32[]{:S(2)}, u32[]{:S(2)}) collective-permute-start(bf16[128,896]{1,0:T(8,128)(2,1)S(1)} %combine.2.refs_0_), channel_id=1, source_target_pairs={{0,3},{1,0},{2,1},{3,2},{4,7},{5,4},{6,5},{7,6},{8,11},{9,8},{10,9... | collective-permute-start | bytes 688136 | tf_op jit(solution)/shard_map/ppermute | solution.py:454
  144.9 1.0 copy-done.22
  146.0 1.3 copy-done.2
  147.2 7.2 %project.2 = (bf16[256,1792]{1,0:T(8,128)(2,1)}, bf16[16,1792]{1,0:T(8,128)(2,1)S(1)}) custom-call(s32[7]{0:T(128)S(1)} %stack.61.at, bf16[4,160,896]{2,1,0:T(8,128)(2,1)S(1)} %bitcast.61, bf16[896,7168]{1,0:T(8,128)(2,1)} %refs_4_, bf16[896,896]{1,0:T(8,128)(2,1)} %collective-permute-done.1.refs_2_.refs_5_, ...), custom_call_target="tpu_custom_call" | custom-call | flops 1644167168 | bytes 14000000 | tf_op jit(solution)/shard_map/project/pallas_call | solution.py:411
  155.0 6.7 %project.3 = bf16[256,1792]{1,0:T(8,128)(2,1)} custom-call(s32[7]{0:T(128)S(1)} %stack.61.at, bf16[128,896]{1,0:T(8,128)(2,1)S(1)} %combine.2.refs_0_, bf16[128,896]{1,0:T(8,128)(2,1)S(1)} %collective-permute-done.15.refs_1_, bf16[128,896]{1,0:T(8,128)(2,1)S(1)} %collective-permute-done.16.refs_2_, ...), custom_call_target="tpu_custom_call", output_to_operand_aliasing={{}: (12, {})} | custom-call | flops 1644167168 | bytes 14000000 | tf_op jit(solution)/shard_map/project/pallas_call | solution.py:411
  (155 shorter events, 18.3 us)
Async XLA Ops:
  7.2 43.3 %all-gather.4.cloned.1.call-start = ((), (), s32[]{:S(2)}) async-start(), calls=%async_computation.2 | async-start | bytes 2293760 | tf_op jit(solution)/shard_map/all_gather | solution.py:463
  10.6 15.0 %copy-start.15 = (s32[1,24]{1,0:T(1,128)S(1)}, s32[1,24]{1,0:T(1,128)}, u32[]{:S(2)}) copy-start(s32[1,24]{1,0:T(1,128)} %param.31) | copy-start | bytes 292
  10.6 15.1 %copy-start.31 = (s32[1,24]{1,0:T(1,128)S(1)}, s32[1,24]{1,0:T(1,128)}, u32[]{:S(2)}) copy-start(s32[1,24]{1,0:T(1,128)} %param.32) | copy-start | bytes 292
  10.6 15.2 %copy-start.26 = (s32[4]{0:T(128)S(1)}, s32[4]{0:T(128)}, u32[]{:S(2)}) copy-start(s32[4]{0:T(128)} %constant.114.clone) | copy-start | bytes 52
  10.6 15.3 %copy-start.24 = (bf16[1,2,4,128]{3,2,1,0:T(4,128)(2,1)S(1)}, bf16[1,2,4,128]{3,2,1,0:T(4,128)(2,1)}, u32[]{:S(2)}) copy-start(bf16[1,2,4,128]{3,2,1,0:T(4,128)(2,1)} %param.27) | copy-start | bytes 6148
  10.7 15.3 %copy-start.25 = (bf16[1,2,4,128]{3,2,1,0:T(4,128)(2,1)S(1)}, bf16[1,2,4,128]{3,2,1,0:T(4,128)(2,1)}, u32[]{:S(2)}) copy-start(bf16[1,2,4,128]{3,2,1,0:T(4,128)(2,1)} %param.28) | copy-start | bytes 6148
  14.7 11.2 %collective-permute-start.7 = (s32[8,128]{1,0:T(8,128)S(1)}, s32[8,128]{1,0:T(8,128)S(1)}, u32[]{:S(2)}, u32[]{:S(2)}) collective-permute-start(s32[8,128]{1,0:T(8,128)S(1)} %pad.23), channel_id=1, source_target_pairs={{0,12},{4,8},{8,4},{12,0},{16,28},{20,24},{24,20},{28,16},{32,44},... | collective-permute-start | bytes 12296 | tf_op jit(solution)/shard_map/ppermute | solution.py:451
  17.8 9.4 %collective-permute-start.6 = (s32[8,128]{1,0:T(8,128)S(1)}, s32[8,128]{1,0:T(8,128)S(1)}, u32[]{:S(2)}, u32[]{:S(2)}) collective-permute-start(s32[8,128]{1,0:T(8,128)S(1)} %pad.23), channel_id=1, source_target_pairs={{0,8},{4,12},{8,0},{12,4},{16,24},{20,28},{24,16},{28,20},{32,40},... | collective-permute-start | bytes 12296 | tf_op jit(solution)/shard_map/ppermute | solution.py:451
  17.8 11.1 %collective-permute-start.3 = (s32[8,128]{1,0:T(8,128)S(1)}, s32[8,128]{1,0:T(8,128)S(1)}, u32[]{:S(2)}, u32[]{:S(2)}) collective-permute-start(s32[8,128]{1,0:T(8,128)S(1)} %pad.23), channel_id=1, source_target_pairs={{0,4},{4,0},{8,12},{12,8},{16,20},{20,16},{24,28},{28,24},{32,36},... | collective-permute-start | bytes 12296 | tf_op jit(solution)/shard_map/ppermute | solution.py:451
  18.3 47.5 %collective-permute-start = (bf16[52,128,128]{2,1,0:T(8,128)(2,1)S(1)}, bf16[52,128,128]{2,1,0:T(8,128)(2,1)S(1)}, u32[]{:S(2)}, u32[]{:S(2)}) collective-permute-start(bf16[52,128,128]{2,1,0:T(8,128)(2,1)S(1)} %pad_maximum_fusion.refs_2_), channel_id=1, source_target_pairs={{0,8},{4,12},{8,0},{12,4},{16,24},{20,28},{24,16},{28,20},{32,40},... | collective-permute-start | bytes 5111816 | tf_op jit(solution)/shard_map/ppermute | solution.py:451
  19.4 13.9 %collective-permute-start.4 = (bf16[52,128,128]{2,1,0:T(8,128)(2,1)S(1)}, bf16[52,128,128]{2,1,0:T(8,128)(2,1)}, u32[]{:S(2)}, u32[]{:S(2)}) collective-permute-start(bf16[52,128,128]{2,1,0:T(8,128)(2,1)S(1)} %pad_maximum_fusion.refs_2_), channel_id=1, source_target_pairs={{0,4},{4,0},{8,12},{12,8},{16,20},{20,16},{24,28},{28,24},{32,36},... | collective-permute-start | bytes 5111816 | tf_op jit(solution)/shard_map/ppermute | solution.py:451
  20.9 44.8 %all-to-all-start = ((bf16[16,2,32,128]{3,2,1,0:T(8,128)(2,1)}), bf16[16,2,32,128]{3,2,1,0:T(8,128)(2,1)}, u32[]{:S(2)}, u32[]{:S(2)}) async-start(bf16[16,2,32,128]{3,2,1,0:T(8,128)(2,1)} %broadcast_in_dim.163), calls=%async_computation | async-start | bytes 524288 | tf_op jit(solution)/shard_map/all_to_all | solution.py:484
  26.0 39.8 %collective-permute-start.1 = (bf16[896,896]{1,0:T(8,128)(2,1)}, bf16[896,896]{1,0:T(8,128)(2,1)}, u32[]{:S(2)}, u32[]{:S(2)}) collective-permute-start(bf16[896,896]{1,0:T(8,128)(2,1)} %get-tuple-element.50), channel_id=1, source_target_pairs={{0,1},{1,2},{2,3},{3,0},{4,5},{5,6},{6,7},{7,4},{8,9},{9,10},{10,1... | collective-permute-start | bytes 4816904 | tf_op jit(solution)/shard_map/ppermute | solution.py:454
  27.2 38.5 %collective-permute-start.2 = (bf16[896,896]{1,0:T(8,128)(2,1)}, bf16[896,896]{1,0:T(8,128)(2,1)}, u32[]{:S(2)}, u32[]{:S(2)}) collective-permute-start(bf16[896,896]{1,0:T(8,128)(2,1)} %get-tuple-element.51), channel_id=1, source_target_pairs={{0,3},{1,0},{2,1},{3,2},{4,7},{5,4},{6,5},{7,6},{8,11},{9,8},{10,9... | collective-permute-start | bytes 4816904 | tf_op jit(solution)/shard_map/ppermute | solution.py:454
  28.9 36.8 %collective-permute-start.5 = (bf16[4,128,128]{2,1,0:T(8,128)(2,1)}, bf16[4,128,128]{2,1,0:T(8,128)(2,1)}, u32[]{:S(2)}, u32[]{:S(2)}) collective-permute-start(bf16[4,128,128]{2,1,0:T(8,128)(2,1)} %pad_maximum_fusion.1), channel_id=1, source_target_pairs={{0,64},{64,0},{1,65},{65,1},{2,66},{66,2},{3,67},{67,3},{4,68},{68... | collective-permute-start | bytes 393224 | tf_op jit(solution)/shard_map/ppermute | solution.py:480
  65.8 19.5 %collective-permute-start.8 = (bf16[52,128,128]{2,1,0:T(8,128)(2,1)S(1)}, bf16[52,128,128]{2,1,0:T(8,128)(2,1)}, u32[]{:S(2)}, u32[]{:S(2)}) collective-permute-start(bf16[52,128,128]{2,1,0:T(8,128)(2,1)S(1)} %collective-permute-done.refs_4_), channel_id=1, source_target_pairs={{0,4},{4,0},{8,12},{12,8},{16,20},{20,16},{24,28},{28,24},{32,36},... | collective-permute-start | bytes 5111816 | tf_op jit(solution)/shard_map/ppermute | solution.py:451
  69.7 50.9 %collective-permute-start.18 = (bf16[896,896]{1,0:T(8,128)(2,1)}, bf16[896,896]{1,0:T(8,128)(2,1)}, u32[]{:S(2)}, u32[]{:S(2)}) collective-permute-start(bf16[896,896]{1,0:T(8,128)(2,1)} %constant_dynamic-slice_fusion), channel_id=1, source_target_pairs={{0,2},{1,3},{2,0},{3,1},{4,6},{5,7},{6,4},{7,5},{8,10},{9,11},{10,... | collective-permute-start | bytes 4816904 | tf_op jit(solution)/shard_map/ppermute | solution.py:454
  80.3 32.8 %all-to-all-start.1 = ((bf16[16,2,32,256]{3,2,1,0:T(8,128)(2,1)}), bf16[16,2,32,256]{3,2,1,0:T(8,128)(2,1)}, u32[]{:S(2)}, u32[]{:S(2)}) async-start(bf16[16,2,32,256]{3,2,1,0:T(8,128)(2,1)} %bitcast.60), calls=%async_computation.1 | async-start | bytes 1048576 | tf_op jit(solution)/shard_map/all_to_all | solution.py:524
  85.2 59.8 %all-gather.6.cloned.1.call-start = ((), (), s32[]{:S(2)}) async-start(), calls=%async_computation.3 | async-start | bytes 1433600 | tf_op jit(solution)/shard_map/all_gather | solution.py:537
  96.6 14.4 %collective-permute-start.9 = (bf16[144,896]{1,0:T(8,128)(2,1)S(1)}, bf16[144,896]{1,0:T(8,128)(2,1)S(1)}, u32[]{:S(2)}, u32[]{:S(2)}) collective-permute-start(bf16[144,896]{1,0:T(8,128)(2,1)S(1)} %get-tuple-element.77), channel_id=1, source_target_pairs={{0,48},{4,52},{8,56},{12,60},{16,0},{20,4},{24,8},{28,12},{32,16},... | collective-permute-start | bytes 774152 | tf_op jit(solution)/shard_map/ppermute | solution.py:448
  98.5 13.2 %collective-permute-start.10 = (bf16[144,896]{1,0:T(8,128)(2,1)S(1)}, bf16[144,896]{1,0:T(8,128)(2,1)S(1)}, u32[]{:S(2)}, u32[]{:S(2)}) collective-permute-start(bf16[144,896]{1,0:T(8,128)(2,1)S(1)} %get-tuple-element.78), channel_id=1, source_target_pairs={{0,16},{4,20},{8,24},{12,28},{16,32},{20,36},{24,40},{28,44},{32,4... | collective-permute-start | bytes 774152 | tf_op jit(solution)/shard_map/ppermute | solution.py:448
  98.5 13.9 %collective-permute-start.11 = (bf16[144,896]{1,0:T(8,128)(2,1)S(1)}, bf16[144,896]{1,0:T(8,128)(2,1)S(1)}, u32[]{:S(2)}, u32[]{:S(2)}) collective-permute-start(bf16[144,896]{1,0:T(8,128)(2,1)S(1)} %get-tuple-element.79), channel_id=1, source_target_pairs={{0,32},{4,36},{8,40},{12,44},{16,48},{20,52},{24,56},{28,60},{32,0... | collective-permute-start | bytes 774152 | tf_op jit(solution)/shard_map/ppermute | solution.py:448
  111.7 28.7 %copy-start.6 = (bf16[144,896]{1,0:T(8,128)(2,1)S(1)}, bf16[144,896]{1,0:T(8,128)(2,1)}, u32[]{:S(2)}) copy-start(bf16[144,896]{1,0:T(8,128)(2,1)} %copy-done.5) | copy-start | bytes 774148
  120.6 24.2 %collective-permute-start.19 = (bf16[896,896]{1,0:T(8,128)(2,1)}, bf16[896,896]{1,0:T(8,128)(2,1)S(1)}, u32[]{:S(2)}, u32[]{:S(2)}) collective-permute-start(bf16[896,896]{1,0:T(8,128)(2,1)} %collective-permute-done.1.refs_2_.refs_5_), channel_id=1, source_target_pairs={{0,4},{4,0},{8,12},{12,8},{16,20},{20,16},{24,28},{28,24},{32,36},... | collective-permute-start | bytes 4816904 | tf_op jit(solution)/shard_map/ppermute | solution.py:451
  122.9 22.0 %collective-permute-start.20 = (bf16[896,896]{1,0:T(8,128)(2,1)}, bf16[896,896]{1,0:T(8,128)(2,1)}, u32[]{:S(2)}, u32[]{:S(2)}) collective-permute-start(bf16[896,896]{1,0:T(8,128)(2,1)} %collective-permute-done.2.refs_3_.refs_6_), channel_id=1, source_target_pairs={{0,4},{4,0},{8,12},{12,8},{16,20},{20,16},{24,28},{28,24},{32,36},... | collective-permute-start | bytes 4816904 | tf_op jit(solution)/shard_map/ppermute | solution.py:451
  123.0 21.9 %collective-permute-start.21 = (bf16[896,896]{1,0:T(8,128)(2,1)}, bf16[896,896]{1,0:T(8,128)(2,1)}, u32[]{:S(2)}, u32[]{:S(2)}) collective-permute-start(bf16[896,896]{1,0:T(8,128)(2,1)} %collective-permute-done.18.refs_4_.refs_7_), channel_id=1, source_target_pairs={{0,4},{4,0},{8,12},{12,8},{16,20},{20,16},{24,28},{28,24},{32,36},... | collective-permute-start | bytes 4816904 | tf_op jit(solution)/shard_map/ppermute | solution.py:451
  123.4 8.4 %collective-permute-start.12 = (bf16[144,896]{1,0:T(8,128)(2,1)S(1)}, bf16[144,896]{1,0:T(8,128)(2,1)S(1)}, u32[]{:S(2)}, u32[]{:S(2)}) collective-permute-start(bf16[144,896]{1,0:T(8,128)(2,1)S(1)} %copy-done.21), channel_id=1, source_target_pairs={{0,48},{4,52},{8,56},{12,60},{16,0},{20,4},{24,8},{28,12},{32,16},... | collective-permute-start | bytes 774152 | tf_op jit(solution)/shard_map/ppermute | solution.py:448
  124.2 8.7 %collective-permute-start.13 = (bf16[144,896]{1,0:T(8,128)(2,1)S(1)}, bf16[144,896]{1,0:T(8,128)(2,1)S(1)}, u32[]{:S(2)}, u32[]{:S(2)}) collective-permute-start(bf16[144,896]{1,0:T(8,128)(2,1)S(1)} %copy-done.19), channel_id=1, source_target_pairs={{0,16},{4,20},{8,24},{12,28},{16,32},{20,36},{24,40},{28,44},{32,4... | collective-permute-start | bytes 774152 | tf_op jit(solution)/shard_map/ppermute | solution.py:448
  131.8 8.6 %collective-permute-start.14 = (bf16[144,896]{1,0:T(8,128)(2,1)S(1)}, bf16[144,896]{1,0:T(8,128)(2,1)S(1)}, u32[]{:S(2)}, u32[]{:S(2)}) collective-permute-start(bf16[144,896]{1,0:T(8,128)(2,1)S(1)} %copy-done.17), channel_id=1, source_target_pairs={{0,32},{4,36},{8,40},{12,44},{16,48},{20,52},{24,56},{28,60},{32,0... | collective-permute-start | bytes 774152 | tf_op jit(solution)/shard_map/ppermute | solution.py:448
  142.0 13.0 %collective-permute-start.15 = (bf16[128,896]{1,0:T(8,128)(2,1)S(1)}, bf16[128,896]{1,0:T(8,128)(2,1)S(1)}, u32[]{:S(2)}, u32[]{:S(2)}) collective-permute-start(bf16[128,896]{1,0:T(8,128)(2,1)S(1)} %combine.2.refs_0_), channel_id=1, source_target_pairs={{0,1},{1,2},{2,3},{3,0},{4,5},{5,6},{6,7},{7,4},{8,9},{9,10},{10,1... | collective-permute-start | bytes 688136 | tf_op jit(solution)/shard_map/ppermute | solution.py:454
  142.4 12.6 %collective-permute-start.16 = (bf16[128,896]{1,0:T(8,128)(2,1)S(1)}, bf16[128,896]{1,0:T(8,128)(2,1)S(1)}, u32[]{:S(2)}, u32[]{:S(2)}) collective-permute-start(bf16[128,896]{1,0:T(8,128)(2,1)S(1)} %combine.2.refs_0_), channel_id=1, source_target_pairs={{0,3},{1,0},{2,1},{3,2},{4,7},{5,4},{6,5},{7,6},{8,11},{9,8},{10,9... | collective-permute-start | bytes 688136 | tf_op jit(solution)/shard_map/ppermute | solution.py:454
  144.8 10.2 %collective-permute-start.17 = (bf16[128,896]{1,0:T(8,128)(2,1)S(1)}, bf16[128,896]{1,0:T(8,128)(2,1)S(1)}, u32[]{:S(2)}, u32[]{:S(2)}) collective-permute-start(bf16[128,896]{1,0:T(8,128)(2,1)S(1)} %combine.2.refs_0_), channel_id=1, source_target_pairs={{0,2},{1,3},{2,0},{3,1},{4,6},{5,7},{6,4},{7,5},{8,10},{9,11},{10,... | collective-permute-start | bytes 688136 | tf_op jit(solution)/shard_map/ppermute | solution.py:454
  (26 other events, 93.7 us)
Sparse Core Ops, SparseCore 0:
  20.2 30.1 all-gather.3
  120.8 23.2 all-gather.5

commit v4 on v3

v4 whole, which is shorter than its diff:
```python
import functools

import jax
import jax.numpy as jnp
from jax import lax
from jax.experimental import pallas as pl
from jax.experimental.pallas import tpu as pltpu
from jax.sharding import PartitionSpec as P

HD = 128
PAGE = 128
BF = jnp.bfloat16
F32 = jnp.float32
NT = (((1,), (1,)), ((), ()))
VM = pl.BlockSpec(memory_space=pltpu.VMEM)
SM = pl.BlockSpec(memory_space=pltpu.SMEM)
HBM = pl.BlockSpec(memory_space=pltpu.HBM)
LITTLE = pl.CostEstimate(flops=1, bytes_accessed=1, transcendentals=0)


def pair_table(ra, rb, tab, cnt, reqs, spans):
    slots = ra.shape[1]
    for r in range(reqs):
        cnt[0, r] = spans

    def count(i, unused):
        for ref in (ra, rb):
            r = ref[0, i]
            cnt[0, r] = cnt[0, r] + 1
        return 0

    lax.fori_loop(0, slots, count, 0)
    total = jnp.int32(0)
    for r in range(reqs):
        tab[3, r] = total
        cnt[1, r] = 2 * total
        n = (cnt[0, r] + 1) // 2

        def owner(p, unused):
            tab[2, p] = r
            tab[1, 2 * p] = 0
            tab[1, 2 * p + 1] = 0
            tab[0, 2 * p] = 0
            tab[0, 2 * p + 1] = 0
            return 0

        lax.fori_loop(total, total + n, owner, 0)
        if spans:
            tab[1, 2 * total] = 200
            cnt[1, r] = 2 * total + 1
        total = total + n
    tab[3, reqs] = total

    def place(i, unused):
        for k, ref in enumerate((ra, rb)):
            r = ref[0, i]
            p = cnt[1, r]
            tab[0, p] = i + k * slots
            tab[1, p] = ref[1, i]
            cnt[1, r] = p + 1
        return 0

    lax.fori_loop(0, slots, place, 0)


def attn_kernel(ra, rb, *refs, first, r0, R, heads, nb):
    *refs, table, cnt = refs
    rows = heads * 128
    half = nb // 2
    if first:
        rel, q_all, ma, mb, num_out, qs_out, den, qv, qs, ks, vs, acc, dacc, p0, p1, sem = refs
    else:
        (bases, qs_in, ma, mb, mc, md, num_in, den_in, o0, o1, o2, o3,
         qs, ks, vs, acc, dacc, p0, p1, tile, stage, sem) = refs
    cs = []

    def copy(src, dst, i):
        c = pltpu.make_async_copy(src, dst, sem.at[i])
        c.start()
        return c

    if first:
        qc = [copy(q_all.at[rel[d]], qv.at[d], 4 + d) for d in range(4)]
        sets = (ma, mb)
    else:
        cs = [copy(qs_in.at[pl.ds(r0, R)], qs, 4), copy(num_in.at[pl.ds(r0, R)], acc, 5)]
        sets = (mc, md)
    for i, m in enumerate(sets):
        cs.append(copy(m.at[pl.ds(0, half)], ks.at[pl.ds(i * half, half)], 2 * i))
        cs.append(copy(m.at[pl.ds(half, half)], vs.at[pl.ds(i * half, half)], 2 * i + 1))
    if not first:
        for i, m in enumerate((ma, mb, mc, md)):
            for j, dst in enumerate((ks, vs)):
                for r in range(R):
                    at = nb + j * 2 + (r0 + r) // 4
                    c = pltpu.make_async_copy(
                        m.at[at, pl.ds((r0 + r) % 4 * 32, 32)],
                        dst.at[nb + r, pl.ds(i * 32, 32)],
                        sem.at[6 + (i * 2 + j) * R + r],
                    )
                    c.start()
                    cs.append(c)
    pair_table(ra, rb, table, cnt, R, 0 if first else 1)
    dacc[...] = jnp.zeros_like(dacc)
    p1[...] = jnp.zeros_like(p1)
    if first:
        acc[...] = jnp.zeros_like(acc)
        for c in qc:
            c.wait()
        for d in range(4):
            for r in range(R):
                for h in range(heads):
                    qs[r, pl.ds(h * 128 + d * 32, 32), :] = qv[d, r, :, pl.ds(h * 128, 128)]
        qs_copy = copy(qs, qs_out, 4)
    else:
        rowi = lax.broadcasted_iota(jnp.int32, (128, 128), 0)
        coli = lax.broadcasted_iota(jnp.int32, (128, 128), 1)

        def pick(i, b):
            g = i // 32
            base = jnp.where(
                g == 0, bases[b], jnp.where(g == 1, bases[b + 1], jnp.where(g == 2, bases[b + 2], bases[b + 3]))
            )
            return base + lax.rem(i, 32)

        tile[...] = jnp.where(pick(rowi, 0) >= pick(coli, 4), coli + 1, 0)
    for c in cs:
        c.wait()
    lane = lax.broadcasted_iota(jnp.int32, (1, 128), 1)
    begin, end = table[3, r0], table[3, r0 + R]

    def pair(p):
        ok = jnp.logical_and(p >= begin, p < end)
        i = jnp.where(ok, 2 * p, 0)
        r = jnp.where(ok, table[2, jnp.where(ok, p, 0)] - r0, 0)
        slots = table[0, i], table[0, i + 1]
        lims = jnp.where(ok, table[1, i], 0), jnp.where(ok, table[1, i + 1], 0)
        return r, slots, lims

    def scores(p, dst):
        r, slots, lims = pair(p)
        if not first:
            slots = [jnp.where(l == 200, nb + r, s) for s, l in zip(slots, lims)]
        K = jnp.concatenate([ks[slots[0]], ks[slots[1]]], axis=0)
        s = lax.dot_general(qs[r], K, NT, preferred_element_type=F32)
        w = jnp.exp(s * HD ** -0.5)
        t = None
        for j in range(2):
            limit = lims[j]
            if first or j:
                keep = (lane < limit)[None]
            else:
                keep = (lane < jnp.where(limit == 200, tile[...], limit))[None]
            one = w[:, j * 128 : (j + 1) * 128].reshape(heads, 128, 128)
            one = jnp.where(keep, one, 0.0).reshape(rows, 128)
            dst[:, j * 128 : (j + 1) * 128] = one.astype(BF)
            t = one if t is None else t + one
        dacc[r] += t

    def products(p, src):
        r, slots, lims = pair(p)
        if not first:
            slots = [jnp.where(l == 200, nb + r, s) for s, l in zip(slots, lims)]
        V = jnp.concatenate([vs[slots[0]], vs[slots[1]]], axis=0)
        acc[r] += jnp.dot(src[...], V, preferred_element_type=F32)

    def step(i, unused):
        p = begin + 2 * i
        products(p - 1, p1)
        scores(p, p0)
        products(p, p0)
        scores(p + 1, p1)
        return 0

    steps = (end - begin + 1) // 2
    lax.fori_loop(0, steps, step, 0)
    products(begin + 2 * steps - 1, p1)

    lane1 = lax.broadcasted_iota(jnp.int32, (128, 128), 1)
    dl = jnp.zeros((128, 128), F32) if first else den_in[...]
    if first:
        num_copy = copy(acc, num_out, 0)
    for r in range(R):
        for h in range(heads):
            col = jnp.sum(dacc[r, pl.ds(h * 128, 128), :], axis=1, keepdims=True)
            dl = dl + jnp.where(lane1 == (r0 + r) * 16 + h, col, 0.0)
    if first:
        den[...] = dl
        num_copy.wait()
        qs_copy.wait()
        return
    outs = [stage.at[d] for d in range(4)]
    for r in range(R):
        for h in range(heads):
            for d in range(4):
                outs[d][r * 32 : r * 32 + 32, h * 128 : h * 128 + 128] = acc[
                    r, h * 128 + d * 32 : h * 128 + d * 32 + 32, :
                ].astype(BF)
    hi = dl.astype(BF)
    lo = (dl - hi.astype(F32)).astype(BF)
    z = jnp.zeros((16, (heads - 4) * 128), BF)
    for d in range(4):
        for k, a in enumerate((hi, lo)):
            outs[d][R * 32 : R * 32 + 16, k * 256 : k * 256 + 128] = a[d * 32 : d * 32 + 16]
            outs[d][R * 32 : R * 32 + 16, k * 256 + 128 : k * 256 + 256] = a[d * 32 + 16 : d * 32 + 32]
        outs[d][R * 32 : R * 32 + 16, 512:] = z
    for c in [copy(stage.at[d], o, d) for d, o in enumerate((o0, o1, o2, o3))]:
        c.wait()


def attn_near(ra, rb, rel, qs, sets, slots):
    R, T, W = qs.shape[1:]
    heads = W // HD
    rows = heads * 128
    nb = 2 * slots
    body = functools.partial(attn_kernel, first=True, r0=0, R=R, heads=heads, nb=nb)
    return pl.pallas_call(
        body,
        in_specs=[SM] * 3 + [HBM] * 3,
        out_specs=[HBM, HBM, VM],
        scratch_shapes=[
            pltpu.VMEM((4, R, T, W), BF),
            pltpu.VMEM((R, rows, 128), BF),
            pltpu.VMEM((nb, 128, 128), BF),
            pltpu.VMEM((nb, 128, 128), BF),
            pltpu.VMEM((R, rows, 128), F32),
            pltpu.VMEM((R, rows, 128), F32),
            pltpu.VMEM((rows, 256), BF),
            pltpu.VMEM((rows, 256), BF),
            pltpu.SemaphoreType.DMA((11,)),
            pltpu.SMEM((4, 80), jnp.int32),
            pltpu.SMEM((2, 16), jnp.int32),
        ],
        out_shape=[
            jax.ShapeDtypeStruct((R, rows, 128), F32),
            jax.ShapeDtypeStruct((R, rows, 128), BF),
            jax.ShapeDtypeStruct((128, 128), F32),
        ],
        compiler_params=pltpu.CompilerParams(vmem_limit_bytes=60 << 20),
        cost_estimate=LITTLE,
        name="attn_near",
    )(ra, rb, rel, qs, *sets)


def attn_far(ra, rb, bases, r0, R, qs, sets, slots, num, den, T, W):
    heads = W // HD
    rows = heads * 128
    nb = 2 * slots
    body = functools.partial(attn_kernel, first=False, r0=r0, R=R, heads=heads, nb=nb)
    return pl.pallas_call(
        body,
        in_specs=[SM] * 3 + [HBM] * 6 + [VM],
        out_specs=[HBM] * 4,
        scratch_shapes=[
            pltpu.VMEM((R, rows, 128), BF),
            pltpu.VMEM((nb + R, 128, 128), BF),
            pltpu.VMEM((nb + R, 128, 128), BF),
            pltpu.VMEM((R, rows, 128), F32),
            pltpu.VMEM((R, rows, 128), F32),
            pltpu.VMEM((rows, 256), BF),
            pltpu.VMEM((rows, 256), BF),
            pltpu.VMEM((128, 128), jnp.int32),
            pltpu.VMEM((4, R * T + 16, W), BF),
            pltpu.SemaphoreType.DMA((6 + 8 * R,)),
            pltpu.SMEM((4, 80), jnp.int32),
            pltpu.SMEM((2, 16), jnp.int32),
        ],
        out_shape=[jax.ShapeDtypeStruct((R * T + 16, W), BF)] * 4,
        compiler_params=pltpu.CompilerParams(vmem_limit_bytes=60 << 20),
        cost_estimate=LITTLE,
        name="attn_far",
    )(ra, rb, bases, qs, *sets, num, den)


def decode_kernel(req, lim, ctx, notes, k_hbm, v_hbm, hand, dk, dv, out, k, v, p, d, o, acc, dacc, sem):
    k_copy = pltpu.make_async_copy(k_hbm, k, sem.at[0])
    v_copy = pltpu.make_async_copy(v_hbm, v, sem.at[1])
    k_copy.start()
    v_copy.start()
    scale = HD ** -0.5
    blocks = k.shape[0]
    handed = hand.shape[1]
    lane = lax.broadcasted_iota(jnp.int32, (1, 128), 1)

    def queries(r):
        return notes[r // 2, pl.ds(pl.multiple_of(r % 2 * 32, 32), 32), :]

    def first_lane(w):
        return jnp.where(lane == 0, jnp.sum(w, axis=1, keepdims=True), 0.0)

    for r in range(handed):
        s = lax.dot_general(queries(r), hand[0, r], NT, preferred_element_type=F32)
        w = jnp.exp(s * scale)
        dacc[r] = first_lane(w)
        acc[r] = jnp.dot(w.astype(BF), hand[1, r], preferred_element_type=F32)
    dacc[handed:] = jnp.zeros_like(dacc[handed:])
    acc[handed:] = jnp.zeros_like(acc[handed:])
    k_copy.wait()
    for i in range(blocks):
        s = lax.dot_general(queries(req[i]), k[i], NT, preferred_element_type=F32)
        w = jnp.where(lane < lim[i], jnp.exp(s * scale), 0.0)
        d[i] = w
        p[i] = w.astype(BF)
    v_copy.wait()
    for i in range(blocks):
        o[i] = jnp.dot(p[i], v[i], preferred_element_type=F32)
    steps = 4
    for j in range(dk.shape[0]):
        r = ctx[0] * dk.shape[0] + j
        s = lax.dot_general(queries(r), dk[j], NT, preferred_element_type=F32)
        row = lax.rem(lax.broadcasted_iota(jnp.int32, s.shape, 0), steps)
        col = lax.broadcasted_iota(jnp.int32, s.shape, 1)
        w = jnp.where(col <= row, jnp.exp(s * scale), 0.0)
        dacc[r] += first_lane(w)
        acc[r] += jnp.dot(w.astype(BF), dv[j], preferred_element_type=F32)
    for i in range(blocks):
        r = req[i]
        acc[r] += o[i]
        dacc[r] += d[i]
    out[:, :, 0:128] = acc[...].astype(BF)
    den = jnp.sum(dacc[...], axis=2, keepdims=True)
    hi = den.astype(BF)
    lo = (den - hi.astype(F32)).astype(BF)
    out[:, :, 128:256] = jnp.where(lane[None] < 64, hi, lo)


def decode(req, lim, ctx, notes, k, v, hand, dk, dv):
    blocks = k.shape[0]
    total = 2 * notes.shape[0]
    return pl.pallas_call(
        decode_kernel,
        in_specs=[SM] * 3 + [VM] + [HBM] * 2 + [VM] * 3,
        out_specs=VM,
        scratch_shapes=[
            pltpu.VMEM(k.shape, BF),
            pltpu.VMEM(v.shape, BF),
            pltpu.VMEM((blocks, 32, 128), BF),
            pltpu.VMEM((blocks, 32, 128), F32),
            pltpu.VMEM((blocks, 32, 128), F32),
            pltpu.VMEM((total, 32, 128), F32),
            pltpu.VMEM((total, 32, 128), F32),
            pltpu.SemaphoreType.DMA((2,)),
        ],
        out_shape=jax.ShapeDtypeStruct((total, 32, 256), BF),
        compiler_params=pltpu.CompilerParams(vmem_limit_bytes=60 << 20),
        cost_estimate=LITTLE,
        name="decode_terms",
    )(req, lim, ctx, notes, k, v, hand, dk, dv)


def combine_kernel(*refs, decode_rows):
    if decode_rows:
        h0, h1, h2, h3, h4, out, parts, small, dec, sem = refs
    else:
        h0, h1, h2, h3, out, parts, sem = refs
    copies = [pltpu.make_async_copy(h, parts.at[i], sem.at[i]) for i, h in enumerate((h0, h1, h2, h3))]
    if decode_rows:
        copies.append(pltpu.make_async_copy(h4, dec, sem.at[4]))
    for c in copies:
        c.start()
    rows = parts.shape[1] - 16
    heads = parts.shape[2] // HD
    if out.shape[0] > rows and not decode_rows:
        out[rows:] = jnp.zeros((out.shape[0] - rows, out.shape[1]), BF)
    for c in copies:
        c.wait()
    if decode_rows:
        sums = jnp.sum(dec[...].astype(F32), axis=0)
        reqs = sums.shape[0]
        dden = sums[:, :, 128:129] + sums[:, :, 192:193]
        att = sums[:, :, :128] / dden
        small[...] = jnp.zeros_like(small)
        for j in range(reqs):
            for h in range(heads):
                small[j * 4 : j * 4 + 4, h * 128 : h * 128 + 128] = att[j, h * 4 : h * 4 + 4]
        out[rows : rows + small.shape[0]] = small[...].astype(BF)

    def total(*at):
        t = parts[(0,) + at].astype(F32)
        for i in range(1, 4):
            t = t + parts[(i,) + at].astype(F32)
        return t

    tail = total(pl.ds(rows, 16), pl.ds(0, 512))
    tail = tail[:, :256] + tail[:, 256:]
    inv = 1.0 / jnp.concatenate([tail[:, :128], tail[:, 128:]], axis=0)
    for r in range(rows // 32):
        for h in range(heads):
            at = (pl.ds(r * 32, 32), pl.ds(h * 128, 128))
            out[at] = (total(*at) * inv[:, r * 16 + h : r * 16 + h + 1]).astype(BF)


def combine(os, dec=None, pad_rows=0):
    rows, width = os[0].shape
    more = [] if dec is None else [dec]
    out_rows = rows if more else rows - 16 + pad_rows
    return pl.pallas_call(
        functools.partial(combine_kernel, decode_rows=len(more)),
        in_specs=[HBM] * (4 + len(more)),
        out_specs=VM,
        scratch_shapes=[pltpu.VMEM((4, rows, width), BF)]
        + ([pltpu.VMEM((16, width), F32), pltpu.VMEM(dec.shape, BF)] if more else [])
        + [pltpu.SemaphoreType.DMA((5,))],
        out_shape=jax.ShapeDtypeStruct((out_rows, width), BF),
        compiler_params=pltpu.CompilerParams(vmem_limit_bytes=60 << 20),
        cost_estimate=pl.CostEstimate(flops=10**6, bytes_accessed=2_500_000, transcendentals=0),
        name="combine",
    )(*os, *more)


def first_kernel(at, x0, x2, w, a2, b2, y, ws, sem):
    depth, half = w.shape[0], ws.shape[2]
    copies = []
    for t, got in enumerate((a2, b2)):
        col = pl.multiple_of(at[t] * half, half)
        for d, part in enumerate((w.at[:, pl.ds(col, half)], got)):
            copies.append(pltpu.make_async_copy(part, ws.at[t, pl.ds(d * depth, depth)], sem.at[t * 2 + d]))
            copies[-1].start()
    x = jnp.concatenate([x0[...], x2[...]], axis=1)
    for t in range(2):
        copies[t * 2].wait()
        copies[t * 2 + 1].wait()
        y[t] = jnp.dot(x, ws[t], preferred_element_type=F32)


def project_first(at, x0, x2, w, a2, b2):
    rows, depth = x0.shape
    half = a2.shape[1]
    return pl.pallas_call(
        first_kernel,
        in_specs=[SM, VM, VM] + [HBM] * 3,
        out_specs=VM,
        out_shape=jax.ShapeDtypeStruct((2, rows, half), F32),
        scratch_shapes=[pltpu.VMEM((2, 2 * depth, half), BF), pltpu.SemaphoreType.DMA((4,))],
        compiler_params=pltpu.CompilerParams(vmem_limit_bytes=60 << 20),
        cost_estimate=LITTLE,
        name="project_first",
    )(at, x0, x2, w, a2, b2)


def project_kernel(at, y0, x1, x3, a1, a3, b1, b3, out, small, ws, y, stage, sem):
    half = stage.shape[2]
    depth = x1.shape[1]
    rows = stage.shape[1]
    copies = []
    for t, parts in enumerate(((a1, a3), (b1, b3))):
        for d, part in enumerate(parts):
            c = pltpu.make_async_copy(part, ws.at[t, pl.ds(d * depth, depth)], sem.at[t * 2 + d])
            c.start()
            copies.append(c)
    y_copy = pltpu.make_async_copy(y0, y, sem.at[6])
    y_copy.start()
    x = jnp.concatenate([x1[...], x3[...]], axis=1)
    outs = []
    for t in range(2):
        side = at[2] if t == 0 else 1 - at[2]
        cols = pl.ds(pl.multiple_of(side * half, half), half)
        copies[t * 2].wait()
        copies[t * 2 + 1].wait()
        total = jnp.dot(x, ws[t], preferred_element_type=F32)
        if t == 0:
            y_copy.wait()
        total = total + y[t]
        stage[t] = total[:rows].astype(BF)
        small[:, cols] = total[rows:].astype(BF)
        c = pltpu.make_async_copy(stage.at[t], out.at[:, cols], sem.at[4 + t])
        c.start()
        outs.append(c)
    for c in outs:
        c.wait()


def project(at, y0, xs, mine, theirs):
    rows, depth = xs[0].shape
    half = mine[0].shape[1]
    rows = rows - 16
    return pl.pallas_call(
        project_kernel,
        in_specs=[SM, HBM] + [VM] * 2 + [HBM] * 4,
        out_specs=[HBM, VM],
        out_shape=[jax.ShapeDtypeStruct((rows, 2 * half), BF), jax.ShapeDtypeStruct((16, 2 * half), BF)],
        scratch_shapes=[
            pltpu.VMEM((2, 2 * depth, half), BF),
            pltpu.VMEM((2, rows + 16, half), F32),
            pltpu.VMEM((2, rows, half), BF),
            pltpu.SemaphoreType.DMA((7,)),
        ],
        compiler_params=pltpu.CompilerParams(vmem_limit_bytes=60 << 20),
        cost_estimate=LITTLE,
        name="project",
    )(at, y0, *xs, *mine, *theirs)


def visible_tokens(req, blk, bounds):
    count = bounds.shape[0]
    hit = req[:, None] == jnp.arange(count, dtype=jnp.int32)[None, :]
    bound = jnp.sum(jnp.where(hit, bounds[None, :], 0), axis=1)
    return jnp.clip(bound - blk * PAGE, 0, PAGE)


def on_device(
    p_query, p_key, p_value, p_cache_k, p_cache_v, p_slot_req, p_slot_blk, p_offsets,
    d_query, d_key, d_value, d_cache_k, d_cache_v, d_slot_req, d_slot_blk, d_lengths, out_weight,
):
    me = lax.axis_index("ctx")
    column = lax.axis_index("tp")
    core = me % 2
    ctx = lax.axis_size("ctx")
    tp = lax.axis_size("tp")

    def along_y(x, d):
        return lax.ppermute(x, "ctx", [(i, i ^ 4 * d) for i in range(ctx)])

    def across(x, bit):
        return lax.ppermute(x, "ctx", [(i, i ^ bit) for i in range(ctx)])

    def along_x(x, d):
        return lax.ppermute(x, "tp", [(i, (i + d) % tp) for i in range(tp)])

    heads = p_query.shape[3] // HD
    reqs, span_len = p_query.shape[1:3]
    slots = p_slot_req.shape[1]
    steps = d_query.shape[2]
    width = heads * HD

    dq = d_query[0].reshape(2, steps, heads, HD).transpose(0, 2, 1, 3).reshape(2, steps * heads, HD)
    dq = jnp.pad(dq, ((0, 0), (0, 32 - steps * heads), (0, 0))).reshape(64, HD)
    dq = jnp.broadcast_to(dq[None], (ctx,) + dq.shape)
    dq, p_key, p_value = lax.optimization_barrier((dq, p_key, p_value))
    notes = lax.all_to_all(dq, "ctx", 0, 0)
    span = jnp.concatenate([p_key[0].reshape(-1, HD), p_value[0].reshape(-1, HD)], axis=0)
    handed = lax.ppermute(span, "sec", [(0, 1), (1, 0)])

    lim0 = visible_tokens(p_slot_req[0], p_slot_blk[0], p_offsets[0])
    note = jnp.pad(jnp.stack([p_slot_req[0], lim0]), ((0, 14), (0, HD - slots))).astype(BF)
    m0 = jnp.concatenate(
        [
            p_cache_k[0].reshape(-1, HD),
            p_cache_v[0].reshape(-1, HD),
            p_key[0].reshape(-1, HD),
            p_value[0].reshape(-1, HD),
            jnp.pad(note, ((0, PAGE - 16), (0, 0))),
        ],
        axis=0,
    ).reshape(-1, PAGE, HD)
    half = out_weight.shape[1] // (2 * tp)
    block = lambda d: lax.dynamic_slice(
        out_weight, (0, (((column + d) % tp) * 2 + core) * half), (out_weight.shape[0], half)
    )
    queries = jnp.broadcast_to(p_query, (ctx // 4,) + p_query.shape[1:])
    m0, queries, notes, handed, a1, a3, a2 = lax.optimization_barrier(
        (m0, queries, notes, handed, block(1), block(3), block(2))
    )
    rings = [[z + 4 * y for y in range(ctx // 4)] for z in range(4)]
    qs = lax.all_to_all(queries, "ctx", 0, 0, axis_index_groups=rings)
    m2 = across(m0, 2)
    m1 = across(m0, 1)
    a1, a3 = along_x(a1, 1), along_x(a3, -1)

    def rows_of(m):
        return m[-1, :2, :slots].astype(jnp.int32)

    rel = jnp.arange(4, dtype=jnp.int32)
    bases = jnp.concatenate([me ^ 4 * rel, me ^ rel]).astype(jnp.int32) * span_len

    pad = ((0, 0), (0, 16 - steps), (0, 0))
    dec = decode(
        d_slot_req[0],
        visible_tokens(d_slot_req[0], d_slot_blk[0], d_lengths[0]),
        me.reshape(1),
        notes,
        d_cache_k[0],
        d_cache_v[0],
        handed.reshape(2, reqs, span_len, HD),
        jnp.pad(d_key[0], pad),
        jnp.pad(d_value[0], pad),
    )
    dec, qs = lax.optimization_barrier((dec, qs))
    dec = lax.all_to_all(dec.reshape(ctx, 2, 32, 256), "ctx", 0, 0)
    num, queries, den = attn_near(rows_of(m0), rows_of(m1), (me // 4) ^ rel, qs, (m0, m1), slots)
    m2, num, queries, den, a1, a3, a2 = lax.optimization_barrier((m2, num, queries, den, a1, a3, a2))
    m3 = across(m2, 1)
    a2 = along_x(a2, 2)
    sets = (m0, m1, m2, m3)
    os = attn_far(rows_of(m2), rows_of(m3), bases, 0, reqs, queries, sets, slots, num, den, span_len, width)
    os, a1, dec = lax.optimization_barrier((os, a1, dec))
    b1 = across(a1, 1)
    x = combine([os[0]] + [along_y(os[d], d) for d in (1, 2, 3)], dec)
    x, b1, a3, a2 = lax.optimization_barrier((x, b1, a3, a2))
    xs = [x, along_x(x, 1), along_x(x, -1), along_x(x, 2)]
    b3, b2 = across(a3, 1), across(a2, 1)
    at = jnp.stack([column * 2 + core, column * 2 + 1 - core, core]).astype(jnp.int32)
    y0 = project_first(at, x, xs[3], out_weight, a2, b2)
    out, small = project(at, y0, xs[1:3], (a1, a3), (b1, b3))
    out_cols = 2 * half
    return out.reshape(1, reqs, span_len, out_cols), small[: 2 * steps].reshape(1, 2, steps, out_cols)


def solution(mesh):
    placed = (
        P("sec", None, "ctx", "tp"),
        P("sec", None, "ctx", "tp"),
        P("sec", None, "ctx", "tp"),
        P("sec", "ctx", None, "tp"),
        P("sec", "ctx", None, "tp"),
        P("sec", "ctx"),
        P("sec", "ctx"),
        P("sec", None),
        P("sec", "ctx", None, "tp"),
        P("sec", "ctx", None, "tp"),
        P("sec", "ctx", None, "tp"),
        P("sec", "ctx", None, "tp"),
        P("sec", "ctx", None, "tp"),
        P("sec", "ctx"),
        P("sec", "ctx"),
        P("sec", None),
        P("tp", None),
    )
    return jax.shard_map(
        on_device,
        mesh=mesh,
        in_specs=placed,
        out_specs=(P("sec", None, "ctx", "tp"), P("sec", "ctx", None, "tp")),
        check_vma=False,
    )
```

time: 170 us -> 167 us (0.982)
  waiting for transfers between devices: 31.4 us -> 53.2 us
  between operations: 14.6 us -> 1.06 us
  local copies, waits for them, and re-layouts: 22.1 us -> 15 us
  Pallas kernels: 58.2 us -> 55.2 us
    all_gather x2 -> x0, waiting for transfers between devices: 17.2 us -> none  [the longest x1 17.2 us: on_device(): qs = lax.all_gather(p_query, 'ctx', axis_index_groups=rings, tiled=True)]
    all_to_all x1 -> x2, waiting for transfers between devices: 0.01 us -> 15.3 us  [the longest x1 15.3 us: on_device(): qs = lax.all_to_all(queries, 'ctx', 0, 0, axis_index_groups=rings)]
    ppermute x6, waiting for transfers between devices: 0.02 us -> 13.9 us  [along_x(): return lax.ppermute(x, 'tp', [(i, (i + d) % tp) for i in range(tp)])]
    ppermute x7 -> x4, waiting for transfers between devices: 14.2 us -> 23.9 us  [the longest x3 23.9 us: along_y(): return lax.ppermute(x, 'ctx', [(i, i ^ 4 * d) for i in range(ctx)])]
    unnamed x65 -> x53, local copies, waits for them, and re-layouts: 13.8 us -> 4.53 us
    all_to_all x1 -> x2, starting transfers between devices: 4.6 us -> 11.8 us  [the longest x1 7.34 us: on_device(): notes = lax.all_to_all(dq, 'ctx', 0, 0)]
    ppermute x9 -> x6, starting transfers between devices: 9.05 us -> 5.51 us  [across(): return lax.ppermute(x, 'ctx', [(i, i ^ bit) for i in range(ctx)])]
    convert_element_type x0 -> x4, other arithmetic: none -> 3.04 us  [rows_of(): return m[-1, :2, :slots].astype(jnp.int32)]
  transfers between devices with their start and end apart: 26 -> 19, of which waited for: 4 -> 7; matrix products, arithmetic and copies ran while one was open for 4% -> 8% of each run, Pallas kernels for 31% -> 28%
where the time goes in v4:
time: 167 us; the launch traced here: 166 us
  Pallas kernels  55.2 us (33%)
  waiting for transfers between devices  53.2 us (32%)
  starting transfers between devices  35.4 us (21%)
  local copies, waits for them, and re-layouts  15 us (9%)
  other arithmetic  6.52 us (4%)
    ppermute x3, waiting for transfers between devices, along_y(): return lax.ppermute(x, 'ctx', [(i, i ^ 4 * d) for i in range(ctx)])  23.9 us
    pallas_call x1, Pallas kernels, attn_far(): pl.pallas_call(body, in_specs=[SM] * 3 + [HBM] * 6 + [VM], out_specs=[HBM...  17.5 us
    all_to_all x1, waiting for transfers between devices, on_device(): qs = lax.all_to_all(queries, 'ctx', 0, 0, axis_index_groups=rings)  15.3 us
    pallas_call x1, Pallas kernels, attn_near(): pl.pallas_call(body, in_specs=[SM] * 3 + [HBM] * 3, out_specs=[HBM, HBM,...  15.3 us
    ppermute x6, waiting for transfers between devices, along_x(): return lax.ppermute(x, 'tp', [(i, (i + d) % tp) for i in range(tp)])  13.9 us
    pallas_call x1, Pallas kernels, project(): pl.pallas_call(project_kernel, in_specs=[SM, HBM] + [VM] * 2 + [HBM] * 4,...  8.44 us
    all_to_all x1, starting transfers between devices, on_device(): notes = lax.all_to_all(dq, 'ctx', 0, 0)  7.34 us
    ppermute x6, starting transfers between devices, along_x(): return lax.ppermute(x, 'tp', [(i, (i + d) % tp) for i in range(tp)])  7.14 us
  transfers between devices with their start and end apart: 19, of which 7 were waited for; matrix products, arithmetic and copies ran while one was open for 8% of the time, Pallas kernels for 28%

profile of v4, /device:TPU:1, one launch (start us, length us, event | category | flops | bytes accessed | tf_op | source)
XLA Modules:
  0.0 166.3 jit_solution(12824060889066413028)
XLA Ops:
  2.2 7.3 %all-to-all-start = ((bf16[16,64,128]{2,1,0:T(8,128)(2,1)}), bf16[16,64,128]{2,1,0:T(8,128)(2,1)S(1)}, u32[]{:S(2)}, u32[]{:S(2)}) async-start(bf16[16,64,128]{2,1,0:T(8,128)(2,1)} %broadcast_in_dim.45), calls=%async_computation | async-start | bytes 524288 | tf_op jit(solution)/shard_map/all_to_all | solution.py:530
  9.6 0.9 pad_maximum_fusion
  10.5 3.4 %collective-permute-start = (bf16[512,128]{1,0:T(8,128)(2,1)S(1)}, bf16[512,128]{1,0:T(8,128)(2,1)S(1)}, u32[]{:S(2)}, u32[]{:S(2)}) collective-permute-start(bf16[512,128]{1,0:T(8,128)(2,1)S(1)} %pad_maximum_fusion), channel_id=1, source_target_pairs={{0,64},{64,0},{1,65},{65,1},{2,66},{66,2},{3,67},{67,3},{4,68},{68... | collective-permute-start | bytes 393224 | tf_op jit(solution)/shard_map/ppermute | solution.py:532
  14.0 1.1 copy-done.8
  15.4 4.7 %constant_dynamic-slice_fusion = (bf16[896,896]{1,0:T(8,128)(2,1)}, bf16[896,896]{1,0:T(8,128)(2,1)}, bf16[896,896]{1,0:T(8,128)(2,1)}) fusion(bf16[896,7168]{1,0:T(8,128)(2,1)} %w.1, s32[]{:T(128)S(6)} %select_n.47, s32[]{:T(128)S(6)} %select_n.45, s32[]{:T(128)S(6)} %select_n.43), kind=kLoop, calls=%fused_computation.18 | loop fusion | bytes 9633804 | tf_op jit(solution)/shard_map/dynamic_slice | solution.py:547
  20.2 1.6 broadcast_in_dim.50
  22.3 1.1 collective-permute-start.1
  23.3 1.2 collective-permute-start.3
  24.6 1.5 collective-permute-start.4
  26.0 4.4 %all-to-all-start.1 = ((bf16[4,8,32,896]{3,2,1,0:T(8,128)(2,1)}), bf16[4,8,32,896]{3,2,1,0:T(8,128)(2,1)}, u32[]{:S(2)}, u32[]{:S(2)}) async-start(bf16[4,8,32,896]{3,2,1,0:T(8,128)(2,1)} %broadcast_in_dim.50), calls=%async_computation.1 | async-start | bytes 3670016 | tf_op jit(solution)/shard_map/all_to_all | solution.py:555
  32.9 4.3 %decode_terms.1 = bf16[32,32,256]{2,1,0:T(8,128)(2,1)} custom-call(s32[24]{0:T(128)} %bitcast.71, s32[24]{0:T(128)} %fusion.8.lim, s32[1]{0:T(128)} %bitcast.20.ctx, bf16[16,64,128]{2,1,0:T(8,128)(2,1)} %copy-done.6, bf16[24,128,128]{2,1,0:T(8,128)(2,1)} %bitcast.56, bf16[24,128,128]{2,1,0:T(8,128)(2,1)} %bitcast.57, bf16[2,8,32,128]{3,2,1,0:T(8,128)(2,1)} %bitcast.65, ...), custom_call_target="tpu_custom_call" | custom-call | flops 1 | bytes 1 | tf_op jit(solution)/shard_map/decode_terms/pallas_call | solution.py:330
  37.8 15.3 %all-to-all-done.1.refs_1_ = bf16[4,8,32,896]{3,2,1,0:T(8,128)(2,1)} async-done(((bf16[4,8,32,896]{3,2,1,0:T(8,128)(2,1)}), bf16[4,8,32,896]{3,2,1,0:T(8,128)(2,1)}, u32[]{:S(2)}, u32[]{:S(2)}) %all-to-all-start.1) | async-done | bytes 1835040 | tf_op jit(solution)/shard_map/all_to_all | solution.py:555
  54.4 15.3 %attn_near.1 = (f32[8,896,128]{2,1,0:T(8,128)}, bf16[8,896,128]{2,1,0:T(8,128)(2,1)}, f32[128,128]{1,0:T(8,128)}) custom-call(s32[2,24]{1,0:T(2,128)} %bitcast_convert_fusion.1.ra, s32[2,24]{1,0:T(2,128)} %fusion.7.rb, s32[4]{0:T(128)} %iota_xor_fusion.1.refs_0_, bf16[4,8,32,896]{3,2,1,0:T(8,128)(2,1)} %all-to-all-done.1.refs_1_, ...), custom_call_target="tpu_custom_call" | custom-call | flops 1 | bytes 1 | tf_op jit(solution)/shard_map/attn_near/pallas_call | solution.py:217
  69.7 1.9 %collective-permute-start.5 = (bf16[53,128,128]{2,1,0:T(8,128)(2,1)}, bf16[53,128,128]{2,1,0:T(8,128)(2,1)S(1)}, u32[]{:S(2)}, u32[]{:S(2)}) collective-permute-start(bf16[53,128,128]{2,1,0:T(8,128)(2,1)} %collective-permute-done.1.refs_4_), channel_id=1, source_target_pairs={{0,4},{4,0},{8,12},{12,8},{16,20},{20,16},{24,28},{28,24},{32,36},... | collective-permute-start | bytes 5210120 | tf_op jit(solution)/shard_map/ppermute | solution.py:515
  71.6 3.6 %all-to-all-start.2 = ((bf16[16,2,32,256]{3,2,1,0:T(8,128)(2,1)}), bf16[16,2,32,256]{3,2,1,0:T(8,128)(2,1)S(1)}, u32[]{:S(2)}, u32[]{:S(2)}) async-start(bf16[16,2,32,256]{3,2,1,0:T(8,128)(2,1)} %bitcast.55), calls=%async_computation.2 | async-start | bytes 1048576 | tf_op jit(solution)/shard_map/all_to_all | solution.py:579
  75.8 1.6 collective-permute-start.10
  77.4 1.2 bitcast_convert_fusion.ra
  79.9 17.5 %attn_far.1 = (bf16[272,896]{1,0:T(8,128)(2,1)}, bf16[272,896]{1,0:T(8,128)(2,1)}, bf16[272,896]{1,0:T(8,128)(2,1)}, bf16[272,896]{1,0:T(8,128)(2,1)}) custom-call(s32[2,24]{1,0:T(2,128)} %bitcast_convert_fusion.ra, s32[2,24]{1,0:T(2,128)} %fusion.6.rb, s32[8]{0:T(128)} %add_multiply_fusion.refs_0_, bf16[8,896,128]{2,1,0:T(8,128)(2,1)} %get-tuple-element.55.refs_1_, ...), custom_call_target="tpu_custom_call" | custom-call | flops 1 | bytes 1 | tf_op jit(solution)/shard_map/attn_far/pallas_call | solution.py:250
  97.8 1.7 collective-permute-start.6
  99.5 2.4 %collective-permute-start.7 = (bf16[272,896]{1,0:T(8,128)(2,1)}, bf16[272,896]{1,0:T(8,128)(2,1)S(1)}, u32[]{:S(2)}, u32[]{:S(2)}) collective-permute-start(bf16[272,896]{1,0:T(8,128)(2,1)} %get-tuple-element.66), channel_id=1, source_target_pairs={{0,32},{4,36},{8,40},{12,44},{16,48},{20,52},{24,56},{28,60},{32,0... | collective-permute-start | bytes 1462280 | tf_op jit(solution)/shard_map/ppermute | solution.py:512
  101.9 9.2 %collective-permute-done.6.refs_1_ = bf16[272,896]{1,0:T(8,128)(2,1)S(1)} collective-permute-done((bf16[272,896]{1,0:T(8,128)(2,1)}, bf16[272,896]{1,0:T(8,128)(2,1)S(1)}, u32[]{:S(2)}, u32[]{:S(2)}) %collective-permute-start.6) | collective-permute-done | bytes 487456 | tf_op jit(solution)/shard_map/ppermute | solution.py:512
  111.1 12.7 %collective-permute-done.7.refs_2_ = bf16[272,896]{1,0:T(8,128)(2,1)S(1)} collective-permute-done((bf16[272,896]{1,0:T(8,128)(2,1)}, bf16[272,896]{1,0:T(8,128)(2,1)S(1)}, u32[]{:S(2)}, u32[]{:S(2)}) %collective-permute-start.7) | collective-permute-done | bytes 487456 | tf_op jit(solution)/shard_map/ppermute | solution.py:512
  123.8 2.0 %collective-permute-done.8.refs_3_ = bf16[272,896]{1,0:T(8,128)(2,1)S(1)} collective-permute-done((bf16[272,896]{1,0:T(8,128)(2,1)}, bf16[272,896]{1,0:T(8,128)(2,1)S(1)}, u32[]{:S(2)}, u32[]{:S(2)}) %collective-permute-start.8) | collective-permute-done | bytes 487456 | tf_op jit(solution)/shard_map/ppermute | solution.py:512
  126.6 2.9 %combine.1.x0 = bf16[272,896]{1,0:T(8,128)(2,1)} custom-call(bf16[272,896]{1,0:T(8,128)(2,1)} %get-tuple-element.64.refs_0_, bf16[272,896]{1,0:T(8,128)(2,1)} %copy-done.9, bf16[272,896]{1,0:T(8,128)(2,1)} %copy-done.10, bf16[272,896]{1,0:T(8,128)(2,1)} %copy-done.11, bf16[16,2,32,256]{3,2,1,0:T(8,128)(2,1)} %copy-done.2), custom_call_target="tpu_custom_call" | custom-call | flops 1000000 | bytes 2500000 | tf_op jit(solution)/shard_map/combine/pallas_call | solution.py:397
  129.5 1.6 collective-permute-start.12
  131.2 1.4 collective-permute-start.11
  132.6 1.3 collective-permute-start.14
  134.6 10.7 %collective-permute-done.11.x2 = bf16[272,896]{1,0:T(8,128)(2,1)} collective-permute-done((bf16[272,896]{1,0:T(8,128)(2,1)}, bf16[272,896]{1,0:T(8,128)(2,1)}, u32[]{:S(2)}, u32[]{:S(2)}) %collective-permute-start.11) | collective-permute-done | bytes 487456 | tf_op jit(solution)/shard_map/ppermute | solution.py:518
  145.4 1.2 copy-done.4
  146.5 6.8 %project_first.1.y0 = f32[2,272,896]{2,1,0:T(8,128)} custom-call(s32[3]{0:T(128)} %pad_add_fusion.at, bf16[272,896]{1,0:T(8,128)(2,1)} %combine.1.x0, bf16[272,896]{1,0:T(8,128)(2,1)} %collective-permute-done.11.x2, bf16[896,7168]{1,0:T(8,128)(2,1)} %w.1, bf16[896,896]{1,0:T(8,128)(2,1)} %collective-permute-done.10.a2, bf16[896,896]{1,0:T(8,128)(2,1)} %copy-done.4), custom_call_target="tpu_custom_call" | custom-call | flops 1 | bytes 1 | tf_op jit(solution)/shard_map/project_first/pallas_call | solution.py:429
  154.2 2.3 %collective-permute-done.13.x1 = bf16[272,896]{1,0:T(8,128)(2,1)} collective-permute-done((bf16[272,896]{1,0:T(8,128)(2,1)}, bf16[272,896]{1,0:T(8,128)(2,1)}, u32[]{:S(2)}, u32[]{:S(2)}) %collective-permute-start.13) | collective-permute-done | bytes 487456 | tf_op jit(solution)/shard_map/ppermute | solution.py:518
  156.5 8.4 %project.1 = (bf16[256,1792]{1,0:T(8,128)(2,1)}, bf16[16,1792]{1,0:T(8,128)(2,1)}) custom-call(s32[3]{0:T(128)} %pad_add_fusion.at, f32[2,272,896]{2,1,0:T(8,128)} %project_first.1.y0, bf16[272,896]{1,0:T(8,128)(2,1)} %collective-permute-done.13.x1, bf16[272,896]{1,0:T(8,128)(2,1)} %collective-permute-done.14.x3, ...), custom_call_target="tpu_custom_call" | custom-call | flops 1 | bytes 1 | tf_op jit(solution)/shard_map/project/pallas_call | solution.py:477
  (91 shorter events, 12.9 us)
Async XLA Ops:
  0.6 13.3 %copy-start.7 = (bf16[1,24,128,128]{3,2,1,0:T(8,128)(2,1)S(1)}, bf16[1,24,128,128]{3,2,1,0:T(8,128)(2,1)}, u32[]{:S(2)}) copy-start(bf16[1,24,128,128]{3,2,1,0:T(8,128)(2,1)} %param.20) | copy-start | bytes 2359300
  2.2 17.9 %all-to-all-start = ((bf16[16,64,128]{2,1,0:T(8,128)(2,1)}), bf16[16,64,128]{2,1,0:T(8,128)(2,1)S(1)}, u32[]{:S(2)}, u32[]{:S(2)}) async-start(bf16[16,64,128]{2,1,0:T(8,128)(2,1)} %broadcast_in_dim.45), calls=%async_computation | async-start | bytes 524288 | tf_op jit(solution)/shard_map/all_to_all | solution.py:530
  9.6 5.6 %copy-start.13 = (bf16[1,8,32,128]{3,2,1,0:T(8,128)(2,1)S(1)}, bf16[1,8,32,128]{3,2,1,0:T(8,128)(2,1)}, u32[]{:S(2)}) copy-start(bf16[1,8,32,128]{3,2,1,0:T(8,128)(2,1)} %param.18) | copy-start | bytes 196612
  10.5 4.8 %copy-start.20 = (s32[1,24]{1,0:T(1,128)S(1)}, s32[1,24]{1,0:T(1,128)}, u32[]{:S(2)}) copy-start(s32[1,24]{1,0:T(1,128)} %param.23) | copy-start | bytes 292
  10.5 9.6 %collective-permute-start = (bf16[512,128]{1,0:T(8,128)(2,1)S(1)}, bf16[512,128]{1,0:T(8,128)(2,1)S(1)}, u32[]{:S(2)}, u32[]{:S(2)}) collective-permute-start(bf16[512,128]{1,0:T(8,128)(2,1)S(1)} %pad_maximum_fusion), channel_id=1, source_target_pairs={{0,64},{64,0},{1,65},{65,1},{2,66},{66,2},{3,67},{67,3},{4,68},{68... | collective-permute-start | bytes 393224 | tf_op jit(solution)/shard_map/ppermute | solution.py:532
  15.4 4.8 %copy-start.12 = (bf16[1,8,32,896]{3,2,1,0:T(8,128)(2,1)S(1)}, bf16[1,8,32,896]{3,2,1,0:T(8,128)(2,1)}, u32[]{:S(2)}) copy-start(bf16[1,8,32,896]{3,2,1,0:T(8,128)(2,1)} %param.17) | copy-start | bytes 1376260
  20.1 17.1 %copy-start = (bf16[6784,128]{1,0:T(8,128)(2,1)}, bf16[6784,128]{1,0:T(8,128)(2,1)S(1)}, u32[]{:S(2)}) copy-start(bf16[6784,128]{1,0:T(8,128)(2,1)S(1)} %pad_dynamic-update-slice_fusion) | copy-start | bytes 5210116
  21.8 8.6 %copy-start.16 = (bf16[1,2,4,128]{3,2,1,0:T(4,128)(2,1)S(1)}, bf16[1,2,4,128]{3,2,1,0:T(4,128)(2,1)}, u32[]{:S(2)}) copy-start(bf16[1,2,4,128]{3,2,1,0:T(4,128)(2,1)} %param.26) | copy-start | bytes 6148
  21.8 9.3 %copy-start.17 = (bf16[1,2,4,128]{3,2,1,0:T(4,128)(2,1)S(1)}, bf16[1,2,4,128]{3,2,1,0:T(4,128)(2,1)}, u32[]{:S(2)}) copy-start(bf16[1,2,4,128]{3,2,1,0:T(4,128)(2,1)} %param.27) | copy-start | bytes 6148
  21.8 10.4 %copy-start.18 = (s32[1,24]{1,0:T(1,128)S(1)}, s32[1,24]{1,0:T(1,128)}, u32[]{:S(2)}) copy-start(s32[1,24]{1,0:T(1,128)} %param.30) | copy-start | bytes 292
  21.8 10.4 %copy-start.22 = (s32[1,32]{1,0:T(1,128)S(1)}, s32[1,32]{1,0:T(1,128)}, u32[]{:S(2)}) copy-start(s32[1,32]{1,0:T(1,128)} %param.32) | copy-start | bytes 388
  21.8 10.6 %copy-start.23 = (s32[1,24]{1,0:T(1,128)S(1)}, s32[1,24]{1,0:T(1,128)}, u32[]{:S(2)}) copy-start(s32[1,24]{1,0:T(1,128)} %param.31) | copy-start | bytes 292
  21.9 31.3 %collective-permute-start.2 = (bf16[53,128,128]{2,1,0:T(8,128)(2,1)S(1)}, bf16[53,128,128]{2,1,0:T(8,128)(2,1)S(1)}, u32[]{:S(2)}, u32[]{:S(2)}) collective-permute-start(bf16[53,128,128]{2,1,0:T(8,128)(2,1)S(1)} %bitcast.50), channel_id=1, source_target_pairs={{0,4},{4,0},{8,12},{12,8},{16,20},{20,16},{24,28},{28,24},{32,36},... | collective-permute-start | bytes 5210120 | tf_op jit(solution)/shard_map/ppermute | solution.py:515
  22.3 47.4 %collective-permute-start.1 = (bf16[53,128,128]{2,1,0:T(8,128)(2,1)S(1)}, bf16[53,128,128]{2,1,0:T(8,128)(2,1)}, u32[]{:S(2)}, u32[]{:S(2)}) collective-permute-start(bf16[53,128,128]{2,1,0:T(8,128)(2,1)S(1)} %bitcast.51), channel_id=1, source_target_pairs={{0,8},{4,12},{8,0},{12,4},{16,24},{20,28},{24,16},{28,20},{32,40},... | collective-permute-start | bytes 5210120 | tf_op jit(solution)/shard_map/ppermute | solution.py:515
  23.3 46.3 %collective-permute-start.3 = (bf16[896,896]{1,0:T(8,128)(2,1)}, bf16[896,896]{1,0:T(8,128)(2,1)}, u32[]{:S(2)}, u32[]{:S(2)}) collective-permute-start(bf16[896,896]{1,0:T(8,128)(2,1)} %get-tuple-element.51), channel_id=1, source_target_pairs={{0,1},{1,2},{2,3},{3,0},{4,5},{5,6},{6,7},{7,4},{8,9},{9,10},{10,1... | collective-permute-start | bytes 4816904 | tf_op jit(solution)/shard_map/ppermute | solution.py:518
  24.6 45.1 %collective-permute-start.4 = (bf16[896,896]{1,0:T(8,128)(2,1)}, bf16[896,896]{1,0:T(8,128)(2,1)}, u32[]{:S(2)}, u32[]{:S(2)}) collective-permute-start(bf16[896,896]{1,0:T(8,128)(2,1)} %get-tuple-element.52), channel_id=1, source_target_pairs={{0,3},{1,0},{2,1},{3,2},{4,7},{5,4},{6,5},{7,6},{8,11},{9,8},{10,9... | collective-permute-start | bytes 4816904 | tf_op jit(solution)/shard_map/ppermute | solution.py:518
  26.0 27.1 %all-to-all-start.1 = ((bf16[4,8,32,896]{3,2,1,0:T(8,128)(2,1)}), bf16[4,8,32,896]{3,2,1,0:T(8,128)(2,1)}, u32[]{:S(2)}, u32[]{:S(2)}) async-start(bf16[4,8,32,896]{3,2,1,0:T(8,128)(2,1)} %broadcast_in_dim.50), calls=%async_computation.1 | async-start | bytes 3670016 | tf_op jit(solution)/shard_map/all_to_all | solution.py:555
  69.7 9.0 %collective-permute-start.5 = (bf16[53,128,128]{2,1,0:T(8,128)(2,1)}, bf16[53,128,128]{2,1,0:T(8,128)(2,1)S(1)}, u32[]{:S(2)}, u32[]{:S(2)}) collective-permute-start(bf16[53,128,128]{2,1,0:T(8,128)(2,1)} %collective-permute-done.1.refs_4_), channel_id=1, source_target_pairs={{0,4},{4,0},{8,12},{12,8},{16,20},{20,16},{24,28},{28,24},{32,36},... | collective-permute-start | bytes 5210120 | tf_op jit(solution)/shard_map/ppermute | solution.py:515
  71.6 25.7 %all-to-all-start.2 = ((bf16[16,2,32,256]{3,2,1,0:T(8,128)(2,1)}), bf16[16,2,32,256]{3,2,1,0:T(8,128)(2,1)S(1)}, u32[]{:S(2)}, u32[]{:S(2)}) async-start(bf16[16,2,32,256]{3,2,1,0:T(8,128)(2,1)} %bitcast.55), calls=%async_computation.2 | async-start | bytes 1048576 | tf_op jit(solution)/shard_map/all_to_all | solution.py:579
  75.8 53.6 %collective-permute-start.10 = (bf16[896,896]{1,0:T(8,128)(2,1)}, bf16[896,896]{1,0:T(8,128)(2,1)}, u32[]{:S(2)}, u32[]{:S(2)}) collective-permute-start(bf16[896,896]{1,0:T(8,128)(2,1)} %get-tuple-element.71), channel_id=1, source_target_pairs={{0,2},{1,3},{2,0},{3,1},{4,6},{5,7},{6,4},{7,5},{8,10},{9,11},{10,... | collective-permute-start | bytes 4816904 | tf_op jit(solution)/shard_map/ppermute | solution.py:518
  97.4 28.4 %copy-start.2 = (bf16[16,2,32,256]{3,2,1,0:T(8,128)(2,1)}, bf16[16,2,32,256]{3,2,1,0:T(8,128)(2,1)S(1)}, u32[]{:S(2)}) copy-start(bf16[16,2,32,256]{3,2,1,0:T(8,128)(2,1)S(1)} %all-to-all-done.2.refs_4_) | copy-start | bytes 1572868
  97.4 32.1 %collective-permute-start.9 = (bf16[896,896]{1,0:T(8,128)(2,1)}, bf16[896,896]{1,0:T(8,128)(2,1)S(1)}, u32[]{:S(2)}, u32[]{:S(2)}) collective-permute-start(bf16[896,896]{1,0:T(8,128)(2,1)} %collective-permute-done.3.a1), channel_id=1, source_target_pairs={{0,4},{4,0},{8,12},{12,8},{16,20},{20,16},{24,28},{28,24},{32,36},... | collective-permute-start | bytes 4816904 | tf_op jit(solution)/shard_map/ppermute | solution.py:515
  97.8 13.3 %collective-permute-start.6 = (bf16[272,896]{1,0:T(8,128)(2,1)}, bf16[272,896]{1,0:T(8,128)(2,1)S(1)}, u32[]{:S(2)}, u32[]{:S(2)}) collective-permute-start(bf16[272,896]{1,0:T(8,128)(2,1)} %get-tuple-element.65), channel_id=1, source_target_pairs={{0,16},{4,20},{8,24},{12,28},{16,0},{20,4},{24,8},{28,12},{32,48},... | collective-permute-start | bytes 1462280 | tf_op jit(solution)/shard_map/ppermute | solution.py:512
  99.5 24.3 %collective-permute-start.7 = (bf16[272,896]{1,0:T(8,128)(2,1)}, bf16[272,896]{1,0:T(8,128)(2,1)S(1)}, u32[]{:S(2)}, u32[]{:S(2)}) collective-permute-start(bf16[272,896]{1,0:T(8,128)(2,1)} %get-tuple-element.66), channel_id=1, source_target_pairs={{0,32},{4,36},{8,40},{12,44},{16,48},{20,52},{24,56},{28,60},{32,0... | collective-permute-start | bytes 1462280 | tf_op jit(solution)/shard_map/ppermute | solution.py:512
  101.9 23.9 %collective-permute-start.8 = (bf16[272,896]{1,0:T(8,128)(2,1)}, bf16[272,896]{1,0:T(8,128)(2,1)S(1)}, u32[]{:S(2)}, u32[]{:S(2)}) collective-permute-start(bf16[272,896]{1,0:T(8,128)(2,1)} %get-tuple-element.67), channel_id=1, source_target_pairs={{0,48},{4,52},{8,56},{12,60},{16,32},{20,36},{24,40},{28,44},{32,1... | collective-permute-start | bytes 1462280 | tf_op jit(solution)/shard_map/ppermute | solution.py:512
  111.1 14.7 %copy-start.9 = (bf16[272,896]{1,0:T(8,128)(2,1)}, bf16[272,896]{1,0:T(8,128)(2,1)S(1)}, u32[]{:S(2)}) copy-start(bf16[272,896]{1,0:T(8,128)(2,1)S(1)} %collective-permute-done.6.refs_1_) | copy-start | bytes 1462276
  129.5 23.8 %copy-start.5 = (bf16[896,896]{1,0:T(8,128)(2,1)}, bf16[896,896]{1,0:T(8,128)(2,1)S(1)}, u32[]{:S(2)}) copy-start(bf16[896,896]{1,0:T(8,128)(2,1)S(1)} %collective-permute-done.9.b1) | copy-start | bytes 4816900
  129.5 15.8 %collective-permute-start.12 = (bf16[896,896]{1,0:T(8,128)(2,1)}, bf16[896,896]{1,0:T(8,128)(2,1)S(1)}, u32[]{:S(2)}, u32[]{:S(2)}) collective-permute-start(bf16[896,896]{1,0:T(8,128)(2,1)} %collective-permute-done.10.a2), channel_id=1, source_target_pairs={{0,4},{4,0},{8,12},{12,8},{16,20},{20,16},{24,28},{28,24},{32,36},... | collective-permute-start | bytes 4816904 | tf_op jit(solution)/shard_map/ppermute | solution.py:515
  131.1 25.4 %collective-permute-start.15 = (bf16[896,896]{1,0:T(8,128)(2,1)}, bf16[896,896]{1,0:T(8,128)(2,1)}, u32[]{:S(2)}, u32[]{:S(2)}) collective-permute-start(bf16[896,896]{1,0:T(8,128)(2,1)} %collective-permute-done.4.a3), channel_id=1, source_target_pairs={{0,4},{4,0},{8,12},{12,8},{16,20},{20,16},{24,28},{28,24},{32,36},... | collective-permute-start | bytes 4816904 | tf_op jit(solution)/shard_map/ppermute | solution.py:515
  131.2 14.2 %collective-permute-start.11 = (bf16[272,896]{1,0:T(8,128)(2,1)}, bf16[272,896]{1,0:T(8,128)(2,1)}, u32[]{:S(2)}, u32[]{:S(2)}) collective-permute-start(bf16[272,896]{1,0:T(8,128)(2,1)} %combine.1.x0), channel_id=1, source_target_pairs={{0,2},{1,3},{2,0},{3,1},{4,6},{5,7},{6,4},{7,5},{8,10},{9,11},{10,... | collective-permute-start | bytes 1462280 | tf_op jit(solution)/shard_map/ppermute | solution.py:518
  132.6 21.6 %collective-permute-start.14 = (bf16[272,896]{1,0:T(8,128)(2,1)}, bf16[272,896]{1,0:T(8,128)(2,1)}, u32[]{:S(2)}, u32[]{:S(2)}) collective-permute-start(bf16[272,896]{1,0:T(8,128)(2,1)} %combine.1.x0), channel_id=1, source_target_pairs={{0,3},{1,0},{2,1},{3,2},{4,7},{5,4},{6,5},{7,6},{8,11},{9,8},{10,9... | collective-permute-start | bytes 1462280 | tf_op jit(solution)/shard_map/ppermute | solution.py:518
  133.9 22.7 %collective-permute-start.13 = (bf16[272,896]{1,0:T(8,128)(2,1)}, bf16[272,896]{1,0:T(8,128)(2,1)}, u32[]{:S(2)}, u32[]{:S(2)}) collective-permute-start(bf16[272,896]{1,0:T(8,128)(2,1)} %combine.1.x0), channel_id=1, source_target_pairs={{0,1},{1,2},{2,3},{3,0},{4,5},{5,6},{6,7},{7,4},{8,9},{9,10},{10,1... | collective-permute-start | bytes 1462280 | tf_op jit(solution)/shard_map/ppermute | solution.py:518
  (11 other events, 25.0 us)

commit v5 on v4

--- a/solution.py
+++ b/solution.py
@@ -71,7 +71,7 @@
         rel, q_all, ma, mb, num_out, qs_out, den, qv, qs, ks, vs, acc, dacc, p0, p1, sem = refs
     else:
         (bases, qs_in, ma, mb, mc, md, num_in, den_in, o0, o1, o2, o3,
-         qs, ks, vs, acc, dacc, p0, p1, tile, stage, sem) = refs
+         qs, ks, vs, acc, dacc, num, p0, p1, tile, stage, sem) = refs
     cs = []
 
     def copy(src, dst, i):
@@ -83,7 +83,7 @@
         qc = [copy(q_all.at[rel[d]], qv.at[d], 4 + d) for d in range(4)]
         sets = (ma, mb)
     else:
-        cs = [copy(qs_in.at[pl.ds(r0, R)], qs, 4), copy(num_in.at[pl.ds(r0, R)], acc, 5)]
+        cs = [copy(qs_in.at[pl.ds(r0, R)], qs, 4)]
         sets = (mc, md)
     for i, m in enumerate(sets):
         cs.append(copy(m.at[pl.ds(0, half)], ks.at[pl.ds(i * half, half)], 2 * i))
@@ -103,8 +103,8 @@
     pair_table(ra, rb, table, cnt, R, 0 if first else 1)
     dacc[...] = jnp.zeros_like(dacc)
     p1[...] = jnp.zeros_like(p1)
+    acc[...] = jnp.zeros_like(acc)
     if first:
-        acc[...] = jnp.zeros_like(acc)
         for c in qc:
             c.wait()
         for d in range(4):
@@ -126,6 +126,8 @@
         tile[...] = jnp.where(pick(rowi, 0) >= pick(coli, 4), coli + 1, 0)
     for c in cs:
         c.wait()
+    if not first:
+        num_copy = copy(num_in.at[pl.ds(r0, R)], num, 5)
     lane = lax.broadcasted_iota(jnp.int32, (1, 128), 1)
     begin, end = table[3, r0], table[3, r0 + R]
 
@@ -190,12 +192,12 @@
         qs_copy.wait()
         return
     outs = [stage.at[d] for d in range(4)]
+    num_copy.wait()
     for r in range(R):
         for h in range(heads):
             for d in range(4):
-                outs[d][r * 32 : r * 32 + 32, h * 128 : h * 128 + 128] = acc[
-                    r, h * 128 + d * 32 : h * 128 + d * 32 + 32, :
-                ].astype(BF)
+                sl = pl.ds(h * 128 + d * 32, 32)
+                outs[d][r * 32 : r * 32 + 32, h * 128 : h * 128 + 128] = (acc[r, sl, :] + num[r, sl, :]).astype(BF)
     hi = dl.astype(BF)
     lo = (dl - hi.astype(F32)).astype(BF)
     z = jnp.zeros((16, (heads - 4) * 128), BF)
@@ -255,6 +257,7 @@
             pltpu.VMEM((R, rows, 128), BF),
             pltpu.VMEM((nb + R, 128, 128), BF),
             pltpu.VMEM((nb + R, 128, 128), BF),
+            pltpu.VMEM((R, rows, 128), F32),
             pltpu.VMEM((R, rows, 128), F32),
             pltpu.VMEM((R, rows, 128), F32),
             pltpu.VMEM((rows, 256), BF),
@@ -446,8 +449,9 @@
     for t, parts in enumerate(((a1, a3), (b1, b3))):
         for d, part in enumerate(parts):
             c = pltpu.make_async_copy(part, ws.at[t, pl.ds(d * depth, depth)], sem.at[t * 2 + d])
-            c.start()
             copies.append(c)
+    copies[0].start()
+    copies[1].start()
     y_copy = pltpu.make_async_copy(y0, y, sem.at[6])
     y_copy.start()
     x = jnp.concatenate([x1[...], x3[...]], axis=1)
@@ -457,6 +461,9 @@
         cols = pl.ds(pl.multiple_of(side * half, half), half)
         copies[t * 2].wait()
         copies[t * 2 + 1].wait()
+        if t == 0:
+            copies[2].start()
+            copies[3].start()
         total = jnp.dot(x, ws[t], preferred_element_type=F32)
         if t == 0:
             y_copy.wait()

time: 167 us -> 166 us (level)
  no operation moved by 1% of the time
where the time goes in v5:
time: 166 us; the launch traced here: 165 us
  Pallas kernels  54.4 us (33%)
  waiting for transfers between devices  53.2 us (32%)
  starting transfers between devices  35.3 us (21%)
  local copies, waits for them, and re-layouts  15 us (9%)
  other arithmetic  6.53 us (4%)
    ppermute x3, waiting for transfers between devices, along_y(): return lax.ppermute(x, 'ctx', [(i, i ^ 4 * d) for i in range(ctx)])  23.9 us
    pallas_call x1, Pallas kernels, attn_far(): pl.pallas_call(body, in_specs=[SM] * 3 + [HBM] * 6 + [VM], out_specs=[HBM...  17.3 us
    all_to_all x1, waiting for transfers between devices, on_device(): qs = lax.all_to_all(queries, 'ctx', 0, 0, axis_index_groups=rings)  15.3 us
    pallas_call x1, Pallas kernels, attn_near(): pl.pallas_call(body, in_specs=[SM] * 3 + [HBM] * 3, out_specs=[HBM, HBM,...  15.3 us
    ppermute x6, waiting for transfers between devices, along_x(): return lax.ppermute(x, 'tp', [(i, (i + d) % tp) for i in range(tp)])  13.9 us
    pallas_call x1, Pallas kernels, project(): pl.pallas_call(project_kernel, in_specs=[SM, HBM] + [VM] * 2 + [HBM] * 4,...  7.75 us
    all_to_all x1, starting transfers between devices, on_device(): notes = lax.all_to_all(dq, 'ctx', 0, 0)  7.34 us
    ppermute x6, starting transfers between devices, along_x(): return lax.ppermute(x, 'tp', [(i, (i + d) % tp) for i in range(tp)])  7.11 us
  transfers between devices with their start and end apart: 19, of which 7 were waited for; matrix products, arithmetic and copies ran while one was open for 8% of the time, Pallas kernels for 28%

profile of v5, /device:TPU:1, one launch (start us, length us, event | category | flops | bytes accessed | tf_op | source)
XLA Modules:
  0.0 165.4 jit_solution(7891767879350760847)
XLA Ops:
  2.2 7.3 %all-to-all-start = ((bf16[16,64,128]{2,1,0:T(8,128)(2,1)}), bf16[16,64,128]{2,1,0:T(8,128)(2,1)S(1)}, u32[]{:S(2)}, u32[]{:S(2)}) async-start(bf16[16,64,128]{2,1,0:T(8,128)(2,1)} %broadcast_in_dim.45), calls=%async_computation | async-start | bytes 524288 | tf_op jit(solution)/shard_map/all_to_all | solution.py:537
  9.6 0.9 pad_maximum_fusion
  10.5 3.4 %collective-permute-start = (bf16[512,128]{1,0:T(8,128)(2,1)S(1)}, bf16[512,128]{1,0:T(8,128)(2,1)S(1)}, u32[]{:S(2)}, u32[]{:S(2)}) collective-permute-start(bf16[512,128]{1,0:T(8,128)(2,1)S(1)} %pad_maximum_fusion), channel_id=1, source_target_pairs={{0,64},{64,0},{1,65},{65,1},{2,66},{66,2},{3,67},{67,3},{4,68},{68... | collective-permute-start | bytes 393224 | tf_op jit(solution)/shard_map/ppermute | solution.py:539
  14.0 1.1 copy-done.8
  15.4 4.7 %constant_dynamic-slice_fusion = (bf16[896,896]{1,0:T(8,128)(2,1)}, bf16[896,896]{1,0:T(8,128)(2,1)}, bf16[896,896]{1,0:T(8,128)(2,1)}) fusion(bf16[896,7168]{1,0:T(8,128)(2,1)} %w.1, s32[]{:T(128)S(6)} %select_n.47, s32[]{:T(128)S(6)} %select_n.45, s32[]{:T(128)S(6)} %select_n.43), kind=kLoop, calls=%fused_computation.18 | loop fusion | bytes 9633804 | tf_op jit(solution)/shard_map/dynamic_slice | solution.py:554
  20.2 1.6 broadcast_in_dim.50
  22.3 1.1 collective-permute-start.1
  23.3 1.2 collective-permute-start.3
  24.6 1.5 collective-permute-start.4
  26.0 4.4 %all-to-all-start.1 = ((bf16[4,8,32,896]{3,2,1,0:T(8,128)(2,1)}), bf16[4,8,32,896]{3,2,1,0:T(8,128)(2,1)}, u32[]{:S(2)}, u32[]{:S(2)}) async-start(bf16[4,8,32,896]{3,2,1,0:T(8,128)(2,1)} %broadcast_in_dim.50), calls=%async_computation.1 | async-start | bytes 3670016 | tf_op jit(solution)/shard_map/all_to_all | solution.py:562
  32.9 4.3 %decode_terms.1 = bf16[32,32,256]{2,1,0:T(8,128)(2,1)} custom-call(s32[24]{0:T(128)} %bitcast.71, s32[24]{0:T(128)} %fusion.8.lim, s32[1]{0:T(128)} %bitcast.20.ctx, bf16[16,64,128]{2,1,0:T(8,128)(2,1)} %copy-done.6, bf16[24,128,128]{2,1,0:T(8,128)(2,1)} %bitcast.56, bf16[24,128,128]{2,1,0:T(8,128)(2,1)} %bitcast.57, bf16[2,8,32,128]{3,2,1,0:T(8,128)(2,1)} %bitcast.65, ...), custom_call_target="tpu_custom_call" | custom-call | flops 1 | bytes 1 | tf_op jit(solution)/shard_map/decode_terms/pallas_call | solution.py:333
  37.8 15.3 %all-to-all-done.1.refs_1_ = bf16[4,8,32,896]{3,2,1,0:T(8,128)(2,1)} async-done(((bf16[4,8,32,896]{3,2,1,0:T(8,128)(2,1)}), bf16[4,8,32,896]{3,2,1,0:T(8,128)(2,1)}, u32[]{:S(2)}, u32[]{:S(2)}) %all-to-all-start.1) | async-done | bytes 1835040 | tf_op jit(solution)/shard_map/all_to_all | solution.py:562
  54.4 15.3 %attn_near.1 = (f32[8,896,128]{2,1,0:T(8,128)}, bf16[8,896,128]{2,1,0:T(8,128)(2,1)}, f32[128,128]{1,0:T(8,128)}) custom-call(s32[2,24]{1,0:T(2,128)} %bitcast_convert_fusion.1.ra, s32[2,24]{1,0:T(2,128)} %fusion.7.rb, s32[4]{0:T(128)} %iota_xor_fusion.1.refs_0_, bf16[4,8,32,896]{3,2,1,0:T(8,128)(2,1)} %all-to-all-done.1.refs_1_, ...), custom_call_target="tpu_custom_call" | custom-call | flops 1 | bytes 1 | tf_op jit(solution)/shard_map/attn_near/pallas_call | solution.py:219
  69.7 1.9 %collective-permute-start.5 = (bf16[53,128,128]{2,1,0:T(8,128)(2,1)}, bf16[53,128,128]{2,1,0:T(8,128)(2,1)S(1)}, u32[]{:S(2)}, u32[]{:S(2)}) collective-permute-start(bf16[53,128,128]{2,1,0:T(8,128)(2,1)} %collective-permute-done.1.refs_4_), channel_id=1, source_target_pairs={{0,4},{4,0},{8,12},{12,8},{16,20},{20,16},{24,28},{28,24},{32,36},... | collective-permute-start | bytes 5210120 | tf_op jit(solution)/shard_map/ppermute | solution.py:522
  71.6 3.5 %all-to-all-start.2 = ((bf16[16,2,32,256]{3,2,1,0:T(8,128)(2,1)}), bf16[16,2,32,256]{3,2,1,0:T(8,128)(2,1)S(1)}, u32[]{:S(2)}, u32[]{:S(2)}) async-start(bf16[16,2,32,256]{3,2,1,0:T(8,128)(2,1)} %bitcast.55), calls=%async_computation.2 | async-start | bytes 1048576 | tf_op jit(solution)/shard_map/all_to_all | solution.py:586
  75.8 1.6 collective-permute-start.10
  77.3 1.2 bitcast_convert_fusion.ra
  79.8 17.3 %attn_far.1 = (bf16[272,896]{1,0:T(8,128)(2,1)}, bf16[272,896]{1,0:T(8,128)(2,1)}, bf16[272,896]{1,0:T(8,128)(2,1)}, bf16[272,896]{1,0:T(8,128)(2,1)}) custom-call(s32[2,24]{1,0:T(2,128)} %bitcast_convert_fusion.ra, s32[2,24]{1,0:T(2,128)} %fusion.6.rb, s32[8]{0:T(128)} %add_multiply_fusion.refs_0_, bf16[8,896,128]{2,1,0:T(8,128)(2,1)} %get-tuple-element.55.refs_1_, ...), custom_call_target="tpu_custom_call" | custom-call | flops 1 | bytes 1 | tf_op jit(solution)/shard_map/attn_far/pallas_call | solution.py:252
  98.5 3.1 %collective-permute-start.7 = (bf16[272,896]{1,0:T(8,128)(2,1)}, bf16[272,896]{1,0:T(8,128)(2,1)S(1)}, u32[]{:S(2)}, u32[]{:S(2)}) collective-permute-start(bf16[272,896]{1,0:T(8,128)(2,1)} %get-tuple-element.66), channel_id=1, source_target_pairs={{0,32},{4,36},{8,40},{12,44},{16,48},{20,52},{24,56},{28,60},{32,0... | collective-permute-start | bytes 1462280 | tf_op jit(solution)/shard_map/ppermute | solution.py:519
  101.6 9.0 %collective-permute-done.6.refs_1_ = bf16[272,896]{1,0:T(8,128)(2,1)S(1)} collective-permute-done((bf16[272,896]{1,0:T(8,128)(2,1)}, bf16[272,896]{1,0:T(8,128)(2,1)S(1)}, u32[]{:S(2)}, u32[]{:S(2)}) %collective-permute-start.6) | collective-permute-done | bytes 487456 | tf_op jit(solution)/shard_map/ppermute | solution.py:519
  110.7 12.9 %collective-permute-done.7.refs_2_ = bf16[272,896]{1,0:T(8,128)(2,1)S(1)} collective-permute-done((bf16[272,896]{1,0:T(8,128)(2,1)}, bf16[272,896]{1,0:T(8,128)(2,1)S(1)}, u32[]{:S(2)}, u32[]{:S(2)}) %collective-permute-start.7) | collective-permute-done | bytes 487456 | tf_op jit(solution)/shard_map/ppermute | solution.py:519
  123.6 2.0 %collective-permute-done.8.refs_3_ = bf16[272,896]{1,0:T(8,128)(2,1)S(1)} collective-permute-done((bf16[272,896]{1,0:T(8,128)(2,1)}, bf16[272,896]{1,0:T(8,128)(2,1)S(1)}, u32[]{:S(2)}, u32[]{:S(2)}) %collective-permute-start.8) | collective-permute-done | bytes 487456 | tf_op jit(solution)/shard_map/ppermute | solution.py:519
  126.3 2.9 %combine.1.x0 = bf16[272,896]{1,0:T(8,128)(2,1)} custom-call(bf16[272,896]{1,0:T(8,128)(2,1)} %get-tuple-element.64.refs_0_, bf16[272,896]{1,0:T(8,128)(2,1)} %copy-done.9, bf16[272,896]{1,0:T(8,128)(2,1)} %copy-done.10, bf16[272,896]{1,0:T(8,128)(2,1)} %copy-done.11, bf16[16,2,32,256]{3,2,1,0:T(8,128)(2,1)} %copy-done.2), custom_call_target="tpu_custom_call" | custom-call | flops 1000000 | bytes 2500000 | tf_op jit(solution)/shard_map/combine/pallas_call | solution.py:400
  129.3 1.6 collective-permute-start.12
  131.0 1.4 collective-permute-start.11
  132.4 1.3 collective-permute-start.14
  134.4 10.7 %collective-permute-done.11.x2 = bf16[272,896]{1,0:T(8,128)(2,1)} collective-permute-done((bf16[272,896]{1,0:T(8,128)(2,1)}, bf16[272,896]{1,0:T(8,128)(2,1)}, u32[]{:S(2)}, u32[]{:S(2)}) %collective-permute-start.11) | collective-permute-done | bytes 487456 | tf_op jit(solution)/shard_map/ppermute | solution.py:525
  145.1 1.2 copy-done.4
  146.3 6.8 %project_first.1.y0 = f32[2,272,896]{2,1,0:T(8,128)} custom-call(s32[3]{0:T(128)} %pad_add_fusion.at, bf16[272,896]{1,0:T(8,128)(2,1)} %combine.1.x0, bf16[272,896]{1,0:T(8,128)(2,1)} %collective-permute-done.11.x2, bf16[896,7168]{1,0:T(8,128)(2,1)} %w.1, bf16[896,896]{1,0:T(8,128)(2,1)} %collective-permute-done.10.a2, bf16[896,896]{1,0:T(8,128)(2,1)} %copy-done.4), custom_call_target="tpu_custom_call" | custom-call | flops 1 | bytes 1 | tf_op jit(solution)/shard_map/project_first/pallas_call | solution.py:432
  153.1 0.9 collective-permute-done.14.x3
  154.0 2.3 %collective-permute-done.13.x1 = bf16[272,896]{1,0:T(8,128)(2,1)} collective-permute-done((bf16[272,896]{1,0:T(8,128)(2,1)}, bf16[272,896]{1,0:T(8,128)(2,1)}, u32[]{:S(2)}, u32[]{:S(2)}) %collective-permute-start.13) | collective-permute-done | bytes 487456 | tf_op jit(solution)/shard_map/ppermute | solution.py:525
  156.3 7.8 %project.1 = (bf16[256,1792]{1,0:T(8,128)(2,1)}, bf16[16,1792]{1,0:T(8,128)(2,1)}) custom-call(s32[3]{0:T(128)} %pad_add_fusion.at, f32[2,272,896]{2,1,0:T(8,128)} %project_first.1.y0, bf16[272,896]{1,0:T(8,128)(2,1)} %collective-permute-done.13.x1, bf16[272,896]{1,0:T(8,128)(2,1)} %collective-permute-done.14.x3, ...), custom_call_target="tpu_custom_call" | custom-call | flops 1 | bytes 1 | tf_op jit(solution)/shard_map/project/pallas_call | solution.py:484
  (91 shorter events, 13.0 us)
Async XLA Ops:
  0.6 13.3 %copy-start.7 = (bf16[1,24,128,128]{3,2,1,0:T(8,128)(2,1)S(1)}, bf16[1,24,128,128]{3,2,1,0:T(8,128)(2,1)}, u32[]{:S(2)}) copy-start(bf16[1,24,128,128]{3,2,1,0:T(8,128)(2,1)} %param.20) | copy-start | bytes 2359300
  2.2 17.9 %all-to-all-start = ((bf16[16,64,128]{2,1,0:T(8,128)(2,1)}), bf16[16,64,128]{2,1,0:T(8,128)(2,1)S(1)}, u32[]{:S(2)}, u32[]{:S(2)}) async-start(bf16[16,64,128]{2,1,0:T(8,128)(2,1)} %broadcast_in_dim.45), calls=%async_computation | async-start | bytes 524288 | tf_op jit(solution)/shard_map/all_to_all | solution.py:537
  9.6 5.6 %copy-start.13 = (bf16[1,8,32,128]{3,2,1,0:T(8,128)(2,1)S(1)}, bf16[1,8,32,128]{3,2,1,0:T(8,128)(2,1)}, u32[]{:S(2)}) copy-start(bf16[1,8,32,128]{3,2,1,0:T(8,128)(2,1)} %param.18) | copy-start | bytes 196612
  10.5 4.8 %copy-start.20 = (s32[1,24]{1,0:T(1,128)S(1)}, s32[1,24]{1,0:T(1,128)}, u32[]{:S(2)}) copy-start(s32[1,24]{1,0:T(1,128)} %param.23) | copy-start | bytes 292
  10.5 9.6 %collective-permute-start = (bf16[512,128]{1,0:T(8,128)(2,1)S(1)}, bf16[512,128]{1,0:T(8,128)(2,1)S(1)}, u32[]{:S(2)}, u32[]{:S(2)}) collective-permute-start(bf16[512,128]{1,0:T(8,128)(2,1)S(1)} %pad_maximum_fusion), channel_id=1, source_target_pairs={{0,64},{64,0},{1,65},{65,1},{2,66},{66,2},{3,67},{67,3},{4,68},{68... | collective-permute-start | bytes 393224 | tf_op jit(solution)/shard_map/ppermute | solution.py:539
  15.4 4.8 %copy-start.12 = (bf16[1,8,32,896]{3,2,1,0:T(8,128)(2,1)S(1)}, bf16[1,8,32,896]{3,2,1,0:T(8,128)(2,1)}, u32[]{:S(2)}) copy-start(bf16[1,8,32,896]{3,2,1,0:T(8,128)(2,1)} %param.17) | copy-start | bytes 1376260
  20.1 17.1 %copy-start = (bf16[6784,128]{1,0:T(8,128)(2,1)}, bf16[6784,128]{1,0:T(8,128)(2,1)S(1)}, u32[]{:S(2)}) copy-start(bf16[6784,128]{1,0:T(8,128)(2,1)S(1)} %pad_dynamic-update-slice_fusion) | copy-start | bytes 5210116
  21.8 8.6 %copy-start.16 = (bf16[1,2,4,128]{3,2,1,0:T(4,128)(2,1)S(1)}, bf16[1,2,4,128]{3,2,1,0:T(4,128)(2,1)}, u32[]{:S(2)}) copy-start(bf16[1,2,4,128]{3,2,1,0:T(4,128)(2,1)} %param.26) | copy-start | bytes 6148
  21.8 9.3 %copy-start.17 = (bf16[1,2,4,128]{3,2,1,0:T(4,128)(2,1)S(1)}, bf16[1,2,4,128]{3,2,1,0:T(4,128)(2,1)}, u32[]{:S(2)}) copy-start(bf16[1,2,4,128]{3,2,1,0:T(4,128)(2,1)} %param.27) | copy-start | bytes 6148
  21.8 10.4 %copy-start.18 = (s32[1,24]{1,0:T(1,128)S(1)}, s32[1,24]{1,0:T(1,128)}, u32[]{:S(2)}) copy-start(s32[1,24]{1,0:T(1,128)} %param.30) | copy-start | bytes 292
  21.8 10.4 %copy-start.22 = (s32[1,32]{1,0:T(1,128)S(1)}, s32[1,32]{1,0:T(1,128)}, u32[]{:S(2)}) copy-start(s32[1,32]{1,0:T(1,128)} %param.32) | copy-start | bytes 388
  21.8 10.6 %copy-start.23 = (s32[1,24]{1,0:T(1,128)S(1)}, s32[1,24]{1,0:T(1,128)}, u32[]{:S(2)}) copy-start(s32[1,24]{1,0:T(1,128)} %param.31) | copy-start | bytes 292
  21.9 31.3 %collective-permute-start.2 = (bf16[53,128,128]{2,1,0:T(8,128)(2,1)S(1)}, bf16[53,128,128]{2,1,0:T(8,128)(2,1)S(1)}, u32[]{:S(2)}, u32[]{:S(2)}) collective-permute-start(bf16[53,128,128]{2,1,0:T(8,128)(2,1)S(1)} %bitcast.50), channel_id=1, source_target_pairs={{0,4},{4,0},{8,12},{12,8},{16,20},{20,16},{24,28},{28,24},{32,36},... | collective-permute-start | bytes 5210120 | tf_op jit(solution)/shard_map/ppermute | solution.py:522
  22.3 47.4 %collective-permute-start.1 = (bf16[53,128,128]{2,1,0:T(8,128)(2,1)S(1)}, bf16[53,128,128]{2,1,0:T(8,128)(2,1)}, u32[]{:S(2)}, u32[]{:S(2)}) collective-permute-start(bf16[53,128,128]{2,1,0:T(8,128)(2,1)S(1)} %bitcast.51), channel_id=1, source_target_pairs={{0,8},{4,12},{8,0},{12,4},{16,24},{20,28},{24,16},{28,20},{32,40},... | collective-permute-start | bytes 5210120 | tf_op jit(solution)/shard_map/ppermute | solution.py:522
  23.3 46.3 %collective-permute-start.3 = (bf16[896,896]{1,0:T(8,128)(2,1)}, bf16[896,896]{1,0:T(8,128)(2,1)}, u32[]{:S(2)}, u32[]{:S(2)}) collective-permute-start(bf16[896,896]{1,0:T(8,128)(2,1)} %get-tuple-element.51), channel_id=1, source_target_pairs={{0,1},{1,2},{2,3},{3,0},{4,5},{5,6},{6,7},{7,4},{8,9},{9,10},{10,1... | collective-permute-start | bytes 4816904 | tf_op jit(solution)/shard_map/ppermute | solution.py:525
  24.6 45.1 %collective-permute-start.4 = (bf16[896,896]{1,0:T(8,128)(2,1)}, bf16[896,896]{1,0:T(8,128)(2,1)}, u32[]{:S(2)}, u32[]{:S(2)}) collective-permute-start(bf16[896,896]{1,0:T(8,128)(2,1)} %get-tuple-element.52), channel_id=1, source_target_pairs={{0,3},{1,0},{2,1},{3,2},{4,7},{5,4},{6,5},{7,6},{8,11},{9,8},{10,9... | collective-permute-start | bytes 4816904 | tf_op jit(solution)/shard_map/ppermute | solution.py:525
  26.0 27.1 %all-to-all-start.1 = ((bf16[4,8,32,896]{3,2,1,0:T(8,128)(2,1)}), bf16[4,8,32,896]{3,2,1,0:T(8,128)(2,1)}, u32[]{:S(2)}, u32[]{:S(2)}) async-start(bf16[4,8,32,896]{3,2,1,0:T(8,128)(2,1)} %broadcast_in_dim.50), calls=%async_computation.1 | async-start | bytes 3670016 | tf_op jit(solution)/shard_map/all_to_all | solution.py:562
  69.7 8.9 %collective-permute-start.5 = (bf16[53,128,128]{2,1,0:T(8,128)(2,1)}, bf16[53,128,128]{2,1,0:T(8,128)(2,1)S(1)}, u32[]{:S(2)}, u32[]{:S(2)}) collective-permute-start(bf16[53,128,128]{2,1,0:T(8,128)(2,1)} %collective-permute-done.1.refs_4_), channel_id=1, source_target_pairs={{0,4},{4,0},{8,12},{12,8},{16,20},{20,16},{24,28},{28,24},{32,36},... | collective-permute-start | bytes 5210120 | tf_op jit(solution)/shard_map/ppermute | solution.py:522
  71.6 25.5 %all-to-all-start.2 = ((bf16[16,2,32,256]{3,2,1,0:T(8,128)(2,1)}), bf16[16,2,32,256]{3,2,1,0:T(8,128)(2,1)S(1)}, u32[]{:S(2)}, u32[]{:S(2)}) async-start(bf16[16,2,32,256]{3,2,1,0:T(8,128)(2,1)} %bitcast.55), calls=%async_computation.2 | async-start | bytes 1048576 | tf_op jit(solution)/shard_map/all_to_all | solution.py:586
  75.8 53.5 %collective-permute-start.10 = (bf16[896,896]{1,0:T(8,128)(2,1)}, bf16[896,896]{1,0:T(8,128)(2,1)}, u32[]{:S(2)}, u32[]{:S(2)}) collective-permute-start(bf16[896,896]{1,0:T(8,128)(2,1)} %get-tuple-element.71), channel_id=1, source_target_pairs={{0,2},{1,3},{2,0},{3,1},{4,6},{5,7},{6,4},{7,5},{8,10},{9,11},{10,... | collective-permute-start | bytes 4816904 | tf_op jit(solution)/shard_map/ppermute | solution.py:525
  97.1 28.4 %copy-start.2 = (bf16[16,2,32,256]{3,2,1,0:T(8,128)(2,1)}, bf16[16,2,32,256]{3,2,1,0:T(8,128)(2,1)S(1)}, u32[]{:S(2)}) copy-start(bf16[16,2,32,256]{3,2,1,0:T(8,128)(2,1)S(1)} %all-to-all-done.2.refs_4_) | copy-start | bytes 1572868
  97.1 32.2 %collective-permute-start.9 = (bf16[896,896]{1,0:T(8,128)(2,1)}, bf16[896,896]{1,0:T(8,128)(2,1)S(1)}, u32[]{:S(2)}, u32[]{:S(2)}) collective-permute-start(bf16[896,896]{1,0:T(8,128)(2,1)} %collective-permute-done.3.a1), channel_id=1, source_target_pairs={{0,4},{4,0},{8,12},{12,8},{16,20},{20,16},{24,28},{28,24},{32,36},... | collective-permute-start | bytes 4816904 | tf_op jit(solution)/shard_map/ppermute | solution.py:522
  97.6 13.0 %collective-permute-start.6 = (bf16[272,896]{1,0:T(8,128)(2,1)}, bf16[272,896]{1,0:T(8,128)(2,1)S(1)}, u32[]{:S(2)}, u32[]{:S(2)}) collective-permute-start(bf16[272,896]{1,0:T(8,128)(2,1)} %get-tuple-element.65), channel_id=1, source_target_pairs={{0,16},{4,20},{8,24},{12,28},{16,0},{20,4},{24,8},{28,12},{32,48},... | collective-permute-start | bytes 1462280 | tf_op jit(solution)/shard_map/ppermute | solution.py:519
  98.5 25.0 %collective-permute-start.7 = (bf16[272,896]{1,0:T(8,128)(2,1)}, bf16[272,896]{1,0:T(8,128)(2,1)S(1)}, u32[]{:S(2)}, u32[]{:S(2)}) collective-permute-start(bf16[272,896]{1,0:T(8,128)(2,1)} %get-tuple-element.66), channel_id=1, source_target_pairs={{0,32},{4,36},{8,40},{12,44},{16,48},{20,52},{24,56},{28,60},{32,0... | collective-permute-start | bytes 1462280 | tf_op jit(solution)/shard_map/ppermute | solution.py:519
  101.6 23.9 %collective-permute-start.8 = (bf16[272,896]{1,0:T(8,128)(2,1)}, bf16[272,896]{1,0:T(8,128)(2,1)S(1)}, u32[]{:S(2)}, u32[]{:S(2)}) collective-permute-start(bf16[272,896]{1,0:T(8,128)(2,1)} %get-tuple-element.67), channel_id=1, source_target_pairs={{0,48},{4,52},{8,56},{12,60},{16,32},{20,36},{24,40},{28,44},{32,1... | collective-permute-start | bytes 1462280 | tf_op jit(solution)/shard_map/ppermute | solution.py:519
  110.6 14.9 %copy-start.9 = (bf16[272,896]{1,0:T(8,128)(2,1)}, bf16[272,896]{1,0:T(8,128)(2,1)S(1)}, u32[]{:S(2)}) copy-start(bf16[272,896]{1,0:T(8,128)(2,1)S(1)} %collective-permute-done.6.refs_1_) | copy-start | bytes 1462276
  129.3 23.8 %copy-start.5 = (bf16[896,896]{1,0:T(8,128)(2,1)}, bf16[896,896]{1,0:T(8,128)(2,1)S(1)}, u32[]{:S(2)}) copy-start(bf16[896,896]{1,0:T(8,128)(2,1)S(1)} %collective-permute-done.9.b1) | copy-start | bytes 4816900
  129.3 15.8 %collective-permute-start.12 = (bf16[896,896]{1,0:T(8,128)(2,1)}, bf16[896,896]{1,0:T(8,128)(2,1)S(1)}, u32[]{:S(2)}, u32[]{:S(2)}) collective-permute-start(bf16[896,896]{1,0:T(8,128)(2,1)} %collective-permute-done.10.a2), channel_id=1, source_target_pairs={{0,4},{4,0},{8,12},{12,8},{16,20},{20,16},{24,28},{28,24},{32,36},... | collective-permute-start | bytes 4816904 | tf_op jit(solution)/shard_map/ppermute | solution.py:522
  130.9 25.4 %collective-permute-start.15 = (bf16[896,896]{1,0:T(8,128)(2,1)}, bf16[896,896]{1,0:T(8,128)(2,1)}, u32[]{:S(2)}, u32[]{:S(2)}) collective-permute-start(bf16[896,896]{1,0:T(8,128)(2,1)} %collective-permute-done.4.a3), channel_id=1, source_target_pairs={{0,4},{4,0},{8,12},{12,8},{16,20},{20,16},{24,28},{28,24},{32,36},... | collective-permute-start | bytes 4816904 | tf_op jit(solution)/shard_map/ppermute | solution.py:522
  131.0 14.2 %collective-permute-start.11 = (bf16[272,896]{1,0:T(8,128)(2,1)}, bf16[272,896]{1,0:T(8,128)(2,1)}, u32[]{:S(2)}, u32[]{:S(2)}) collective-permute-start(bf16[272,896]{1,0:T(8,128)(2,1)} %combine.1.x0), channel_id=1, source_target_pairs={{0,2},{1,3},{2,0},{3,1},{4,6},{5,7},{6,4},{7,5},{8,10},{9,11},{10,... | collective-permute-start | bytes 1462280 | tf_op jit(solution)/shard_map/ppermute | solution.py:525
  132.4 21.6 %collective-permute-start.14 = (bf16[272,896]{1,0:T(8,128)(2,1)}, bf16[272,896]{1,0:T(8,128)(2,1)}, u32[]{:S(2)}, u32[]{:S(2)}) collective-permute-start(bf16[272,896]{1,0:T(8,128)(2,1)} %combine.1.x0), channel_id=1, source_target_pairs={{0,3},{1,0},{2,1},{3,2},{4,7},{5,4},{6,5},{7,6},{8,11},{9,8},{10,9... | collective-permute-start | bytes 1462280 | tf_op jit(solution)/shard_map/ppermute | solution.py:525
  133.6 22.7 %collective-permute-start.13 = (bf16[272,896]{1,0:T(8,128)(2,1)}, bf16[272,896]{1,0:T(8,128)(2,1)}, u32[]{:S(2)}, u32[]{:S(2)}) collective-permute-start(bf16[272,896]{1,0:T(8,128)(2,1)} %combine.1.x0), channel_id=1, source_target_pairs={{0,1},{1,2},{2,3},{3,0},{4,5},{5,6},{6,7},{7,4},{8,9},{9,10},{10,1... | collective-permute-start | bytes 1462280 | tf_op jit(solution)/shard_map/ppermute | solution.py:525
  (11 other events, 25.0 us)
